TPU v7x, 32 devices: a whole 2x2x4 slice. The times are simulated.
32 devices in a mesh: row: 4 (over y, x), col: 8 (over z, core).
Axes of the slice: x: 2, y: 2, z: 4, core: 2. Of those that a mesh axis runs over, the one named last changes fastest.
Arguments:
- evecs: float32 [2048, 1024], P('row', 'col'), may hold values from -6 to 6
- offsets: int32 [4, 2], replicated, may hold values from 0 to 127, as said below
- refl: float32 [4, 2, 16, 64, 192], P(None, None, 'row', 'col'), may hold values from -6 to 6, as said below
Outputs:
- rotated: float32 [2048, 1024], P('row', 'col')
Inputs may be any that keep to these rules, and one draw needn't show every extreme that they name: Within each round and sweep the windows start at offsets plus multiples of 128; some entry is 0 and some is 127 in every draw. `refl`: each block's triangular factor T is the inverse of the strictly upper part of V^T V plus half its diagonal, so that I - V T V^T is orthogonal.
All inputs are finite; a program needn't handle non-finite values.
Results may differ from a plain program's by a relative error of at most 0.0003.
Values sent between devices are 32-bit elements; how exact they have to be, the bound alone decides.
No kernel may reach another device: no remote copies, remote signals or barrier semaphores. Data moves between devices by JAX's collectives and lax.ppermute only.
A program may use at most 64 MiB of HBM per device.

v0:
```python
import functools

import jax
import jax.numpy as jnp
from jax import lax
from jax.experimental import pallas as pl
from jax.experimental.pallas import tpu as pltpu
from jax.sharding import PartitionSpec as P

WINDOW = 128
HALF = 2 * WINDOW
CORES = 2
STAGE = 3
VMEM_LIMIT = 24 * 1024 * 1024
VMEM = pl.BlockSpec(memory_space=pltpu.VMEM)


def shifted(value, axis, by):
    devices = lax.axis_size(axis)
    return lax.ppermute(value, axis, [(i, (i + by) % devices) for i in range(devices)])


def swapped(value, bit):
    devices = lax.axis_size("col")
    return lax.ppermute(value, "col", [(i, i ^ bit) for i in range(devices)])


class Plan:
    def __init__(self, rounds, nwin):
        self.nwin = nwin
        self.phases = []
        for ph in range(rounds + 1):
            away = ph % 2 == 1
            entries = []
            self_carry = None
            if ph > 0:
                a, b = 2 * ph - 2, 2 * ph - 1
                if away:
                    entries += [(a, nwin - 1), None, (b, nwin - 1), (b, nwin)]
                    self_carry = (1, self.count(ph - 1) - 1)
                else:
                    entries += [(a, 1), (b, 0), (b, 1), None]
                    self_carry = (3, self.count(ph - 1) - (nwin - 1))
            if ph < rounds:
                base = 2 if away else 0
                for sweep in (2 * ph, 2 * ph + 1):
                    entries += [(sweep, base + k) for k in range(nwin - 1)]
            self.phases.append((entries, self_carry))
        groups = [[ph] for ph in range(rounds - 1)] + [[rounds - 1, rounds]]
        self.groups = []
        self.where = {}
        edge_at = 0
        for g, members in enumerate(groups):
            wanted = [w for ph in members for w in self.phases[ph][0] if w is not None]
            own = [w for w in wanted if w[1] < nwin]
            edge = [w for w in wanted if w[1] == nwin]
            place = 0
            for part in (own, edge):
                for i, w in enumerate(part):
                    self.where[w] = (g, place + i, place + len(part) + i // 2, i % 2)
                place += len(part) + (len(part) + 1) // 2
            own_tiles = len(own) + (len(own) + 1) // 2
            edge_tiles = place - own_tiles
            self.groups.append((own, edge, own_tiles, edge_tiles, edge_at))
            edge_at += edge_tiles
        self.edge_tiles = edge_at

    def count(self, ph):
        return len(self.phases[ph][0])


def pack_kernel(plan, refl_ref, *outs):
    size = refl_ref.shape[-1] - WINDOW
    mine = refl_ref.shape[-2]

    def fill(out, at, windows):
        for i, (sweep, k) in enumerate(windows):
            out[at + i] = refl_ref[sweep // 2, sweep % 2, k, :, :WINDOW]
        at += len(windows)
        for i in range(0, len(windows), 2):
            halves = []
            for sweep, k in windows[i : i + 2]:
                halves.append(refl_ref[sweep // 2, sweep % 2, k, :, WINDOW:])
            if len(halves) == 1:
                halves.append(jnp.zeros((mine, size), jnp.float32))
            out[at + i // 2] = jnp.concatenate(halves, -1)

    for group, out in zip(plan.groups, outs):
        fill(out, 0, group[0])
    for group in plan.groups:
        if group[1]:
            fill(outs[-1], group[4], [(sweep, 0) for sweep, _ in group[1]])


def pack(plan, refl):
    mine = refl.shape[3]
    counts = [group[2] for group in plan.groups] + [plan.edge_tiles]
    return pl.pallas_call(
        functools.partial(pack_kernel, plan),
        out_shape=tuple(jax.ShapeDtypeStruct((n, mine, WINDOW), jnp.float32) for n in counts),
        in_specs=[VMEM],
        out_specs=(VMEM,) * len(counts),
        compiler_params=pltpu.CompilerParams(vmem_limit_bytes=VMEM_LIMIT),
    )(refl)


def split(value):
    high = value.astype(jnp.bfloat16)
    return high, (value - high.astype(jnp.float32)).astype(jnp.bfloat16)


def fold(value):
    half = value.shape[1] // 2
    return value[:, :half] + value[:, half:]


def matrix_kernel(plan, ph, masked, *refs):
    entries, carry = plan.phases[ph]
    operands = list(refs)
    refs = operands[1:] if masked else operands
    offsets = operands[0][...] if masked else None
    old_ref = refs.pop(0) if carry else None
    tiles = refs.pop()
    out_ref = refs.pop()
    parts = refs
    here = lax.axis_index("col")
    if len(parts) == 2:
        for m in range(parts[0].shape[0]):
            other = lax.bitwise_xor(here, m * CORES)
            tiles[other] = parts[0][m]
            tiles[lax.bitwise_xor(other, 1)] = parts[1][m]
    else:
        tiles = parts[0]
    size = tiles.shape[0] * tiles.shape[2]
    last = lax.axis_index("row") == lax.axis_size("row") - 1
    lane = lax.broadcasted_iota(jnp.int32, (size, WINDOW), 1)
    row_id = lax.broadcasted_iota(jnp.int32, (WINDOW, WINDOW), 0)
    col_id = lax.broadcasted_iota(jnp.int32, (WINDOW, WINDOW), 1)
    unit = jnp.where(row_id == col_id, 1.0, 0.0).astype(jnp.float32)

    def first(window):
        sweep, k = window
        _, vec_tile, fac_tile, side = plan.where[window]
        vectors = tiles[:, vec_tile].reshape(size, WINDOW)
        factors = tiles[:, fac_tile].reshape(size, WINDOW)
        if k == plan.nwin - 1:
            start = offsets[sweep % 2 : sweep % 2 + 1, sweep // 2 : sweep // 2 + 1]
            limit = jnp.where(last, WINDOW - start, WINDOW)
            vectors = jnp.where(lane < limit, vectors, 0.0)
        rows_hi, rows_lo = split(vectors)
        pair = jnp.concatenate([rows_hi, rows_lo], 1)
        blank = jnp.zeros_like(pair)
        stack = [blank, pair, blank, pair] if side else [pair, blank, pair, blank]
        scaled = jnp.dot(
            jnp.concatenate(split(factors), 1),
            jnp.concatenate(stack, 0),
            preferred_element_type=jnp.float32,
        )
        return jnp.concatenate([rows_hi, rows_lo], 0), scaled

    def second(rows, scaled):
        pair = jnp.concatenate(split(fold(scaled)), 1)
        product = lax.dot_general(
            rows,
            jnp.concatenate([pair, pair], 0),
            (((0,), (0,)), ((), ())),
            preferred_element_type=jnp.float32,
        )
        return jnp.concatenate(split(unit - fold(product)), 1)

    fresh = [i for i, window in enumerate(entries) if window is not None]
    for at in range(0, len(fresh), STAGE):
        some = fresh[at : at + STAGE]
        halves = [first(entries[i]) for i in some]
        for i, half in zip(some, halves):
            out_ref[i] = second(*half)
    if carry:
        out_ref[carry[0]] = old_ref[carry[1]]


def matrices(plan, ph, offsets, before, parts):
    count = plan.count(ph)
    carried = (before,) if plan.phases[ph][1] else ()
    masked = any(w is not None and w[1] == plan.nwin - 1 for w in plan.phases[ph][0])
    operands = [*([offsets] if masked else []), *carried, *parts]
    whole = (sum(part.shape[0] for part in parts),) + parts[0].shape[1:]
    return pl.pallas_call(
        functools.partial(matrix_kernel, plan, ph, masked),
        out_shape=jax.ShapeDtypeStruct((count, WINDOW, 2 * WINDOW), jnp.bfloat16),
        in_specs=[VMEM] * len(operands),
        out_specs=VMEM,
        scratch_shapes=[pltpu.VMEM(whole, jnp.float32)],
        compiler_params=pltpu.CompilerParams(vmem_limit_bytes=VMEM_LIMIT),
        cost_estimate=pl.CostEstimate(
            flops=count * 12 * 64 * 128 * 192, bytes_accessed=count * 100000, transcendentals=0
        ),
    )(*operands)


def apply_windows(field, at, count, first, mats):
    rows = field[pl.ds(at, count * WINDOW), :]
    updated = []
    for k in range(count):
        pair = jnp.concatenate(split(rows[k * WINDOW : (k + 1) * WINDOW]), 1)
        both = jnp.dot(
            mats[first + k],
            jnp.concatenate([pair, pair], 0),
            preferred_element_type=jnp.float32,
        )
        updated.append(fold(both))
    field[pl.ds(at, count * WINDOW), :] = jnp.concatenate(updated, 0)


def phase_kernel(ph, rounds, nwin, nparts, offsets_ref, *refs):
    parts = refs[:nparts]
    mats = refs[nparts]
    outs = refs[nparts + 1 : -1]
    field = refs[-1]
    place = 0
    for part in parts:
        field[place : place + part.shape[0], :] = part[...]
        place += part.shape[0]
    offsets = offsets_ref[...]
    at = 0
    if ph > 0:
        a, b = offsets[0, ph - 1], offsets[1, ph - 1]
        step = jnp.where(b < a, 1, 0)
        start = nwin - 3 if ph % 2 else 1
        apply_windows(field, a + WINDOW * start, 1, 0, mats)
        start = nwin - 4 if ph % 2 else 0
        apply_windows(field, b + WINDOW * (start + step), 2, 1 + step, mats)
        at = 4
    if ph < rounds:
        a, b = offsets[0, ph], offsets[1, ph]
        step = jnp.where(b < a, 1, 0)
        apply_windows(field, a, nwin - 1, at, mats)
        apply_windows(field, b + WINDOW * step, nwin - 2, at + nwin - 1 + step, mats)
    place = 0
    for out in outs:
        out[...] = field[place : place + out.shape[0], :]
        place += out.shape[0]


def phase(ph, rounds, nwin, offsets, parts, mats, sizes):
    rows = sum(part.shape[0] for part in parts)
    cols = parts[0].shape[1]
    operands = [offsets, *parts, mats]
    return pl.pallas_call(
        functools.partial(phase_kernel, ph, rounds, nwin, len(parts)),
        out_shape=tuple(jax.ShapeDtypeStruct((n, cols), jnp.float32) for n in sizes),
        in_specs=[VMEM] * len(operands),
        out_specs=(VMEM,) * len(sizes),
        scratch_shapes=[pltpu.VMEM((rows, cols), jnp.float32)],
        compiler_params=pltpu.CompilerParams(vmem_limit_bytes=VMEM_LIMIT),
        cost_estimate=pl.CostEstimate(
            flops=8 * 6 * WINDOW * WINDOW * cols, bytes_accessed=2000000, transcendentals=0
        ),
    )(*operands)


def after(value, earlier):
    return lax.optimization_barrier((value, earlier))[0]


class Gather:
    def __init__(self, plan, packed, size):
        self.plan = plan
        self.size = size
        *own, edge = packed
        devices = lax.axis_size("col")
        self.chips = devices // CORES
        self.stepwise = edge.shape[1] % 8 == 0 and devices == 4 * CORES
        self.held = {}
        self.shared = {}
        if self.stepwise:
            self.direct(0, own[0])
        ahead = shifted(edge, "row", -1)
        self.own = []
        for (_, _, _, edge_tiles, edge_at), tiles in zip(plan.groups, own):
            if edge_tiles:
                tiles = jnp.concatenate([tiles, ahead[edge_at : edge_at + edge_tiles]], 0)
            self.own.append(tiles)
        if self.stepwise:
            self.doubled(1, self.own[1], self.held[0][-1])

    def direct(self, g, tiles):
        others = [swapped(tiles, CORES * m) for m in range(1, self.chips)]
        self.held[g] = [part.reshape((1,) + tiles.shape) for part in [tiles] + others]

    def doubled(self, g, tiles, earlier=None):
        pair = (tiles, swapped(tiles, CORES))
        pair = jnp.stack(pair if earlier is None else after(pair, earlier))
        self.held[g] = [pair, swapped(pair, 2 * CORES)]

    def together(self, groups):
        if self.stepwise:
            self.direct(groups[0], jnp.concatenate([self.own[g] for g in groups], 0))
            at = 0
            for g in groups:
                self.shared[g] = (groups[0], at, self.own[g].shape[0])
                at += self.own[g].shape[0]

    def receive(self, g, earlier=None, ready=None):
        if self.stepwise:
            source, at, count = self.shared.get(g, (g, 0, self.own[g].shape[0]))
            pieces = self.held[source]
            if ready is not None:
                pieces = after(pieces, ready)
            same = jnp.concatenate([piece[:, at : at + count] for piece in pieces], 0)
            if earlier is not None:
                same = after(same, earlier)
            return (same, swapped(same, 1))
        whole = lax.all_gather(self.own[g], "col", axis=0)
        whole = jnp.moveaxis(whole, 0, 1).reshape(1, whole.shape[1], self.size, WINDOW)
        return (whole,)


def shards(evecs, offsets, refl):
    rows = evecs.shape[0]
    nwin = rows // WINDOW
    rounds = refl.shape[0]
    size = refl.shape[4] - WINDOW
    plan = Plan(rounds, nwin)
    offsets = offsets.T
    groups = len(plan.groups)
    gather = Gather(plan, pack(plan, refl), size)
    rest = rows - HALF
    parts = [evecs]
    mats = None
    results = []
    gather.together(range(2, groups))
    for ph in range(rounds):
        if ph < groups:
            ready = results[min(ph, 2) - 1] if ph else None
            tiles = gather.receive(ph, {2: parts, 3: results[-1]}.get(ph) if ph else None, ready)
        mats = matrices(plan, ph, offsets, mats, tiles)
        away = ph % 2 == 1
        sizes = (rest, HALF) if away else (HALF, rest)
        halves = phase(ph, rounds, nwin, offsets, parts, mats, sizes)
        result, kept = (halves[1], halves[0]) if away else halves
        results.append(result)
        moved = shifted(result, "row", 1 if away else -1)
        parts = [moved, kept] if away else [kept, moved]
    mats = matrices(plan, rounds, offsets, mats, tiles)
    (result,) = phase(rounds, rounds, nwin, offsets, parts, mats, (rows,))
    if rounds % 2:
        result = jnp.concatenate([shifted(result[rest:], "row", 1), result[:rest]], 0)
    return result


def solution(mesh):
    placed = (P("row", "col"), P(), P(None, None, "row", "col", None))
    return jax.shard_map(
        shards, mesh=mesh, in_specs=placed, out_specs=P("row", "col"), check_vma=False
    )
```

profile of v0, /device:TPU:0, one launch (start us, length us, event | category | flops | bytes accessed | tf_op | source)
XLA Modules:
  0.0 52.7 jit_solution(2632577216337219041)
XLA Ops:
  0.0 0.9 %copy-done.1 = f32[4,2,4,8,192]{4,3,2,1,0:T(8,128)S(1)} copy-done((f32[4,2,4,8,192]{4,3,2,1,0:T(8,128)S(1)}, f32[4,2,4,8,192]{4,3,2,1,0:T(8,128)}, u32[]{:S(2)}) %copy-start.1) | copy-done | bytes 196632
  1.0 3.9 %collective-permute-start.5 = (f32[10,8,128]{2,1,0:T(8,128)S(1)}, f32[10,8,128]{2,1,0:T(8,128)S(1)}, u32[]{:S(2)}, u32[]{:S(2)}) collective-permute-start(f32[10,8,128]{2,1,0:T(8,128)S(1)} %get-tuple-element.32), channel_id=1, source_target_pairs={{0,24},{8,0},{16,8},{24,16},{1,25},{9,1},{17,9},{25,17},{2,26},{10... | collective-permute-start | bytes 122888 | tf_op jit(solution)/shard_map/ppermute | solution.py:20
  5.0 3.6 %collective-permute-start.2 = (f32[9,8,128]{2,1,0:T(8,128)S(1)}, f32[9,8,128]{2,1,0:T(8,128)S(1)}, u32[]{:S(2)}, u32[]{:S(2)}) collective-permute-start(f32[9,8,128]{2,1,0:T(8,128)S(1)} %get-tuple-element.28), channel_id=1, source_target_pairs={{0,6},{1,7},{2,4},{3,5},{4,2},{5,3},{6,0},{7,1},{8,14},{9,15},{10,... | collective-permute-start | bytes 110600 | tf_op jit(solution)/shard_map/ppermute | solution.py:25
  8.6 0.8 %collective-permute-start = (f32[9,8,128]{2,1,0:T(8,128)S(1)}, f32[9,8,128]{2,1,0:T(8,128)S(1)}, u32[]{:S(2)}, u32[]{:S(2)}) collective-permute-start(f32[9,8,128]{2,1,0:T(8,128)S(1)} %get-tuple-element.28), channel_id=1, source_target_pairs={{0,2},{1,3},{2,0},{3,1},{4,6},{5,7},{6,4},{7,5},{8,10},{9,11},{10,... | collective-permute-start | bytes 110600 | tf_op jit(solution)/shard_map/ppermute | solution.py:25
  9.4 1.3 %collective-permute-start.6 = (f32[14,8,128]{2,1,0:T(8,128)S(1)}, f32[14,8,128]{2,1,0:T(8,128)S(1)}, u32[]{:S(2)}, u32[]{:S(2)}) collective-permute-start(f32[14,8,128]{2,1,0:T(8,128)S(1)} %pad_maximum_fusion.5), channel_id=1, source_target_pairs={{0,2},{1,3},{2,0},{3,1},{4,6},{5,7},{6,4},{7,5},{8,10},{9,11},{10,... | collective-permute-start | bytes 172040 | tf_op jit(solution)/shard_map/ppermute | solution.py:25
  10.7 0.4 collective-permute-done.2
  11.1 2.4 %collective-permute-done.1 = f32[9,8,128]{2,1,0:T(8,128)S(1)} collective-permute-done((f32[9,8,128]{2,1,0:T(8,128)S(1)}, f32[9,8,128]{2,1,0:T(8,128)S(1)}, u32[]{:S(2)}, u32[]{:S(2)}) %collective-permute-start.1) | collective-permute-done | bytes 36896 | tf_op jit(solution)/shard_map/ppermute | solution.py:25
  13.6 0.4 collective-permute-done.6
  14.1 2.1 %collective-permute-start.7 = (f32[2,14,8,128]{3,2,1,0:T(8,128)S(1)}, f32[2,14,8,128]{3,2,1,0:T(8,128)S(1)}, u32[]{:S(2)}, u32[]{:S(2)}) collective-permute-start(f32[2,14,8,128]{3,2,1,0:T(8,128)S(1)} %pad_maximum_fusion.4), channel_id=1, source_target_pairs={{0,4},{1,5},{2,6},{3,7},{4,0},{5,1},{6,2},{7,3},{8,12},{9,13},{10,... | collective-permute-start | bytes 344072 | tf_op jit(solution)/shard_map/ppermute | solution.py:25
  16.2 0.6 %shard_map.38.refs_1_ = bf16[6,128,256]{2,1,0:T(8,128)(2,1)S(1)} custom-call(f32[4,9,8,128]{3,2,1,0:T(8,128)S(1)} %pad_maximum_fusion.2.refs_0_, f32[4,9,8,128]{3,2,1,0:T(8,128)S(1)} %collective-permute-done.3.refs_1_), custom_call_target="tpu_custom_call" | custom-call | flops 113246208 | bytes 600000 | tf_op jit(solution)/shard_map/pallas_call | solution.py:187
  16.8 0.7 %copy-done.2 = s32[4,2]{0,1:T(2,128)S(1)} copy-done((s32[4,2]{0,1:T(2,128)S(1)}, s32[4,2]{0,1:T(2,128)}, u32[]{:S(2)}) %copy-start.2) | copy-done | bytes 56
  17.5 0.5 shard_map.39
  18.0 4.5 %collective-permute-done.7 = f32[2,14,8,128]{3,2,1,0:T(8,128)S(1)} collective-permute-done((f32[2,14,8,128]{3,2,1,0:T(8,128)S(1)}, f32[2,14,8,128]{3,2,1,0:T(8,128)S(1)}, u32[]{:S(2)}, u32[]{:S(2)}) %collective-permute-start.7) | collective-permute-done | bytes 114720 | tf_op jit(solution)/shard_map/ppermute | solution.py:25
  22.6 0.6 %collective-permute-start.4 = (f32[256,128]{1,0:T(8,128)S(1)}, f32[256,128]{1,0:T(8,128)S(1)}, u32[]{:S(2)}, u32[]{:S(2)}) collective-permute-start(f32[256,128]{1,0:T(8,128)S(1)} %get-tuple-element.30), channel_id=1, source_target_pairs={{0,24},{8,0},{16,8},{24,16},{1,25},{9,1},{17,9},{25,17},{2,26},{10... | collective-permute-start | bytes 393224 | tf_op jit(solution)/shard_map/ppermute | solution.py:20
  23.3 2.5 %collective-permute-start.10 = (f32[33,8,128]{2,1,0:T(8,128)S(1)}, f32[33,8,128]{2,1,0:T(8,128)S(1)}, u32[]{:S(2)}, u32[]{:S(2)}) collective-permute-start(f32[33,8,128]{2,1,0:T(8,128)S(1)} %get-tuple-element.51), channel_id=1, source_target_pairs={{0,2},{1,3},{2,0},{3,1},{4,6},{5,7},{6,4},{7,5},{8,10},{9,11},{10,... | collective-permute-start | bytes 405512 | tf_op jit(solution)/shard_map/ppermute | solution.py:25
  25.8 1.9 %collective-permute-start.12 = (f32[33,8,128]{2,1,0:T(8,128)S(1)}, f32[33,8,128]{2,1,0:T(8,128)S(1)}, u32[]{:S(2)}, u32[]{:S(2)}) collective-permute-start(f32[33,8,128]{2,1,0:T(8,128)S(1)} %get-tuple-element.51), channel_id=1, source_target_pairs={{0,6},{1,7},{2,4},{3,5},{4,2},{5,3},{6,0},{7,1},{8,14},{9,15},{10,... | collective-permute-start | bytes 405512 | tf_op jit(solution)/shard_map/ppermute | solution.py:25
  27.7 0.9 %shard_map.40.refs_2_.refs_0_ = bf16[10,128,256]{2,1,0:T(8,128)(2,1)S(1)} custom-call(s32[2,4]{1,0:T(2,128)S(1)} %bitcast.13, bf16[6,128,256]{2,1,0:T(8,128)(2,1)S(1)} %shard_map.38.refs_1_, f32[4,14,8,128]{3,2,1,0:T(8,128)S(1)} %constant_dynamic-update-slice_fusion.refs_2_, f32[4,14,8,128]{3,2,1,0:T(8,128)S(1)} %collective-permute-done.8.refs_3_), custom_call_target="tpu_custom_call" | custom-call | flops 188743680 | bytes 1000000 | tf_op jit(solution)/shard_map/pallas_call | solution.py:187
  28.5 0.9 %shard_map.41 = (f32[256,128]{1,0:T(8,128)S(1)}, f32[256,128]{1,0:T(8,128)S(1)}) custom-call(s32[2,4]{1,0:T(2,128)S(1)} %bitcast.14, f32[256,128]{1,0:T(8,128)S(1)} %get-tuple-element.29.refs_0_, f32[256,128]{1,0:T(8,128)S(1)} %collective-permute-done.4.refs_1_, bf16[10,128,256]{2,1,0:T(8,128)(2,1)S(1)} %shard_map.40.refs_2_.refs_0_), custom_call_target="tpu_custom_call" | custom-call | flops 100663296 | bytes 2000000 | tf_op jit(solution)/shard_map/pallas_call | solution.py:248
  29.4 1.5 %collective-permute-start.9 = (f32[256,128]{1,0:T(8,128)S(1)}, f32[256,128]{1,0:T(8,128)S(1)}, u32[]{:S(2)}, u32[]{:S(2)}) collective-permute-start(f32[256,128]{1,0:T(8,128)S(1)} %get-tuple-element.37), channel_id=1, source_target_pairs={{0,8},{8,16},{16,24},{24,0},{1,9},{9,17},{17,25},{25,1},{2,10},{10... | collective-permute-start | bytes 393224 | tf_op jit(solution)/shard_map/ppermute | solution.py:20
  31.0 1.7 %collective-permute-done.11 = f32[33,8,128]{2,1,0:T(8,128)S(1)} collective-permute-done((f32[33,8,128]{2,1,0:T(8,128)S(1)}, f32[33,8,128]{2,1,0:T(8,128)S(1)}, u32[]{:S(2)}, u32[]{:S(2)}) %collective-permute-start.11) | collective-permute-done | bytes 135200 | tf_op jit(solution)/shard_map/ppermute | solution.py:25
  32.6 2.6 %collective-permute-done.10 = f32[33,8,128]{2,1,0:T(8,128)S(1)} collective-permute-done((f32[33,8,128]{2,1,0:T(8,128)S(1)}, f32[33,8,128]{2,1,0:T(8,128)S(1)}, u32[]{:S(2)}, u32[]{:S(2)}) %collective-permute-start.10) | collective-permute-done | bytes 135200 | tf_op jit(solution)/shard_map/ppermute | solution.py:25
  35.5 1.4 %collective-permute-done.13.refs_2_ = f32[4,14,8,128]{3,2,1,0:T(8,128)S(1)} collective-permute-done((f32[4,14,8,128]{3,2,1,0:T(8,128)S(1)}, f32[4,14,8,128]{3,2,1,0:T(8,128)S(1)}, u32[]{:S(2)}, u32[]{:S(2)}) %collective-permute-start.13) | collective-permute-done | bytes 229408 | tf_op jit(solution)/shard_map/ppermute | solution.py:25
  36.9 0.8 %shard_map.42.refs_2_.refs_1_ = bf16[10,128,256]{2,1,0:T(8,128)(2,1)S(1)} custom-call(bf16[10,128,256]{2,1,0:T(8,128)(2,1)S(1)} %shard_map.40.refs_2_.refs_0_, f32[4,14,8,128]{3,2,1,0:T(8,128)S(1)} %pad_maximum_fusion.1.refs_1_, f32[4,14,8,128]{3,2,1,0:T(8,128)S(1)} %collective-permute-done.13.refs_2_), custom_call_target="tpu_custom_call" | custom-call | flops 188743680 | bytes 1000000 | tf_op jit(solution)/shard_map/pallas_call | solution.py:187
  37.7 0.9 %shard_map.43 = (f32[256,128]{1,0:T(8,128)S(1)}, f32[256,128]{1,0:T(8,128)S(1)}) custom-call(s32[2,4]{1,0:T(2,128)S(1)} %bitcast.15, f32[256,128]{1,0:T(8,128)S(1)} %collective-permute-done.9.refs_0_, f32[256,128]{1,0:T(8,128)S(1)} %get-tuple-element.38.refs_1_, bf16[10,128,256]{2,1,0:T(8,128)(2,1)S(1)} %shard_map.42.refs_2_.refs_1_), custom_call_target="tpu_custom_call" | custom-call | flops 100663296 | bytes 2000000 | tf_op jit(solution)/shard_map/pallas_call | solution.py:248
  38.9 1.4 %collective-permute-start.14 = (f32[256,128]{1,0:T(8,128)S(1)}, f32[256,128]{1,0:T(8,128)S(1)}, u32[]{:S(2)}, u32[]{:S(2)}) collective-permute-start(f32[256,128]{1,0:T(8,128)S(1)} %get-tuple-element.47), channel_id=1, source_target_pairs={{0,24},{8,0},{16,8},{24,16},{1,25},{9,1},{17,9},{25,17},{2,26},{10... | collective-permute-start | bytes 393224 | tf_op jit(solution)/shard_map/ppermute | solution.py:20
  40.3 0.9 %shard_map.44.refs_2_.refs_0_ = bf16[10,128,256]{2,1,0:T(8,128)(2,1)S(1)} custom-call(s32[2,4]{1,0:T(2,128)S(1)} %bitcast.16, bf16[10,128,256]{2,1,0:T(8,128)(2,1)S(1)} %shard_map.42.refs_2_.refs_1_, f32[4,19,8,128]{3,2,1,0:T(8,128)S(1)} %pad_maximum_fusion.refs_2_.refs_1_, f32[4,19,8,128]{3,2,1,0:T(8,128)S(1)} %collective-permute-done.15.refs_3_.refs_2_), custom_call_target="tpu_custom_call" | custom-call | flops 188743680 | bytes 1000000 | tf_op jit(solution)/shard_map/pallas_call | solution.py:187
  41.2 3.4 %collective-permute-done.14.refs_1_ = f32[256,128]{1,0:T(8,128)S(1)} collective-permute-done((f32[256,128]{1,0:T(8,128)S(1)}, f32[256,128]{1,0:T(8,128)S(1)}, u32[]{:S(2)}, u32[]{:S(2)}) %collective-permute-start.14) | collective-permute-done | bytes 131104 | tf_op jit(solution)/shard_map/ppermute | solution.py:20
  44.6 0.9 %shard_map.45 = (f32[256,128]{1,0:T(8,128)S(1)}, f32[256,128]{1,0:T(8,128)S(1)}) custom-call(s32[2,4]{1,0:T(2,128)S(1)} %bitcast.17, f32[256,128]{1,0:T(8,128)S(1)} %get-tuple-element.46.refs_0_, f32[256,128]{1,0:T(8,128)S(1)} %collective-permute-done.14.refs_1_, bf16[10,128,256]{2,1,0:T(8,128)(2,1)S(1)} %shard_map.44.refs_2_.refs_0_), custom_call_target="tpu_custom_call" | custom-call | flops 100663296 | bytes 2000000 | tf_op jit(solution)/shard_map/pallas_call | solution.py:248
  45.6 2.4 %collective-permute-start.16 = (f32[256,128]{1,0:T(8,128)S(1)}, f32[256,128]{1,0:T(8,128)S(1)}, u32[]{:S(2)}, u32[]{:S(2)}) collective-permute-start(f32[256,128]{1,0:T(8,128)S(1)} %get-tuple-element.49), channel_id=1, source_target_pairs={{0,8},{8,16},{16,24},{24,0},{1,9},{9,17},{17,25},{25,1},{2,10},{10... | collective-permute-start | bytes 393224 | tf_op jit(solution)/shard_map/ppermute | solution.py:20
  48.0 0.4 shard_map.46.refs_2_
  48.4 3.1 %collective-permute-done.16.refs_0_ = f32[256,128]{1,0:T(8,128)S(1)} collective-permute-done((f32[256,128]{1,0:T(8,128)S(1)}, f32[256,128]{1,0:T(8,128)S(1)}, u32[]{:S(2)}, u32[]{:S(2)}) %collective-permute-start.16) | collective-permute-done | bytes 131104 | tf_op jit(solution)/shard_map/ppermute | solution.py:20
  51.5 1.2 %shard_map.47 = f32[512,128]{1,0:T(8,128)} custom-call(s32[2,4]{1,0:T(2,128)S(1)} %bitcast.18, f32[256,128]{1,0:T(8,128)S(1)} %collective-permute-done.16.refs_0_, f32[256,128]{1,0:T(8,128)S(1)} %get-tuple-element.50.refs_1_, bf16[4,128,256]{2,1,0:T(8,128)(2,1)S(1)} %shard_map.46.refs_2_), custom_call_target="tpu_custom_call" | custom-call | flops 100663296 | bytes 2000000 | tf_op jit(solution)/shard_map/pallas_call | solution.py:248
  (36 shorter events, 0.8 us)
Async XLA Ops:
  0.0 0.9 %copy-start.1 = (f32[4,2,4,8,192]{4,3,2,1,0:T(8,128)S(1)}, f32[4,2,4,8,192]{4,3,2,1,0:T(8,128)}, u32[]{:S(2)}) copy-start(f32[4,2,4,8,192]{4,3,2,1,0:T(8,128)} %refl_ref.1) | copy-start | bytes 589828
  1.0 8.3 %collective-permute-start.5 = (f32[10,8,128]{2,1,0:T(8,128)S(1)}, f32[10,8,128]{2,1,0:T(8,128)S(1)}, u32[]{:S(2)}, u32[]{:S(2)}) collective-permute-start(f32[10,8,128]{2,1,0:T(8,128)S(1)} %get-tuple-element.32), channel_id=1, source_target_pairs={{0,24},{8,0},{16,8},{24,16},{1,25},{9,1},{17,9},{25,17},{2,26},{10... | collective-permute-start | bytes 122888 | tf_op jit(solution)/shard_map/ppermute | solution.py:20
  5.0 6.1 %collective-permute-start.2 = (f32[9,8,128]{2,1,0:T(8,128)S(1)}, f32[9,8,128]{2,1,0:T(8,128)S(1)}, u32[]{:S(2)}, u32[]{:S(2)}) collective-permute-start(f32[9,8,128]{2,1,0:T(8,128)S(1)} %get-tuple-element.28), channel_id=1, source_target_pairs={{0,6},{1,7},{2,4},{3,5},{4,2},{5,3},{6,0},{7,1},{8,14},{9,15},{10,... | collective-permute-start | bytes 110600 | tf_op jit(solution)/shard_map/ppermute | solution.py:25
  8.6 5.0 %collective-permute-start.1 = (f32[9,8,128]{2,1,0:T(8,128)S(1)}, f32[9,8,128]{2,1,0:T(8,128)S(1)}, u32[]{:S(2)}, u32[]{:S(2)}) collective-permute-start(f32[9,8,128]{2,1,0:T(8,128)S(1)} %get-tuple-element.28), channel_id=1, source_target_pairs={{0,4},{1,5},{2,6},{3,7},{4,0},{5,1},{6,2},{7,3},{8,12},{9,13},{10,... | collective-permute-start | bytes 110600 | tf_op jit(solution)/shard_map/ppermute | solution.py:25
  8.6 5.0 %collective-permute-start = (f32[9,8,128]{2,1,0:T(8,128)S(1)}, f32[9,8,128]{2,1,0:T(8,128)S(1)}, u32[]{:S(2)}, u32[]{:S(2)}) collective-permute-start(f32[9,8,128]{2,1,0:T(8,128)S(1)} %get-tuple-element.28), channel_id=1, source_target_pairs={{0,2},{1,3},{2,0},{3,1},{4,6},{5,7},{6,4},{7,5},{8,10},{9,11},{10,... | collective-permute-start | bytes 110600 | tf_op jit(solution)/shard_map/ppermute | solution.py:25
  9.4 4.6 %collective-permute-start.6 = (f32[14,8,128]{2,1,0:T(8,128)S(1)}, f32[14,8,128]{2,1,0:T(8,128)S(1)}, u32[]{:S(2)}, u32[]{:S(2)}) collective-permute-start(f32[14,8,128]{2,1,0:T(8,128)S(1)} %pad_maximum_fusion.5), channel_id=1, source_target_pairs={{0,2},{1,3},{2,0},{3,1},{4,6},{5,7},{6,4},{7,5},{8,10},{9,11},{10,... | collective-permute-start | bytes 172040 | tf_op jit(solution)/shard_map/ppermute | solution.py:25
  13.6 2.6 %collective-permute-start.3 = (f32[4,9,8,128]{3,2,1,0:T(8,128)S(1)}, f32[4,9,8,128]{3,2,1,0:T(8,128)S(1)}, u32[]{:S(2)}, u32[]{:S(2)}) collective-permute-start(f32[4,9,8,128]{3,2,1,0:T(8,128)S(1)} %pad_maximum_fusion.2.refs_0_), channel_id=1, source_target_pairs={{0,1},{1,0},{2,3},{3,2},{4,5},{5,4},{6,7},{7,6},{8,9},{9,8},{10,11... | collective-permute-start | bytes 442376 | tf_op jit(solution)/shard_map/ppermute | solution.py:25
  14.0 2.8 %copy-start = (f32[512,128]{1,0:T(8,128)S(1)}, f32[512,128]{1,0:T(8,128)}, u32[]{:S(2)}) copy-start(f32[512,128]{1,0:T(8,128)} %refs_0_.1) | copy-start | bytes 786436
  14.1 8.4 %collective-permute-start.7 = (f32[2,14,8,128]{3,2,1,0:T(8,128)S(1)}, f32[2,14,8,128]{3,2,1,0:T(8,128)S(1)}, u32[]{:S(2)}, u32[]{:S(2)}) collective-permute-start(f32[2,14,8,128]{3,2,1,0:T(8,128)S(1)} %pad_maximum_fusion.4), channel_id=1, source_target_pairs={{0,4},{1,5},{2,6},{3,7},{4,0},{5,1},{6,2},{7,3},{8,12},{9,13},{10,... | collective-permute-start | bytes 344072 | tf_op jit(solution)/shard_map/ppermute | solution.py:25
  16.8 0.7 %copy-start.2 = (s32[4,2]{0,1:T(2,128)S(1)}, s32[4,2]{0,1:T(2,128)}, u32[]{:S(2)}) copy-start(s32[4,2]{0,1:T(2,128)} %param.4) | copy-start | bytes 100
  22.5 5.1 %collective-permute-start.8 = (f32[4,14,8,128]{3,2,1,0:T(8,128)S(1)}, f32[4,14,8,128]{3,2,1,0:T(8,128)S(1)}, u32[]{:S(2)}, u32[]{:S(2)}) collective-permute-start(f32[4,14,8,128]{3,2,1,0:T(8,128)S(1)} %constant_dynamic-update-slice_fusion.refs_2_), channel_id=1, source_target_pairs={{0,1},{1,0},{2,3},{3,2},{4,5},{5,4},{6,7},{7,6},{8,9},{9,8},{10,11... | collective-permute-start | bytes 688136 | tf_op jit(solution)/shard_map/ppermute | solution.py:25
  22.6 5.9 %collective-permute-start.4 = (f32[256,128]{1,0:T(8,128)S(1)}, f32[256,128]{1,0:T(8,128)S(1)}, u32[]{:S(2)}, u32[]{:S(2)}) collective-permute-start(f32[256,128]{1,0:T(8,128)S(1)} %get-tuple-element.30), channel_id=1, source_target_pairs={{0,24},{8,0},{16,8},{24,16},{1,25},{9,1},{17,9},{25,17},{2,26},{10... | collective-permute-start | bytes 393224 | tf_op jit(solution)/shard_map/ppermute | solution.py:20
  23.2 9.4 %collective-permute-start.11 = (f32[33,8,128]{2,1,0:T(8,128)S(1)}, f32[33,8,128]{2,1,0:T(8,128)S(1)}, u32[]{:S(2)}, u32[]{:S(2)}) collective-permute-start(f32[33,8,128]{2,1,0:T(8,128)S(1)} %get-tuple-element.51), channel_id=1, source_target_pairs={{0,4},{1,5},{2,6},{3,7},{4,0},{5,1},{6,2},{7,3},{8,12},{9,13},{10,... | collective-permute-start | bytes 405512 | tf_op jit(solution)/shard_map/ppermute | solution.py:25
  23.3 11.9 %collective-permute-start.10 = (f32[33,8,128]{2,1,0:T(8,128)S(1)}, f32[33,8,128]{2,1,0:T(8,128)S(1)}, u32[]{:S(2)}, u32[]{:S(2)}) collective-permute-start(f32[33,8,128]{2,1,0:T(8,128)S(1)} %get-tuple-element.51), channel_id=1, source_target_pairs={{0,2},{1,3},{2,0},{3,1},{4,6},{5,7},{6,4},{7,5},{8,10},{9,11},{10,... | collective-permute-start | bytes 405512 | tf_op jit(solution)/shard_map/ppermute | solution.py:25
  25.8 9.4 %collective-permute-start.12 = (f32[33,8,128]{2,1,0:T(8,128)S(1)}, f32[33,8,128]{2,1,0:T(8,128)S(1)}, u32[]{:S(2)}, u32[]{:S(2)}) collective-permute-start(f32[33,8,128]{2,1,0:T(8,128)S(1)} %get-tuple-element.51), channel_id=1, source_target_pairs={{0,6},{1,7},{2,4},{3,5},{4,2},{5,3},{6,0},{7,1},{8,14},{9,15},{10,... | collective-permute-start | bytes 405512 | tf_op jit(solution)/shard_map/ppermute | solution.py:25
  29.4 6.0 %collective-permute-start.9 = (f32[256,128]{1,0:T(8,128)S(1)}, f32[256,128]{1,0:T(8,128)S(1)}, u32[]{:S(2)}, u32[]{:S(2)}) collective-permute-start(f32[256,128]{1,0:T(8,128)S(1)} %get-tuple-element.37), channel_id=1, source_target_pairs={{0,8},{8,16},{16,24},{24,0},{1,9},{9,17},{17,25},{25,1},{2,10},{10... | collective-permute-start | bytes 393224 | tf_op jit(solution)/shard_map/ppermute | solution.py:20
  35.4 1.5 %collective-permute-start.13 = (f32[4,14,8,128]{3,2,1,0:T(8,128)S(1)}, f32[4,14,8,128]{3,2,1,0:T(8,128)S(1)}, u32[]{:S(2)}, u32[]{:S(2)}) collective-permute-start(f32[4,14,8,128]{3,2,1,0:T(8,128)S(1)} %pad_maximum_fusion.1.refs_1_), channel_id=1, source_target_pairs={{0,1},{1,0},{2,3},{3,2},{4,5},{5,4},{6,7},{7,6},{8,9},{9,8},{10,11... | collective-permute-start | bytes 688136 | tf_op jit(solution)/shard_map/ppermute | solution.py:25
  38.6 1.7 %collective-permute-start.15 = (f32[4,19,8,128]{3,2,1,0:T(8,128)S(1)}, f32[4,19,8,128]{3,2,1,0:T(8,128)S(1)}, u32[]{:S(2)}, u32[]{:S(2)}) collective-permute-start(f32[4,19,8,128]{3,2,1,0:T(8,128)S(1)} %pad_maximum_fusion.refs_2_.refs_1_), channel_id=1, source_target_pairs={{0,1},{1,0},{2,3},{3,2},{4,5},{5,4},{6,7},{7,6},{8,9},{9,8},{10,11... | collective-permute-start | bytes 933896 | tf_op jit(solution)/shard_map/ppermute | solution.py:25
  38.9 5.8 %collective-permute-start.14 = (f32[256,128]{1,0:T(8,128)S(1)}, f32[256,128]{1,0:T(8,128)S(1)}, u32[]{:S(2)}, u32[]{:S(2)}) collective-permute-start(f32[256,128]{1,0:T(8,128)S(1)} %get-tuple-element.47), channel_id=1, source_target_pairs={{0,24},{8,0},{16,8},{24,16},{1,25},{9,1},{17,9},{25,17},{2,26},{10... | collective-permute-start | bytes 393224 | tf_op jit(solution)/shard_map/ppermute | solution.py:20
  45.6 5.9 %collective-permute-start.16 = (f32[256,128]{1,0:T(8,128)S(1)}, f32[256,128]{1,0:T(8,128)S(1)}, u32[]{:S(2)}, u32[]{:S(2)}) collective-permute-start(f32[256,128]{1,0:T(8,128)S(1)} %get-tuple-element.49), channel_id=1, source_target_pairs={{0,8},{8,16},{16,24},{24,0},{1,9},{9,17},{17,25},{25,1},{2,10},{10... | collective-permute-start | bytes 393224 | tf_op jit(solution)/shard_map/ppermute | solution.py:20
where the time goes:
time: 53 us; the launch traced here: 52.7 us
  starting transfers between devices  22.6 us (43%)
  waiting for transfers between devices  19.9 us (38%)
  Pallas kernels  8.2 us (15%)
  local copies, waits for them, and re-layouts  1.69 us (3%)
    ppermute x12, waiting for transfers between devices, swapped(): return lax.ppermute(value, 'col', [(i, i ^ bit) for i in range(devices)])  13.4 us
    ppermute x12, starting transfers between devices, swapped(): return lax.ppermute(value, 'col', [(i, i ^ bit) for i in range(devices)])  12.6 us
    ppermute x5, starting transfers between devices, shifted(): lax.ppermute(value, axis, [(i, (i + by) % devices) for i in range(devices)])  9.92 us
    ppermute x5, waiting for transfers between devices, shifted(): lax.ppermute(value, axis, [(i, (i + by) % devices) for i in range(devices)])  6.54 us
    pallas_call x5, Pallas kernels, phase(): pl.pallas_call(functools.partial(phase_kernel, ph, rounds, nwin, len(part...  4.46 us
    pallas_call x5, Pallas kernels, matrices(): pl.pallas_call(functools.partial(matrix_kernel, plan, ph, masked), out_sh...  3.65 us
    unnamed x7, local copies, waits for them, and re-layouts  1.63 us
  transfers between devices with their start and end apart: 17, of which 10 were waited for; matrix products, arithmetic and copies ran while one was open for 0% of the time, Pallas kernels for 8%

commit v1 on v0

--- a/solution.py
+++ b/solution.py
@@ -199,16 +199,16 @@
 
 def apply_windows(field, at, count, first, mats):
     rows = field[pl.ds(at, count * WINDOW), :]
-    updated = []
+    stacks = []
     for k in range(count):
         pair = jnp.concatenate(split(rows[k * WINDOW : (k + 1) * WINDOW]), 1)
-        both = jnp.dot(
-            mats[first + k],
-            jnp.concatenate([pair, pair], 0),
-            preferred_element_type=jnp.float32,
-        )
-        updated.append(fold(both))
-    field[pl.ds(at, count * WINDOW), :] = jnp.concatenate(updated, 0)
+        stacks.append(jnp.concatenate([pair, pair], 0))
+    products = [
+        jnp.dot(mats[first + k], stack, preferred_element_type=jnp.float32)
+        for k, stack in enumerate(stacks)
+    ]
+    updated = jnp.concatenate([fold(product) for product in products], 0)
+    field[pl.ds(at, count * WINDOW), :] = updated
 
 
 def phase_kernel(ph, rounds, nwin, nparts, offsets_ref, *refs):
@@ -327,12 +327,12 @@
     rest = rows - HALF
     parts = [evecs]
     mats = None
-    results = []
+    results, movements = [], []
     gather.together(range(2, groups))
     for ph in range(rounds):
         if ph < groups:
             ready = results[min(ph, 2) - 1] if ph else None
-            tiles = gather.receive(ph, {2: parts, 3: results[-1]}.get(ph) if ph else None, ready)
+            tiles = gather.receive(ph, movements[1] if ph > 1 else None, ready)
         mats = matrices(plan, ph, offsets, mats, tiles)
         away = ph % 2 == 1
         sizes = (rest, HALF) if away else (HALF, rest)
@@ -340,6 +340,7 @@
         result, kept = (halves[1], halves[0]) if away else halves
         results.append(result)
         moved = shifted(result, "row", 1 if away else -1)
+        movements.append(moved)
         parts = [moved, kept] if away else [kept, moved]
     mats = matrices(plan, rounds, offsets, mats, tiles)
     (result,) = phase(rounds, rounds, nwin, offsets, parts, mats, (rows,))

time: 53 us -> 52.7 us (level)
  waiting for transfers between devices: 19.9 us -> 19.1 us
    ppermute x12, waiting for transfers between devices: 13.4 us -> 12.9 us  [swapped(): return lax.ppermute(value, 'col', [(i, i ^ bit) for i in range(devices)])]
  transfers between devices with their start and end apart: 17 -> 17, of which waited for: 10 -> 9; matrix products, arithmetic and copies ran while one was open for 0% -> 0% of each run, Pallas kernels for 8% -> 11%
where the time goes in v1:
time: 52.7 us; the launch traced here: 52.4 us
  starting transfers between devices  23 us (44%)
  waiting for transfers between devices  19.1 us (36%)
  Pallas kernels  8.21 us (16%)
  local copies, waits for them, and re-layouts  1.69 us (3%)
    ppermute x12, starting transfers between devices, swapped(): return lax.ppermute(value, 'col', [(i, i ^ bit) for i in range(devices)])  13 us
    ppermute x12, waiting for transfers between devices, swapped(): return lax.ppermute(value, 'col', [(i, i ^ bit) for i in range(devices)])  12.9 us
    ppermute x5, starting transfers between devices, shifted(): lax.ppermute(value, axis, [(i, (i + by) % devices) for i in range(devices)])  9.99 us
    ppermute x5, waiting for transfers between devices, shifted(): lax.ppermute(value, axis, [(i, (i + by) % devices) for i in range(devices)])  6.25 us
    pallas_call x5, Pallas kernels, phase(): pl.pallas_call(functools.partial(phase_kernel, ph, rounds, nwin, len(part...  4.46 us
    pallas_call x5, Pallas kernels, matrices(): pl.pallas_call(functools.partial(matrix_kernel, plan, ph, masked), out_sh...  3.66 us
    unnamed x7, local copies, waits for them, and re-layouts  1.63 us
  transfers between devices with their start and end apart: 17, of which 9 were waited for; matrix products, arithmetic and copies ran while one was open for 0% of the time, Pallas kernels for 11%

profile of v1, /device:TPU:0, one launch (start us, length us, event | category | flops | bytes accessed | tf_op | source)
XLA Modules:
  0.0 52.4 jit_solution(6848859860488046200)
XLA Ops:
  0.0 0.9 %copy-done.1 = f32[4,2,4,8,192]{4,3,2,1,0:T(8,128)S(1)} copy-done((f32[4,2,4,8,192]{4,3,2,1,0:T(8,128)S(1)}, f32[4,2,4,8,192]{4,3,2,1,0:T(8,128)}, u32[]{:S(2)}) %copy-start.1) | copy-done | bytes 196632
  1.0 3.9 %collective-permute-start.5 = (f32[10,8,128]{2,1,0:T(8,128)S(1)}, f32[10,8,128]{2,1,0:T(8,128)S(1)}, u32[]{:S(2)}, u32[]{:S(2)}) collective-permute-start(f32[10,8,128]{2,1,0:T(8,128)S(1)} %get-tuple-element.32), channel_id=1, source_target_pairs={{0,24},{8,0},{16,8},{24,16},{1,25},{9,1},{17,9},{25,17},{2,26},{10... | collective-permute-start | bytes 122888 | tf_op jit(solution)/shard_map/ppermute | solution.py:20
  5.0 3.6 %collective-permute-start.2 = (f32[9,8,128]{2,1,0:T(8,128)S(1)}, f32[9,8,128]{2,1,0:T(8,128)S(1)}, u32[]{:S(2)}, u32[]{:S(2)}) collective-permute-start(f32[9,8,128]{2,1,0:T(8,128)S(1)} %get-tuple-element.28), channel_id=1, source_target_pairs={{0,6},{1,7},{2,4},{3,5},{4,2},{5,3},{6,0},{7,1},{8,14},{9,15},{10,... | collective-permute-start | bytes 110600 | tf_op jit(solution)/shard_map/ppermute | solution.py:25
  8.6 0.8 %collective-permute-start = (f32[9,8,128]{2,1,0:T(8,128)S(1)}, f32[9,8,128]{2,1,0:T(8,128)S(1)}, u32[]{:S(2)}, u32[]{:S(2)}) collective-permute-start(f32[9,8,128]{2,1,0:T(8,128)S(1)} %get-tuple-element.28), channel_id=1, source_target_pairs={{0,2},{1,3},{2,0},{3,1},{4,6},{5,7},{6,4},{7,5},{8,10},{9,11},{10,... | collective-permute-start | bytes 110600 | tf_op jit(solution)/shard_map/ppermute | solution.py:25
  9.4 1.3 %collective-permute-start.6 = (f32[14,8,128]{2,1,0:T(8,128)S(1)}, f32[14,8,128]{2,1,0:T(8,128)S(1)}, u32[]{:S(2)}, u32[]{:S(2)}) collective-permute-start(f32[14,8,128]{2,1,0:T(8,128)S(1)} %pad_maximum_fusion.5), channel_id=1, source_target_pairs={{0,2},{1,3},{2,0},{3,1},{4,6},{5,7},{6,4},{7,5},{8,10},{9,11},{10,... | collective-permute-start | bytes 172040 | tf_op jit(solution)/shard_map/ppermute | solution.py:25
  10.7 0.4 collective-permute-done.2
  11.1 2.4 %collective-permute-done.1 = f32[9,8,128]{2,1,0:T(8,128)S(1)} collective-permute-done((f32[9,8,128]{2,1,0:T(8,128)S(1)}, f32[9,8,128]{2,1,0:T(8,128)S(1)}, u32[]{:S(2)}, u32[]{:S(2)}) %collective-permute-start.1) | collective-permute-done | bytes 36896 | tf_op jit(solution)/shard_map/ppermute | solution.py:25
  14.1 2.1 %collective-permute-start.7 = (f32[2,14,8,128]{3,2,1,0:T(8,128)S(1)}, f32[2,14,8,128]{3,2,1,0:T(8,128)S(1)}, u32[]{:S(2)}, u32[]{:S(2)}) collective-permute-start(f32[2,14,8,128]{3,2,1,0:T(8,128)S(1)} %pad_maximum_fusion.4), channel_id=1, source_target_pairs={{0,4},{1,5},{2,6},{3,7},{4,0},{5,1},{6,2},{7,3},{8,12},{9,13},{10,... | collective-permute-start | bytes 344072 | tf_op jit(solution)/shard_map/ppermute | solution.py:25
  16.2 0.6 %shard_map.38.refs_1_ = bf16[6,128,256]{2,1,0:T(8,128)(2,1)S(1)} custom-call(f32[4,9,8,128]{3,2,1,0:T(8,128)S(1)} %pad_maximum_fusion.2.refs_0_, f32[4,9,8,128]{3,2,1,0:T(8,128)S(1)} %collective-permute-done.3.refs_1_), custom_call_target="tpu_custom_call" | custom-call | flops 113246208 | bytes 600000 | tf_op jit(solution)/shard_map/pallas_call | solution.py:187
  16.8 0.7 %copy-done.2 = s32[4,2]{0,1:T(2,128)S(1)} copy-done((s32[4,2]{0,1:T(2,128)S(1)}, s32[4,2]{0,1:T(2,128)}, u32[]{:S(2)}) %copy-start.2) | copy-done | bytes 56
  17.5 0.5 shard_map.39
  18.0 4.5 %collective-permute-done.7 = f32[2,14,8,128]{3,2,1,0:T(8,128)S(1)} collective-permute-done((f32[2,14,8,128]{3,2,1,0:T(8,128)S(1)}, f32[2,14,8,128]{3,2,1,0:T(8,128)S(1)}, u32[]{:S(2)}, u32[]{:S(2)}) %collective-permute-start.7) | collective-permute-done | bytes 114720 | tf_op jit(solution)/shard_map/ppermute | solution.py:25
  22.6 0.6 %collective-permute-start.4 = (f32[256,128]{1,0:T(8,128)S(1)}, f32[256,128]{1,0:T(8,128)S(1)}, u32[]{:S(2)}, u32[]{:S(2)}) collective-permute-start(f32[256,128]{1,0:T(8,128)S(1)} %get-tuple-element.30), channel_id=1, source_target_pairs={{0,24},{8,0},{16,8},{24,16},{1,25},{9,1},{17,9},{25,17},{2,26},{10... | collective-permute-start | bytes 393224 | tf_op jit(solution)/shard_map/ppermute | solution.py:20
  23.3 2.5 %collective-permute-start.10 = (f32[33,8,128]{2,1,0:T(8,128)S(1)}, f32[33,8,128]{2,1,0:T(8,128)S(1)}, u32[]{:S(2)}, u32[]{:S(2)}) collective-permute-start(f32[33,8,128]{2,1,0:T(8,128)S(1)} %get-tuple-element.51), channel_id=1, source_target_pairs={{0,2},{1,3},{2,0},{3,1},{4,6},{5,7},{6,4},{7,5},{8,10},{9,11},{10,... | collective-permute-start | bytes 405512 | tf_op jit(solution)/shard_map/ppermute | solution.py:25
  25.8 1.9 %collective-permute-start.12 = (f32[33,8,128]{2,1,0:T(8,128)S(1)}, f32[33,8,128]{2,1,0:T(8,128)S(1)}, u32[]{:S(2)}, u32[]{:S(2)}) collective-permute-start(f32[33,8,128]{2,1,0:T(8,128)S(1)} %get-tuple-element.51), channel_id=1, source_target_pairs={{0,6},{1,7},{2,4},{3,5},{4,2},{5,3},{6,0},{7,1},{8,14},{9,15},{10,... | collective-permute-start | bytes 405512 | tf_op jit(solution)/shard_map/ppermute | solution.py:25
  27.7 0.9 %shard_map.40.refs_2_.refs_0_ = bf16[10,128,256]{2,1,0:T(8,128)(2,1)S(1)} custom-call(s32[2,4]{1,0:T(2,128)S(1)} %bitcast.13, bf16[6,128,256]{2,1,0:T(8,128)(2,1)S(1)} %shard_map.38.refs_1_, f32[4,14,8,128]{3,2,1,0:T(8,128)S(1)} %constant_dynamic-update-slice_fusion.refs_2_, f32[4,14,8,128]{3,2,1,0:T(8,128)S(1)} %collective-permute-done.8.refs_3_), custom_call_target="tpu_custom_call" | custom-call | flops 188743680 | bytes 1000000 | tf_op jit(solution)/shard_map/pallas_call | solution.py:187
  28.5 0.9 %shard_map.41 = (f32[256,128]{1,0:T(8,128)S(1)}, f32[256,128]{1,0:T(8,128)S(1)}) custom-call(s32[2,4]{1,0:T(2,128)S(1)} %bitcast.14, f32[256,128]{1,0:T(8,128)S(1)} %get-tuple-element.29.refs_0_, f32[256,128]{1,0:T(8,128)S(1)} %collective-permute-done.4.refs_1_, bf16[10,128,256]{2,1,0:T(8,128)(2,1)S(1)} %shard_map.40.refs_2_.refs_0_), custom_call_target="tpu_custom_call" | custom-call | flops 100663296 | bytes 2000000 | tf_op jit(solution)/shard_map/pallas_call | solution.py:248
  29.4 1.5 %collective-permute-start.9 = (f32[256,128]{1,0:T(8,128)S(1)}, f32[256,128]{1,0:T(8,128)S(1)}, u32[]{:S(2)}, u32[]{:S(2)}) collective-permute-start(f32[256,128]{1,0:T(8,128)S(1)} %get-tuple-element.37), channel_id=1, source_target_pairs={{0,8},{8,16},{16,24},{24,0},{1,9},{9,17},{17,25},{25,1},{2,10},{10... | collective-permute-start | bytes 393224 | tf_op jit(solution)/shard_map/ppermute | solution.py:20
  31.0 1.7 %collective-permute-done.11 = f32[33,8,128]{2,1,0:T(8,128)S(1)} collective-permute-done((f32[33,8,128]{2,1,0:T(8,128)S(1)}, f32[33,8,128]{2,1,0:T(8,128)S(1)}, u32[]{:S(2)}, u32[]{:S(2)}) %collective-permute-start.11) | collective-permute-done | bytes 135200 | tf_op jit(solution)/shard_map/ppermute | solution.py:25
  32.6 2.6 %collective-permute-done.10 = f32[33,8,128]{2,1,0:T(8,128)S(1)} collective-permute-done((f32[33,8,128]{2,1,0:T(8,128)S(1)}, f32[33,8,128]{2,1,0:T(8,128)S(1)}, u32[]{:S(2)}, u32[]{:S(2)}) %collective-permute-start.10) | collective-permute-done | bytes 135200 | tf_op jit(solution)/shard_map/ppermute | solution.py:25
  35.5 0.6 %collective-permute-start.15 = (f32[4,19,8,128]{3,2,1,0:T(8,128)S(1)}, f32[4,19,8,128]{3,2,1,0:T(8,128)S(1)}, u32[]{:S(2)}, u32[]{:S(2)}) collective-permute-start(f32[4,19,8,128]{3,2,1,0:T(8,128)S(1)} %pad_maximum_fusion.refs_2_.refs_1_), channel_id=1, source_target_pairs={{0,1},{1,0},{2,3},{3,2},{4,5},{5,4},{6,7},{7,6},{8,9},{9,8},{10,11... | collective-permute-start | bytes 933896 | tf_op jit(solution)/shard_map/ppermute | solution.py:25
  36.0 0.9 %collective-permute-done.13.refs_2_ = f32[4,14,8,128]{3,2,1,0:T(8,128)S(1)} collective-permute-done((f32[4,14,8,128]{3,2,1,0:T(8,128)S(1)}, f32[4,14,8,128]{3,2,1,0:T(8,128)S(1)}, u32[]{:S(2)}, u32[]{:S(2)}) %collective-permute-start.13) | collective-permute-done | bytes 229408 | tf_op jit(solution)/shard_map/ppermute | solution.py:25
  36.9 0.8 %shard_map.42.refs_2_.refs_1_ = bf16[10,128,256]{2,1,0:T(8,128)(2,1)S(1)} custom-call(bf16[10,128,256]{2,1,0:T(8,128)(2,1)S(1)} %shard_map.40.refs_2_.refs_0_, f32[4,14,8,128]{3,2,1,0:T(8,128)S(1)} %pad_maximum_fusion.1.refs_1_, f32[4,14,8,128]{3,2,1,0:T(8,128)S(1)} %collective-permute-done.13.refs_2_), custom_call_target="tpu_custom_call" | custom-call | flops 188743680 | bytes 1000000 | tf_op jit(solution)/shard_map/pallas_call | solution.py:187
  37.8 0.9 %shard_map.43 = (f32[256,128]{1,0:T(8,128)S(1)}, f32[256,128]{1,0:T(8,128)S(1)}) custom-call(s32[2,4]{1,0:T(2,128)S(1)} %bitcast.15, f32[256,128]{1,0:T(8,128)S(1)} %collective-permute-done.9.refs_0_, f32[256,128]{1,0:T(8,128)S(1)} %get-tuple-element.38.refs_1_, bf16[10,128,256]{2,1,0:T(8,128)(2,1)S(1)} %shard_map.42.refs_2_.refs_1_), custom_call_target="tpu_custom_call" | custom-call | flops 100663296 | bytes 2000000 | tf_op jit(solution)/shard_map/pallas_call | solution.py:248
  38.7 1.5 %collective-permute-start.14 = (f32[256,128]{1,0:T(8,128)S(1)}, f32[256,128]{1,0:T(8,128)S(1)}, u32[]{:S(2)}, u32[]{:S(2)}) collective-permute-start(f32[256,128]{1,0:T(8,128)S(1)} %get-tuple-element.47), channel_id=1, source_target_pairs={{0,24},{8,0},{16,8},{24,16},{1,25},{9,1},{17,9},{25,17},{2,26},{10... | collective-permute-start | bytes 393224 | tf_op jit(solution)/shard_map/ppermute | solution.py:20
  40.2 0.9 %shard_map.44.refs_2_.refs_0_ = bf16[10,128,256]{2,1,0:T(8,128)(2,1)S(1)} custom-call(s32[2,4]{1,0:T(2,128)S(1)} %bitcast.16, bf16[10,128,256]{2,1,0:T(8,128)(2,1)S(1)} %shard_map.42.refs_2_.refs_1_, f32[4,19,8,128]{3,2,1,0:T(8,128)S(1)} %pad_maximum_fusion.refs_2_.refs_1_, f32[4,19,8,128]{3,2,1,0:T(8,128)S(1)} %collective-permute-done.15.refs_3_.refs_2_), custom_call_target="tpu_custom_call" | custom-call | flops 188743680 | bytes 1000000 | tf_op jit(solution)/shard_map/pallas_call | solution.py:187
  41.1 3.2 %collective-permute-done.14.refs_1_ = f32[256,128]{1,0:T(8,128)S(1)} collective-permute-done((f32[256,128]{1,0:T(8,128)S(1)}, f32[256,128]{1,0:T(8,128)S(1)}, u32[]{:S(2)}, u32[]{:S(2)}) %collective-permute-start.14) | collective-permute-done | bytes 131104 | tf_op jit(solution)/shard_map/ppermute | solution.py:20
  44.3 0.9 %shard_map.45 = (f32[256,128]{1,0:T(8,128)S(1)}, f32[256,128]{1,0:T(8,128)S(1)}) custom-call(s32[2,4]{1,0:T(2,128)S(1)} %bitcast.17, f32[256,128]{1,0:T(8,128)S(1)} %get-tuple-element.46.refs_0_, f32[256,128]{1,0:T(8,128)S(1)} %collective-permute-done.14.refs_1_, bf16[10,128,256]{2,1,0:T(8,128)(2,1)S(1)} %shard_map.44.refs_2_.refs_0_), custom_call_target="tpu_custom_call" | custom-call | flops 100663296 | bytes 2000000 | tf_op jit(solution)/shard_map/pallas_call | solution.py:248
  45.2 2.5 %collective-permute-start.16 = (f32[256,128]{1,0:T(8,128)S(1)}, f32[256,128]{1,0:T(8,128)S(1)}, u32[]{:S(2)}, u32[]{:S(2)}) collective-permute-start(f32[256,128]{1,0:T(8,128)S(1)} %get-tuple-element.49), channel_id=1, source_target_pairs={{0,8},{8,16},{16,24},{24,0},{1,9},{9,17},{17,25},{25,1},{2,10},{10... | collective-permute-start | bytes 393224 | tf_op jit(solution)/shard_map/ppermute | solution.py:20
  47.7 0.4 shard_map.46.refs_2_
  48.1 3.0 %collective-permute-done.16.refs_0_ = f32[256,128]{1,0:T(8,128)S(1)} collective-permute-done((f32[256,128]{1,0:T(8,128)S(1)}, f32[256,128]{1,0:T(8,128)S(1)}, u32[]{:S(2)}, u32[]{:S(2)}) %collective-permute-start.16) | collective-permute-done | bytes 131104 | tf_op jit(solution)/shard_map/ppermute | solution.py:20
  51.1 1.2 %shard_map.47 = f32[512,128]{1,0:T(8,128)} custom-call(s32[2,4]{1,0:T(2,128)S(1)} %bitcast.18, f32[256,128]{1,0:T(8,128)S(1)} %collective-permute-done.16.refs_0_, f32[256,128]{1,0:T(8,128)S(1)} %get-tuple-element.50.refs_1_, bf16[4,128,256]{2,1,0:T(8,128)(2,1)S(1)} %shard_map.46.refs_2_), custom_call_target="tpu_custom_call" | custom-call | flops 100663296 | bytes 2000000 | tf_op jit(solution)/shard_map/pallas_call | solution.py:248
  (36 shorter events, 1.0 us)
Async XLA Ops:
  0.0 0.9 %copy-start.1 = (f32[4,2,4,8,192]{4,3,2,1,0:T(8,128)S(1)}, f32[4,2,4,8,192]{4,3,2,1,0:T(8,128)}, u32[]{:S(2)}) copy-start(f32[4,2,4,8,192]{4,3,2,1,0:T(8,128)} %refl_ref.1) | copy-start | bytes 589828
  1.0 8.3 %collective-permute-start.5 = (f32[10,8,128]{2,1,0:T(8,128)S(1)}, f32[10,8,128]{2,1,0:T(8,128)S(1)}, u32[]{:S(2)}, u32[]{:S(2)}) collective-permute-start(f32[10,8,128]{2,1,0:T(8,128)S(1)} %get-tuple-element.32), channel_id=1, source_target_pairs={{0,24},{8,0},{16,8},{24,16},{1,25},{9,1},{17,9},{25,17},{2,26},{10... | collective-permute-start | bytes 122888 | tf_op jit(solution)/shard_map/ppermute | solution.py:20
  5.0 6.1 %collective-permute-start.2 = (f32[9,8,128]{2,1,0:T(8,128)S(1)}, f32[9,8,128]{2,1,0:T(8,128)S(1)}, u32[]{:S(2)}, u32[]{:S(2)}) collective-permute-start(f32[9,8,128]{2,1,0:T(8,128)S(1)} %get-tuple-element.28), channel_id=1, source_target_pairs={{0,6},{1,7},{2,4},{3,5},{4,2},{5,3},{6,0},{7,1},{8,14},{9,15},{10,... | collective-permute-start | bytes 110600 | tf_op jit(solution)/shard_map/ppermute | solution.py:25
  8.6 5.0 %collective-permute-start.1 = (f32[9,8,128]{2,1,0:T(8,128)S(1)}, f32[9,8,128]{2,1,0:T(8,128)S(1)}, u32[]{:S(2)}, u32[]{:S(2)}) collective-permute-start(f32[9,8,128]{2,1,0:T(8,128)S(1)} %get-tuple-element.28), channel_id=1, source_target_pairs={{0,4},{1,5},{2,6},{3,7},{4,0},{5,1},{6,2},{7,3},{8,12},{9,13},{10,... | collective-permute-start | bytes 110600 | tf_op jit(solution)/shard_map/ppermute | solution.py:25
  8.6 5.0 %collective-permute-start = (f32[9,8,128]{2,1,0:T(8,128)S(1)}, f32[9,8,128]{2,1,0:T(8,128)S(1)}, u32[]{:S(2)}, u32[]{:S(2)}) collective-permute-start(f32[9,8,128]{2,1,0:T(8,128)S(1)} %get-tuple-element.28), channel_id=1, source_target_pairs={{0,2},{1,3},{2,0},{3,1},{4,6},{5,7},{6,4},{7,5},{8,10},{9,11},{10,... | collective-permute-start | bytes 110600 | tf_op jit(solution)/shard_map/ppermute | solution.py:25
  9.4 4.6 %collective-permute-start.6 = (f32[14,8,128]{2,1,0:T(8,128)S(1)}, f32[14,8,128]{2,1,0:T(8,128)S(1)}, u32[]{:S(2)}, u32[]{:S(2)}) collective-permute-start(f32[14,8,128]{2,1,0:T(8,128)S(1)} %pad_maximum_fusion.5), channel_id=1, source_target_pairs={{0,2},{1,3},{2,0},{3,1},{4,6},{5,7},{6,4},{7,5},{8,10},{9,11},{10,... | collective-permute-start | bytes 172040 | tf_op jit(solution)/shard_map/ppermute | solution.py:25
  13.6 2.6 %collective-permute-start.3 = (f32[4,9,8,128]{3,2,1,0:T(8,128)S(1)}, f32[4,9,8,128]{3,2,1,0:T(8,128)S(1)}, u32[]{:S(2)}, u32[]{:S(2)}) collective-permute-start(f32[4,9,8,128]{3,2,1,0:T(8,128)S(1)} %pad_maximum_fusion.2.refs_0_), channel_id=1, source_target_pairs={{0,1},{1,0},{2,3},{3,2},{4,5},{5,4},{6,7},{7,6},{8,9},{9,8},{10,11... | collective-permute-start | bytes 442376 | tf_op jit(solution)/shard_map/ppermute | solution.py:25
  14.0 2.8 %copy-start = (f32[512,128]{1,0:T(8,128)S(1)}, f32[512,128]{1,0:T(8,128)}, u32[]{:S(2)}) copy-start(f32[512,128]{1,0:T(8,128)} %refs_0_.1) | copy-start | bytes 786436
  14.1 8.4 %collective-permute-start.7 = (f32[2,14,8,128]{3,2,1,0:T(8,128)S(1)}, f32[2,14,8,128]{3,2,1,0:T(8,128)S(1)}, u32[]{:S(2)}, u32[]{:S(2)}) collective-permute-start(f32[2,14,8,128]{3,2,1,0:T(8,128)S(1)} %pad_maximum_fusion.4), channel_id=1, source_target_pairs={{0,4},{1,5},{2,6},{3,7},{4,0},{5,1},{6,2},{7,3},{8,12},{9,13},{10,... | collective-permute-start | bytes 344072 | tf_op jit(solution)/shard_map/ppermute | solution.py:25
  16.8 0.7 %copy-start.2 = (s32[4,2]{0,1:T(2,128)S(1)}, s32[4,2]{0,1:T(2,128)}, u32[]{:S(2)}) copy-start(s32[4,2]{0,1:T(2,128)} %param.4) | copy-start | bytes 100
  22.5 5.1 %collective-permute-start.8 = (f32[4,14,8,128]{3,2,1,0:T(8,128)S(1)}, f32[4,14,8,128]{3,2,1,0:T(8,128)S(1)}, u32[]{:S(2)}, u32[]{:S(2)}) collective-permute-start(f32[4,14,8,128]{3,2,1,0:T(8,128)S(1)} %constant_dynamic-update-slice_fusion.refs_2_), channel_id=1, source_target_pairs={{0,1},{1,0},{2,3},{3,2},{4,5},{5,4},{6,7},{7,6},{8,9},{9,8},{10,11... | collective-permute-start | bytes 688136 | tf_op jit(solution)/shard_map/ppermute | solution.py:25
  22.6 5.9 %collective-permute-start.4 = (f32[256,128]{1,0:T(8,128)S(1)}, f32[256,128]{1,0:T(8,128)S(1)}, u32[]{:S(2)}, u32[]{:S(2)}) collective-permute-start(f32[256,128]{1,0:T(8,128)S(1)} %get-tuple-element.30), channel_id=1, source_target_pairs={{0,24},{8,0},{16,8},{24,16},{1,25},{9,1},{17,9},{25,17},{2,26},{10... | collective-permute-start | bytes 393224 | tf_op jit(solution)/shard_map/ppermute | solution.py:20
  23.2 9.4 %collective-permute-start.11 = (f32[33,8,128]{2,1,0:T(8,128)S(1)}, f32[33,8,128]{2,1,0:T(8,128)S(1)}, u32[]{:S(2)}, u32[]{:S(2)}) collective-permute-start(f32[33,8,128]{2,1,0:T(8,128)S(1)} %get-tuple-element.51), channel_id=1, source_target_pairs={{0,4},{1,5},{2,6},{3,7},{4,0},{5,1},{6,2},{7,3},{8,12},{9,13},{10,... | collective-permute-start | bytes 405512 | tf_op jit(solution)/shard_map/ppermute | solution.py:25
  23.3 11.9 %collective-permute-start.10 = (f32[33,8,128]{2,1,0:T(8,128)S(1)}, f32[33,8,128]{2,1,0:T(8,128)S(1)}, u32[]{:S(2)}, u32[]{:S(2)}) collective-permute-start(f32[33,8,128]{2,1,0:T(8,128)S(1)} %get-tuple-element.51), channel_id=1, source_target_pairs={{0,2},{1,3},{2,0},{3,1},{4,6},{5,7},{6,4},{7,5},{8,10},{9,11},{10,... | collective-permute-start | bytes 405512 | tf_op jit(solution)/shard_map/ppermute | solution.py:25
  25.8 9.4 %collective-permute-start.12 = (f32[33,8,128]{2,1,0:T(8,128)S(1)}, f32[33,8,128]{2,1,0:T(8,128)S(1)}, u32[]{:S(2)}, u32[]{:S(2)}) collective-permute-start(f32[33,8,128]{2,1,0:T(8,128)S(1)} %get-tuple-element.51), channel_id=1, source_target_pairs={{0,6},{1,7},{2,4},{3,5},{4,2},{5,3},{6,0},{7,1},{8,14},{9,15},{10,... | collective-permute-start | bytes 405512 | tf_op jit(solution)/shard_map/ppermute | solution.py:25
  29.4 6.0 %collective-permute-start.9 = (f32[256,128]{1,0:T(8,128)S(1)}, f32[256,128]{1,0:T(8,128)S(1)}, u32[]{:S(2)}, u32[]{:S(2)}) collective-permute-start(f32[256,128]{1,0:T(8,128)S(1)} %get-tuple-element.37), channel_id=1, source_target_pairs={{0,8},{8,16},{16,24},{24,0},{1,9},{9,17},{17,25},{25,1},{2,10},{10... | collective-permute-start | bytes 393224 | tf_op jit(solution)/shard_map/ppermute | solution.py:20
  35.4 1.5 %collective-permute-start.13 = (f32[4,14,8,128]{3,2,1,0:T(8,128)S(1)}, f32[4,14,8,128]{3,2,1,0:T(8,128)S(1)}, u32[]{:S(2)}, u32[]{:S(2)}) collective-permute-start(f32[4,14,8,128]{3,2,1,0:T(8,128)S(1)} %pad_maximum_fusion.1.refs_1_), channel_id=1, source_target_pairs={{0,1},{1,0},{2,3},{3,2},{4,5},{5,4},{6,7},{7,6},{8,9},{9,8},{10,11... | collective-permute-start | bytes 688136 | tf_op jit(solution)/shard_map/ppermute | solution.py:25
  35.5 4.7 %collective-permute-start.15 = (f32[4,19,8,128]{3,2,1,0:T(8,128)S(1)}, f32[4,19,8,128]{3,2,1,0:T(8,128)S(1)}, u32[]{:S(2)}, u32[]{:S(2)}) collective-permute-start(f32[4,19,8,128]{3,2,1,0:T(8,128)S(1)} %pad_maximum_fusion.refs_2_.refs_1_), channel_id=1, source_target_pairs={{0,1},{1,0},{2,3},{3,2},{4,5},{5,4},{6,7},{7,6},{8,9},{9,8},{10,11... | collective-permute-start | bytes 933896 | tf_op jit(solution)/shard_map/ppermute | solution.py:25
  38.7 5.6 %collective-permute-start.14 = (f32[256,128]{1,0:T(8,128)S(1)}, f32[256,128]{1,0:T(8,128)S(1)}, u32[]{:S(2)}, u32[]{:S(2)}) collective-permute-start(f32[256,128]{1,0:T(8,128)S(1)} %get-tuple-element.47), channel_id=1, source_target_pairs={{0,24},{8,0},{16,8},{24,16},{1,25},{9,1},{17,9},{25,17},{2,26},{10... | collective-permute-start | bytes 393224 | tf_op jit(solution)/shard_map/ppermute | solution.py:20
  45.2 5.9 %collective-permute-start.16 = (f32[256,128]{1,0:T(8,128)S(1)}, f32[256,128]{1,0:T(8,128)S(1)}, u32[]{:S(2)}, u32[]{:S(2)}) collective-permute-start(f32[256,128]{1,0:T(8,128)S(1)} %get-tuple-element.49), channel_id=1, source_target_pairs={{0,8},{8,16},{16,24},{24,0},{1,9},{9,17},{17,25},{25,1},{2,10},{10... | collective-permute-start | bytes 393224 | tf_op jit(solution)/shard_map/ppermute | solution.py:20

commit v2 on v1

--- a/solution.py
+++ b/solution.py
@@ -332,7 +332,7 @@
     for ph in range(rounds):
         if ph < groups:
             ready = results[min(ph, 2) - 1] if ph else None
-            tiles = gather.receive(ph, movements[1] if ph > 1 else None, ready)
+            tiles = gather.receive(ph, movements[min(ph, 2) - 1] if ph else None, ready)
         mats = matrices(plan, ph, offsets, mats, tiles)
         away = ph % 2 == 1
         sizes = (rest, HALF) if away else (HALF, rest)

time: 52.7 us -> 54.4 us (1.032)
  waiting for transfers between devices: 19.1 us -> 23 us
  starting transfers between devices: 23 us -> 21.1 us
    ppermute x12, waiting for transfers between devices: 12.9 us -> 15.1 us  [swapped(): return lax.ppermute(value, 'col', [(i, i ^ bit) for i in range(devices)])]
    ppermute x5, starting transfers between devices: 9.99 us -> 8.09 us  [shifted(): lax.ppermute(value, axis, [(i, (i + by) % devices) for i in range(devices)])]
    ppermute x5, waiting for transfers between devices: 6.25 us -> 7.89 us  [shifted(): lax.ppermute(value, axis, [(i, (i + by) % devices) for i in range(devices)])]
    unnamed x7 -> x6, local copies, waits for them, and re-layouts: 1.63 us -> 1.62 us
  transfers between devices with their start and end apart: 17 -> 17, of which waited for: 9 -> 10; matrix products, arithmetic and copies ran while one was open for 0% -> 0% of each run, Pallas kernels for 11% -> 11%
where the time goes in v2:
time: 54.4 us; the launch traced here: 54.2 us
  waiting for transfers between devices  23 us (42%)
  starting transfers between devices  21.1 us (39%)
  Pallas kernels  8.21 us (15%)
  local copies, waits for them, and re-layouts  1.67 us (3%)
    ppermute x12, waiting for transfers between devices, swapped(): return lax.ppermute(value, 'col', [(i, i ^ bit) for i in range(devices)])  15.1 us
    ppermute x12, starting transfers between devices, swapped(): return lax.ppermute(value, 'col', [(i, i ^ bit) for i in range(devices)])  13 us
    ppermute x5, starting transfers between devices, shifted(): lax.ppermute(value, axis, [(i, (i + by) % devices) for i in range(devices)])  8.09 us
    ppermute x5, waiting for transfers between devices, shifted(): lax.ppermute(value, axis, [(i, (i + by) % devices) for i in range(devices)])  7.89 us
    pallas_call x5, Pallas kernels, phase(): pl.pallas_call(functools.partial(phase_kernel, ph, rounds, nwin, len(part...  4.47 us
    pallas_call x5, Pallas kernels, matrices(): pl.pallas_call(functools.partial(matrix_kernel, plan, ph, masked), out_sh...  3.66 us
    unnamed x6, local copies, waits for them, and re-layouts  1.62 us
  transfers between devices with their start and end apart: 17, of which 10 were waited for; matrix products, arithmetic and copies ran while one was open for 0% of the time, Pallas kernels for 11%

profile of v2, /device:TPU:0, one launch (start us, length us, event | category | flops | bytes accessed | tf_op | source)
XLA Modules:
  0.0 54.2 jit_solution(13279163702536810806)
XLA Ops:
  0.0 0.9 %copy-done.1 = f32[4,2,4,8,192]{4,3,2,1,0:T(8,128)S(1)} copy-done((f32[4,2,4,8,192]{4,3,2,1,0:T(8,128)S(1)}, f32[4,2,4,8,192]{4,3,2,1,0:T(8,128)}, u32[]{:S(2)}) %copy-start.1) | copy-done | bytes 196632
  1.0 3.9 %collective-permute-start.5 = (f32[10,8,128]{2,1,0:T(8,128)S(1)}, f32[10,8,128]{2,1,0:T(8,128)S(1)}, u32[]{:S(2)}, u32[]{:S(2)}) collective-permute-start(f32[10,8,128]{2,1,0:T(8,128)S(1)} %get-tuple-element.33), channel_id=1, source_target_pairs={{0,24},{8,0},{16,8},{24,16},{1,25},{9,1},{17,9},{25,17},{2,26},{10... | collective-permute-start | bytes 122888 | tf_op jit(solution)/shard_map/ppermute | solution.py:20
  5.0 3.6 %collective-permute-start.2 = (f32[9,8,128]{2,1,0:T(8,128)S(1)}, f32[9,8,128]{2,1,0:T(8,128)S(1)}, u32[]{:S(2)}, u32[]{:S(2)}) collective-permute-start(f32[9,8,128]{2,1,0:T(8,128)S(1)} %get-tuple-element.29), channel_id=1, source_target_pairs={{0,6},{1,7},{2,4},{3,5},{4,2},{5,3},{6,0},{7,1},{8,14},{9,15},{10,... | collective-permute-start | bytes 110600 | tf_op jit(solution)/shard_map/ppermute | solution.py:25
  8.6 0.8 %collective-permute-start = (f32[9,8,128]{2,1,0:T(8,128)S(1)}, f32[9,8,128]{2,1,0:T(8,128)S(1)}, u32[]{:S(2)}, u32[]{:S(2)}) collective-permute-start(f32[9,8,128]{2,1,0:T(8,128)S(1)} %get-tuple-element.29), channel_id=1, source_target_pairs={{0,2},{1,3},{2,0},{3,1},{4,6},{5,7},{6,4},{7,5},{8,10},{9,11},{10,... | collective-permute-start | bytes 110600 | tf_op jit(solution)/shard_map/ppermute | solution.py:25
  9.4 1.3 %collective-permute-start.6 = (f32[14,8,128]{2,1,0:T(8,128)S(1)}, f32[14,8,128]{2,1,0:T(8,128)S(1)}, u32[]{:S(2)}, u32[]{:S(2)}) collective-permute-start(f32[14,8,128]{2,1,0:T(8,128)S(1)} %pad_maximum_fusion.6), channel_id=1, source_target_pairs={{0,2},{1,3},{2,0},{3,1},{4,6},{5,7},{6,4},{7,5},{8,10},{9,11},{10,... | collective-permute-start | bytes 172040 | tf_op jit(solution)/shard_map/ppermute | solution.py:25
  11.1 2.4 %collective-permute-done.1 = f32[9,8,128]{2,1,0:T(8,128)S(1)} collective-permute-done((f32[9,8,128]{2,1,0:T(8,128)S(1)}, f32[9,8,128]{2,1,0:T(8,128)S(1)}, u32[]{:S(2)}, u32[]{:S(2)}) %collective-permute-start.1) | collective-permute-done | bytes 36896 | tf_op jit(solution)/shard_map/ppermute | solution.py:25
  14.1 2.1 %collective-permute-start.7 = (f32[2,14,8,128]{3,2,1,0:T(8,128)S(1)}, f32[2,14,8,128]{3,2,1,0:T(8,128)S(1)}, u32[]{:S(2)}, u32[]{:S(2)}) collective-permute-start(f32[2,14,8,128]{3,2,1,0:T(8,128)S(1)} %pad_maximum_fusion.5), channel_id=1, source_target_pairs={{0,4},{1,5},{2,6},{3,7},{4,0},{5,1},{6,2},{7,3},{8,12},{9,13},{10,... | collective-permute-start | bytes 344072 | tf_op jit(solution)/shard_map/ppermute | solution.py:25
  16.2 0.6 %shard_map.38.refs_1_ = bf16[6,128,256]{2,1,0:T(8,128)(2,1)S(1)} custom-call(f32[4,9,8,128]{3,2,1,0:T(8,128)S(1)} %pad_maximum_fusion.3.refs_0_, f32[4,9,8,128]{3,2,1,0:T(8,128)S(1)} %collective-permute-done.3.refs_1_), custom_call_target="tpu_custom_call" | custom-call | flops 113246208 | bytes 600000 | tf_op jit(solution)/shard_map/pallas_call | solution.py:187
  16.8 0.7 %copy-done.2 = s32[4,2]{0,1:T(2,128)S(1)} copy-done((s32[4,2]{0,1:T(2,128)S(1)}, s32[4,2]{0,1:T(2,128)}, u32[]{:S(2)}) %copy-start.2) | copy-done | bytes 56
  17.5 0.5 shard_map.39
  18.0 0.7 %collective-permute-start.4 = (f32[256,128]{1,0:T(8,128)S(1)}, f32[256,128]{1,0:T(8,128)S(1)}, u32[]{:S(2)}, u32[]{:S(2)}) collective-permute-start(f32[256,128]{1,0:T(8,128)S(1)} %get-tuple-element.31), channel_id=1, source_target_pairs={{0,24},{8,0},{16,8},{24,16},{1,25},{9,1},{17,9},{25,17},{2,26},{10... | collective-permute-start | bytes 393224 | tf_op jit(solution)/shard_map/ppermute | solution.py:20
  18.7 3.8 %collective-permute-done.7 = f32[2,14,8,128]{3,2,1,0:T(8,128)S(1)} collective-permute-done((f32[2,14,8,128]{3,2,1,0:T(8,128)S(1)}, f32[2,14,8,128]{3,2,1,0:T(8,128)S(1)}, u32[]{:S(2)}, u32[]{:S(2)}) %collective-permute-start.7) | collective-permute-done | bytes 114720 | tf_op jit(solution)/shard_map/ppermute | solution.py:25
  22.5 0.6 %collective-permute-done.4.refs_1_ = f32[256,128]{1,0:T(8,128)S(1)} collective-permute-done((f32[256,128]{1,0:T(8,128)S(1)}, f32[256,128]{1,0:T(8,128)S(1)}, u32[]{:S(2)}, u32[]{:S(2)}) %collective-permute-start.4) | collective-permute-done | bytes 131104 | tf_op jit(solution)/shard_map/ppermute | solution.py:20
  23.2 1.3 %collective-permute-start.11 = (f32[33,8,128]{2,1,0:T(8,128)S(1)}, f32[33,8,128]{2,1,0:T(8,128)S(1)}, u32[]{:S(2)}, u32[]{:S(2)}) collective-permute-start(f32[33,8,128]{2,1,0:T(8,128)S(1)} %get-tuple-element.53), channel_id=1, source_target_pairs={{0,4},{1,5},{2,6},{3,7},{4,0},{5,1},{6,2},{7,3},{8,12},{9,13},{10,... | collective-permute-start | bytes 405512 | tf_op jit(solution)/shard_map/ppermute | solution.py:25
  24.4 0.8 %collective-permute-start.10 = (f32[33,8,128]{2,1,0:T(8,128)S(1)}, f32[33,8,128]{2,1,0:T(8,128)S(1)}, u32[]{:S(2)}, u32[]{:S(2)}) collective-permute-start(f32[33,8,128]{2,1,0:T(8,128)S(1)} %get-tuple-element.53), channel_id=1, source_target_pairs={{0,2},{1,3},{2,0},{3,1},{4,6},{5,7},{6,4},{7,5},{8,10},{9,11},{10,... | collective-permute-start | bytes 405512 | tf_op jit(solution)/shard_map/ppermute | solution.py:25
  25.2 2.4 %collective-permute-start.12 = (f32[33,8,128]{2,1,0:T(8,128)S(1)}, f32[33,8,128]{2,1,0:T(8,128)S(1)}, u32[]{:S(2)}, u32[]{:S(2)}) collective-permute-start(f32[33,8,128]{2,1,0:T(8,128)S(1)} %get-tuple-element.53), channel_id=1, source_target_pairs={{0,6},{1,7},{2,4},{3,5},{4,2},{5,3},{6,0},{7,1},{8,14},{9,15},{10,... | collective-permute-start | bytes 405512 | tf_op jit(solution)/shard_map/ppermute | solution.py:25
  27.6 0.9 %shard_map.40.refs_2_.refs_0_ = bf16[10,128,256]{2,1,0:T(8,128)(2,1)S(1)} custom-call(s32[2,4]{1,0:T(2,128)S(1)} %bitcast.13, bf16[6,128,256]{2,1,0:T(8,128)(2,1)S(1)} %shard_map.38.refs_1_, f32[4,14,8,128]{3,2,1,0:T(8,128)S(1)} %pad_maximum_fusion.1.refs_2_, f32[4,14,8,128]{3,2,1,0:T(8,128)S(1)} %collective-permute-done.8.refs_3_), custom_call_target="tpu_custom_call" | custom-call | flops 188743680 | bytes 1000000 | tf_op jit(solution)/shard_map/pallas_call | solution.py:187
  28.5 0.9 %shard_map.41 = (f32[256,128]{1,0:T(8,128)S(1)}, f32[256,128]{1,0:T(8,128)S(1)}) custom-call(s32[2,4]{1,0:T(2,128)S(1)} %bitcast.14, f32[256,128]{1,0:T(8,128)S(1)} %get-tuple-element.30.refs_0_, f32[256,128]{1,0:T(8,128)S(1)} %collective-permute-done.4.refs_1_, bf16[10,128,256]{2,1,0:T(8,128)(2,1)S(1)} %shard_map.40.refs_2_.refs_0_), custom_call_target="tpu_custom_call" | custom-call | flops 100663296 | bytes 2000000 | tf_op jit(solution)/shard_map/pallas_call | solution.py:248
  29.4 0.5 collective-permute-start.9
  29.9 3.5 %collective-permute-done.11 = f32[33,8,128]{2,1,0:T(8,128)S(1)} collective-permute-done((f32[33,8,128]{2,1,0:T(8,128)S(1)}, f32[33,8,128]{2,1,0:T(8,128)S(1)}, u32[]{:S(2)}, u32[]{:S(2)}) %collective-permute-start.11) | collective-permute-done | bytes 135200 | tf_op jit(solution)/shard_map/ppermute | solution.py:25
  33.4 3.7 %collective-permute-done.12 = f32[33,8,128]{2,1,0:T(8,128)S(1)} collective-permute-done((f32[33,8,128]{2,1,0:T(8,128)S(1)}, f32[33,8,128]{2,1,0:T(8,128)S(1)}, u32[]{:S(2)}, u32[]{:S(2)}) %collective-permute-start.12) | collective-permute-done | bytes 135200 | tf_op jit(solution)/shard_map/ppermute | solution.py:25
  37.3 0.6 %collective-permute-start.15 = (f32[4,19,8,128]{3,2,1,0:T(8,128)S(1)}, f32[4,19,8,128]{3,2,1,0:T(8,128)S(1)}, u32[]{:S(2)}, u32[]{:S(2)}) collective-permute-start(f32[4,19,8,128]{3,2,1,0:T(8,128)S(1)} %pad_maximum_fusion.refs_2_.refs_1_), channel_id=1, source_target_pairs={{0,1},{1,0},{2,3},{3,2},{4,5},{5,4},{6,7},{7,6},{8,9},{9,8},{10,11... | collective-permute-start | bytes 933896 | tf_op jit(solution)/shard_map/ppermute | solution.py:25
  37.9 0.9 %collective-permute-done.13.refs_2_ = f32[4,14,8,128]{3,2,1,0:T(8,128)S(1)} collective-permute-done((f32[4,14,8,128]{3,2,1,0:T(8,128)S(1)}, f32[4,14,8,128]{3,2,1,0:T(8,128)S(1)}, u32[]{:S(2)}, u32[]{:S(2)}) %collective-permute-start.13) | collective-permute-done | bytes 229408 | tf_op jit(solution)/shard_map/ppermute | solution.py:25
  38.8 0.8 %shard_map.42.refs_2_.refs_1_ = bf16[10,128,256]{2,1,0:T(8,128)(2,1)S(1)} custom-call(bf16[10,128,256]{2,1,0:T(8,128)(2,1)S(1)} %shard_map.40.refs_2_.refs_0_, f32[4,14,8,128]{3,2,1,0:T(8,128)S(1)} %pad_maximum_fusion.2.refs_1_, f32[4,14,8,128]{3,2,1,0:T(8,128)S(1)} %collective-permute-done.13.refs_2_), custom_call_target="tpu_custom_call" | custom-call | flops 188743680 | bytes 1000000 | tf_op jit(solution)/shard_map/pallas_call | solution.py:187
  39.6 0.9 %shard_map.43 = (f32[256,128]{1,0:T(8,128)S(1)}, f32[256,128]{1,0:T(8,128)S(1)}) custom-call(s32[2,4]{1,0:T(2,128)S(1)} %bitcast.15, f32[256,128]{1,0:T(8,128)S(1)} %collective-permute-done.9.refs_0_, f32[256,128]{1,0:T(8,128)S(1)} %get-tuple-element.40.refs_1_, bf16[10,128,256]{2,1,0:T(8,128)(2,1)S(1)} %shard_map.42.refs_2_.refs_1_), custom_call_target="tpu_custom_call" | custom-call | flops 100663296 | bytes 2000000 | tf_op jit(solution)/shard_map/pallas_call | solution.py:248
  40.6 1.5 %collective-permute-start.14 = (f32[256,128]{1,0:T(8,128)S(1)}, f32[256,128]{1,0:T(8,128)S(1)}, u32[]{:S(2)}, u32[]{:S(2)}) collective-permute-start(f32[256,128]{1,0:T(8,128)S(1)} %get-tuple-element.49), channel_id=1, source_target_pairs={{0,24},{8,0},{16,8},{24,16},{1,25},{9,1},{17,9},{25,17},{2,26},{10... | collective-permute-start | bytes 393224 | tf_op jit(solution)/shard_map/ppermute | solution.py:20
  42.0 0.9 %shard_map.44.refs_2_.refs_0_ = bf16[10,128,256]{2,1,0:T(8,128)(2,1)S(1)} custom-call(s32[2,4]{1,0:T(2,128)S(1)} %bitcast.16, bf16[10,128,256]{2,1,0:T(8,128)(2,1)S(1)} %shard_map.42.refs_2_.refs_1_, f32[4,19,8,128]{3,2,1,0:T(8,128)S(1)} %pad_maximum_fusion.refs_2_.refs_1_, f32[4,19,8,128]{3,2,1,0:T(8,128)S(1)} %collective-permute-done.15.refs_3_.refs_2_), custom_call_target="tpu_custom_call" | custom-call | flops 188743680 | bytes 1000000 | tf_op jit(solution)/shard_map/pallas_call | solution.py:187
  43.0 3.2 %collective-permute-done.14.refs_1_ = f32[256,128]{1,0:T(8,128)S(1)} collective-permute-done((f32[256,128]{1,0:T(8,128)S(1)}, f32[256,128]{1,0:T(8,128)S(1)}, u32[]{:S(2)}, u32[]{:S(2)}) %collective-permute-start.14) | collective-permute-done | bytes 131104 | tf_op jit(solution)/shard_map/ppermute | solution.py:20
  46.2 0.9 %shard_map.45 = (f32[256,128]{1,0:T(8,128)S(1)}, f32[256,128]{1,0:T(8,128)S(1)}) custom-call(s32[2,4]{1,0:T(2,128)S(1)} %bitcast.17, f32[256,128]{1,0:T(8,128)S(1)} %get-tuple-element.48.refs_0_, f32[256,128]{1,0:T(8,128)S(1)} %collective-permute-done.14.refs_1_, bf16[10,128,256]{2,1,0:T(8,128)(2,1)S(1)} %shard_map.44.refs_2_.refs_0_), custom_call_target="tpu_custom_call" | custom-call | flops 100663296 | bytes 2000000 | tf_op jit(solution)/shard_map/pallas_call | solution.py:248
  47.1 1.4 %collective-permute-start.16 = (f32[256,128]{1,0:T(8,128)S(1)}, f32[256,128]{1,0:T(8,128)S(1)}, u32[]{:S(2)}, u32[]{:S(2)}) collective-permute-start(f32[256,128]{1,0:T(8,128)S(1)} %get-tuple-element.51), channel_id=1, source_target_pairs={{0,8},{8,16},{16,24},{24,0},{1,9},{9,17},{17,25},{25,1},{2,10},{10... | collective-permute-start | bytes 393224 | tf_op jit(solution)/shard_map/ppermute | solution.py:20
  49.0 4.1 %collective-permute-done.16.refs_0_ = f32[256,128]{1,0:T(8,128)S(1)} collective-permute-done((f32[256,128]{1,0:T(8,128)S(1)}, f32[256,128]{1,0:T(8,128)S(1)}, u32[]{:S(2)}, u32[]{:S(2)}) %collective-permute-start.16) | collective-permute-done | bytes 131104 | tf_op jit(solution)/shard_map/ppermute | solution.py:20
  53.0 1.2 %shard_map.47 = f32[512,128]{1,0:T(8,128)} custom-call(s32[2,4]{1,0:T(2,128)S(1)} %bitcast.18, f32[256,128]{1,0:T(8,128)S(1)} %collective-permute-done.16.refs_0_, f32[256,128]{1,0:T(8,128)S(1)} %get-tuple-element.52.refs_1_, bf16[4,128,256]{2,1,0:T(8,128)(2,1)S(1)} %shard_map.46.refs_2_), custom_call_target="tpu_custom_call" | custom-call | flops 100663296 | bytes 2000000 | tf_op jit(solution)/shard_map/pallas_call | solution.py:248
  (35 shorter events, 1.7 us)
Async XLA Ops:
  0.0 0.9 %copy-start.1 = (f32[4,2,4,8,192]{4,3,2,1,0:T(8,128)S(1)}, f32[4,2,4,8,192]{4,3,2,1,0:T(8,128)}, u32[]{:S(2)}) copy-start(f32[4,2,4,8,192]{4,3,2,1,0:T(8,128)} %refl_ref.1) | copy-start | bytes 589828
  1.0 8.3 %collective-permute-start.5 = (f32[10,8,128]{2,1,0:T(8,128)S(1)}, f32[10,8,128]{2,1,0:T(8,128)S(1)}, u32[]{:S(2)}, u32[]{:S(2)}) collective-permute-start(f32[10,8,128]{2,1,0:T(8,128)S(1)} %get-tuple-element.33), channel_id=1, source_target_pairs={{0,24},{8,0},{16,8},{24,16},{1,25},{9,1},{17,9},{25,17},{2,26},{10... | collective-permute-start | bytes 122888 | tf_op jit(solution)/shard_map/ppermute | solution.py:20
  5.0 6.1 %collective-permute-start.2 = (f32[9,8,128]{2,1,0:T(8,128)S(1)}, f32[9,8,128]{2,1,0:T(8,128)S(1)}, u32[]{:S(2)}, u32[]{:S(2)}) collective-permute-start(f32[9,8,128]{2,1,0:T(8,128)S(1)} %get-tuple-element.29), channel_id=1, source_target_pairs={{0,6},{1,7},{2,4},{3,5},{4,2},{5,3},{6,0},{7,1},{8,14},{9,15},{10,... | collective-permute-start | bytes 110600 | tf_op jit(solution)/shard_map/ppermute | solution.py:25
  8.6 5.0 %collective-permute-start.1 = (f32[9,8,128]{2,1,0:T(8,128)S(1)}, f32[9,8,128]{2,1,0:T(8,128)S(1)}, u32[]{:S(2)}, u32[]{:S(2)}) collective-permute-start(f32[9,8,128]{2,1,0:T(8,128)S(1)} %get-tuple-element.29), channel_id=1, source_target_pairs={{0,4},{1,5},{2,6},{3,7},{4,0},{5,1},{6,2},{7,3},{8,12},{9,13},{10,... | collective-permute-start | bytes 110600 | tf_op jit(solution)/shard_map/ppermute | solution.py:25
  8.6 5.0 %collective-permute-start = (f32[9,8,128]{2,1,0:T(8,128)S(1)}, f32[9,8,128]{2,1,0:T(8,128)S(1)}, u32[]{:S(2)}, u32[]{:S(2)}) collective-permute-start(f32[9,8,128]{2,1,0:T(8,128)S(1)} %get-tuple-element.29), channel_id=1, source_target_pairs={{0,2},{1,3},{2,0},{3,1},{4,6},{5,7},{6,4},{7,5},{8,10},{9,11},{10,... | collective-permute-start | bytes 110600 | tf_op jit(solution)/shard_map/ppermute | solution.py:25
  9.4 4.6 %collective-permute-start.6 = (f32[14,8,128]{2,1,0:T(8,128)S(1)}, f32[14,8,128]{2,1,0:T(8,128)S(1)}, u32[]{:S(2)}, u32[]{:S(2)}) collective-permute-start(f32[14,8,128]{2,1,0:T(8,128)S(1)} %pad_maximum_fusion.6), channel_id=1, source_target_pairs={{0,2},{1,3},{2,0},{3,1},{4,6},{5,7},{6,4},{7,5},{8,10},{9,11},{10,... | collective-permute-start | bytes 172040 | tf_op jit(solution)/shard_map/ppermute | solution.py:25
  13.6 2.6 %collective-permute-start.3 = (f32[4,9,8,128]{3,2,1,0:T(8,128)S(1)}, f32[4,9,8,128]{3,2,1,0:T(8,128)S(1)}, u32[]{:S(2)}, u32[]{:S(2)}) collective-permute-start(f32[4,9,8,128]{3,2,1,0:T(8,128)S(1)} %pad_maximum_fusion.3.refs_0_), channel_id=1, source_target_pairs={{0,1},{1,0},{2,3},{3,2},{4,5},{5,4},{6,7},{7,6},{8,9},{9,8},{10,11... | collective-permute-start | bytes 442376 | tf_op jit(solution)/shard_map/ppermute | solution.py:25
  14.0 2.8 %copy-start = (f32[512,128]{1,0:T(8,128)S(1)}, f32[512,128]{1,0:T(8,128)}, u32[]{:S(2)}) copy-start(f32[512,128]{1,0:T(8,128)} %refs_0_.1) | copy-start | bytes 786436
  14.1 8.4 %collective-permute-start.7 = (f32[2,14,8,128]{3,2,1,0:T(8,128)S(1)}, f32[2,14,8,128]{3,2,1,0:T(8,128)S(1)}, u32[]{:S(2)}, u32[]{:S(2)}) collective-permute-start(f32[2,14,8,128]{3,2,1,0:T(8,128)S(1)} %pad_maximum_fusion.5), channel_id=1, source_target_pairs={{0,4},{1,5},{2,6},{3,7},{4,0},{5,1},{6,2},{7,3},{8,12},{9,13},{10,... | collective-permute-start | bytes 344072 | tf_op jit(solution)/shard_map/ppermute | solution.py:25
  16.8 0.7 %copy-start.2 = (s32[4,2]{0,1:T(2,128)S(1)}, s32[4,2]{0,1:T(2,128)}, u32[]{:S(2)}) copy-start(s32[4,2]{0,1:T(2,128)} %param.4) | copy-start | bytes 100
  18.0 5.1 %collective-permute-start.4 = (f32[256,128]{1,0:T(8,128)S(1)}, f32[256,128]{1,0:T(8,128)S(1)}, u32[]{:S(2)}, u32[]{:S(2)}) collective-permute-start(f32[256,128]{1,0:T(8,128)S(1)} %get-tuple-element.31), channel_id=1, source_target_pairs={{0,24},{8,0},{16,8},{24,16},{1,25},{9,1},{17,9},{25,17},{2,26},{10... | collective-permute-start | bytes 393224 | tf_op jit(solution)/shard_map/ppermute | solution.py:20
  23.1 4.5 %collective-permute-start.8 = (f32[4,14,8,128]{3,2,1,0:T(8,128)S(1)}, f32[4,14,8,128]{3,2,1,0:T(8,128)S(1)}, u32[]{:S(2)}, u32[]{:S(2)}) collective-permute-start(f32[4,14,8,128]{3,2,1,0:T(8,128)S(1)} %pad_maximum_fusion.1.refs_2_), channel_id=1, source_target_pairs={{0,1},{1,0},{2,3},{3,2},{4,5},{5,4},{6,7},{7,6},{8,9},{9,8},{10,11... | collective-permute-start | bytes 688136 | tf_op jit(solution)/shard_map/ppermute | solution.py:25
  23.2 10.2 %collective-permute-start.11 = (f32[33,8,128]{2,1,0:T(8,128)S(1)}, f32[33,8,128]{2,1,0:T(8,128)S(1)}, u32[]{:S(2)}, u32[]{:S(2)}) collective-permute-start(f32[33,8,128]{2,1,0:T(8,128)S(1)} %get-tuple-element.53), channel_id=1, source_target_pairs={{0,4},{1,5},{2,6},{3,7},{4,0},{5,1},{6,2},{7,3},{8,12},{9,13},{10,... | collective-permute-start | bytes 405512 | tf_op jit(solution)/shard_map/ppermute | solution.py:25
  24.4 9.0 %collective-permute-start.10 = (f32[33,8,128]{2,1,0:T(8,128)S(1)}, f32[33,8,128]{2,1,0:T(8,128)S(1)}, u32[]{:S(2)}, u32[]{:S(2)}) collective-permute-start(f32[33,8,128]{2,1,0:T(8,128)S(1)} %get-tuple-element.53), channel_id=1, source_target_pairs={{0,2},{1,3},{2,0},{3,1},{4,6},{5,7},{6,4},{7,5},{8,10},{9,11},{10,... | collective-permute-start | bytes 405512 | tf_op jit(solution)/shard_map/ppermute | solution.py:25
  25.2 11.9 %collective-permute-start.12 = (f32[33,8,128]{2,1,0:T(8,128)S(1)}, f32[33,8,128]{2,1,0:T(8,128)S(1)}, u32[]{:S(2)}, u32[]{:S(2)}) collective-permute-start(f32[33,8,128]{2,1,0:T(8,128)S(1)} %get-tuple-element.53), channel_id=1, source_target_pairs={{0,6},{1,7},{2,4},{3,5},{4,2},{5,3},{6,0},{7,1},{8,14},{9,15},{10,... | collective-permute-start | bytes 405512 | tf_op jit(solution)/shard_map/ppermute | solution.py:25
  29.4 7.8 %collective-permute-start.9 = (f32[256,128]{1,0:T(8,128)S(1)}, f32[256,128]{1,0:T(8,128)S(1)}, u32[]{:S(2)}, u32[]{:S(2)}) collective-permute-start(f32[256,128]{1,0:T(8,128)S(1)} %get-tuple-element.39), channel_id=1, source_target_pairs={{0,8},{8,16},{16,24},{24,0},{1,9},{9,17},{17,25},{25,1},{2,10},{10... | collective-permute-start | bytes 393224 | tf_op jit(solution)/shard_map/ppermute | solution.py:20
  37.2 1.6 %collective-permute-start.13 = (f32[4,14,8,128]{3,2,1,0:T(8,128)S(1)}, f32[4,14,8,128]{3,2,1,0:T(8,128)S(1)}, u32[]{:S(2)}, u32[]{:S(2)}) collective-permute-start(f32[4,14,8,128]{3,2,1,0:T(8,128)S(1)} %pad_maximum_fusion.2.refs_1_), channel_id=1, source_target_pairs={{0,1},{1,0},{2,3},{3,2},{4,5},{5,4},{6,7},{7,6},{8,9},{9,8},{10,11... | collective-permute-start | bytes 688136 | tf_op jit(solution)/shard_map/ppermute | solution.py:25
  37.3 4.7 %collective-permute-start.15 = (f32[4,19,8,128]{3,2,1,0:T(8,128)S(1)}, f32[4,19,8,128]{3,2,1,0:T(8,128)S(1)}, u32[]{:S(2)}, u32[]{:S(2)}) collective-permute-start(f32[4,19,8,128]{3,2,1,0:T(8,128)S(1)} %pad_maximum_fusion.refs_2_.refs_1_), channel_id=1, source_target_pairs={{0,1},{1,0},{2,3},{3,2},{4,5},{5,4},{6,7},{7,6},{8,9},{9,8},{10,11... | collective-permute-start | bytes 933896 | tf_op jit(solution)/shard_map/ppermute | solution.py:25
  40.6 5.6 %collective-permute-start.14 = (f32[256,128]{1,0:T(8,128)S(1)}, f32[256,128]{1,0:T(8,128)S(1)}, u32[]{:S(2)}, u32[]{:S(2)}) collective-permute-start(f32[256,128]{1,0:T(8,128)S(1)} %get-tuple-element.49), channel_id=1, source_target_pairs={{0,24},{8,0},{16,8},{24,16},{1,25},{9,1},{17,9},{25,17},{2,26},{10... | collective-permute-start | bytes 393224 | tf_op jit(solution)/shard_map/ppermute | solution.py:20
  47.1 5.9 %collective-permute-start.16 = (f32[256,128]{1,0:T(8,128)S(1)}, f32[256,128]{1,0:T(8,128)S(1)}, u32[]{:S(2)}, u32[]{:S(2)}) collective-permute-start(f32[256,128]{1,0:T(8,128)S(1)} %get-tuple-element.51), channel_id=1, source_target_pairs={{0,8},{8,16},{16,24},{24,0},{1,9},{9,17},{17,25},{25,1},{2,10},{10... | collective-permute-start | bytes 393224 | tf_op jit(solution)/shard_map/ppermute | solution.py:20

commit v3 on v1

--- a/solution.py
+++ b/solution.py
@@ -281,16 +281,11 @@
                 tiles = jnp.concatenate([tiles, ahead[edge_at : edge_at + edge_tiles]], 0)
             self.own.append(tiles)
         if self.stepwise:
-            self.doubled(1, self.own[1], self.held[0][-1])
+            self.direct(1, self.own[1])
 
     def direct(self, g, tiles):
         others = [swapped(tiles, CORES * m) for m in range(1, self.chips)]
         self.held[g] = [part.reshape((1,) + tiles.shape) for part in [tiles] + others]
-
-    def doubled(self, g, tiles, earlier=None):
-        pair = (tiles, swapped(tiles, CORES))
-        pair = jnp.stack(pair if earlier is None else after(pair, earlier))
-        self.held[g] = [pair, swapped(pair, 2 * CORES)]
 
     def together(self, groups):
         if self.stepwise:

time: 52.7 us -> 54 us (1.025)
  waiting for transfers between devices: 19.1 us -> 20.7 us
    ppermute x5, waiting for transfers between devices: 6.25 us -> 9.38 us  [shifted(): lax.ppermute(value, axis, [(i, (i + by) % devices) for i in range(devices)])]
    ppermute x5, starting transfers between devices: 9.99 us -> 7.54 us  [shifted(): lax.ppermute(value, axis, [(i, (i + by) % devices) for i in range(devices)])]
    ppermute x12 -> x13, starting transfers between devices: 13 us -> 15.4 us  [swapped(): return lax.ppermute(value, 'col', [(i, i ^ bit) for i in range(devices)])]
    ppermute x12 -> x13, waiting for transfers between devices: 12.9 us -> 11.3 us  [swapped(): return lax.ppermute(value, 'col', [(i, i ^ bit) for i in range(devices)])]
    unnamed x7 -> x9, local copies, waits for them, and re-layouts: 1.63 us -> 1.64 us
  transfers between devices with their start and end apart: 17 -> 18, of which waited for: 9 -> 9; matrix products, arithmetic and copies ran while one was open for 0% -> 0% of each run, Pallas kernels for 11% -> 11%
where the time goes in v3:
time: 54 us; the launch traced here: 53.8 us
  starting transfers between devices  22.9 us (42%)
  waiting for transfers between devices  20.7 us (38%)
  Pallas kernels  8.2 us (15%)
  local copies, waits for them, and re-layouts  1.7 us (3%)
    ppermute x13, starting transfers between devices, swapped(): return lax.ppermute(value, 'col', [(i, i ^ bit) for i in range(devices)])  15.4 us
    ppermute x13, waiting for transfers between devices, swapped(): return lax.ppermute(value, 'col', [(i, i ^ bit) for i in range(devices)])  11.3 us
    ppermute x5, waiting for transfers between devices, shifted(): lax.ppermute(value, axis, [(i, (i + by) % devices) for i in range(devices)])  9.38 us
    ppermute x5, starting transfers between devices, shifted(): lax.ppermute(value, axis, [(i, (i + by) % devices) for i in range(devices)])  7.54 us
    pallas_call x5, Pallas kernels, phase(): pl.pallas_call(functools.partial(phase_kernel, ph, rounds, nwin, len(part...  4.46 us
    pallas_call x5, Pallas kernels, matrices(): pl.pallas_call(functools.partial(matrix_kernel, plan, ph, masked), out_sh...  3.66 us
    unnamed x9, local copies, waits for them, and re-layouts  1.64 us
  transfers between devices with their start and end apart: 18, of which 9 were waited for; matrix products, arithmetic and copies ran while one was open for 0% of the time, Pallas kernels for 11%

profile of v3, /device:TPU:0, one launch (start us, length us, event | category | flops | bytes accessed | tf_op | source)
XLA Modules:
  0.0 53.8 jit_solution(1261257251160354059)
XLA Ops:
  0.0 0.9 %copy-done.1 = f32[4,2,4,8,192]{4,3,2,1,0:T(8,128)S(1)} copy-done((f32[4,2,4,8,192]{4,3,2,1,0:T(8,128)S(1)}, f32[4,2,4,8,192]{4,3,2,1,0:T(8,128)}, u32[]{:S(2)}) %copy-start.1) | copy-done | bytes 196632
  1.0 5.1 %collective-permute-start.2 = (f32[9,8,128]{2,1,0:T(8,128)S(1)}, f32[9,8,128]{2,1,0:T(8,128)S(1)}, u32[]{:S(2)}, u32[]{:S(2)}) collective-permute-start(f32[9,8,128]{2,1,0:T(8,128)S(1)} %get-tuple-element.28), channel_id=1, source_target_pairs={{0,6},{1,7},{2,4},{3,5},{4,2},{5,3},{6,0},{7,1},{8,14},{9,15},{10,... | collective-permute-start | bytes 110600 | tf_op jit(solution)/shard_map/ppermute | solution.py:25
  6.2 0.6 %collective-permute-start = (f32[9,8,128]{2,1,0:T(8,128)S(1)}, f32[9,8,128]{2,1,0:T(8,128)S(1)}, u32[]{:S(2)}, u32[]{:S(2)}) collective-permute-start(f32[9,8,128]{2,1,0:T(8,128)S(1)} %get-tuple-element.28), channel_id=1, source_target_pairs={{0,2},{1,3},{2,0},{3,1},{4,6},{5,7},{6,4},{7,5},{8,10},{9,11},{10,... | collective-permute-start | bytes 110600 | tf_op jit(solution)/shard_map/ppermute | solution.py:25
  6.8 2.6 %collective-permute-start.5 = (f32[10,8,128]{2,1,0:T(8,128)S(1)}, f32[10,8,128]{2,1,0:T(8,128)S(1)}, u32[]{:S(2)}, u32[]{:S(2)}) collective-permute-start(f32[10,8,128]{2,1,0:T(8,128)S(1)} %get-tuple-element.32), channel_id=1, source_target_pairs={{0,24},{8,0},{16,8},{24,16},{1,25},{9,1},{17,9},{25,17},{2,26},{10... | collective-permute-start | bytes 122888 | tf_op jit(solution)/shard_map/ppermute | solution.py:20
  9.4 1.6 %collective-permute-done.1 = f32[9,8,128]{2,1,0:T(8,128)S(1)} collective-permute-done((f32[9,8,128]{2,1,0:T(8,128)S(1)}, f32[9,8,128]{2,1,0:T(8,128)S(1)}, u32[]{:S(2)}, u32[]{:S(2)}) %collective-permute-start.1) | collective-permute-done | bytes 36896 | tf_op jit(solution)/shard_map/ppermute | solution.py:25
  11.2 2.1 %collective-permute-start.7 = (f32[14,8,128]{2,1,0:T(8,128)S(1)}, f32[14,8,128]{2,1,0:T(8,128)S(1)}, u32[]{:S(2)}, u32[]{:S(2)}) collective-permute-start(f32[14,8,128]{2,1,0:T(8,128)S(1)} %get-tuple-element.53), channel_id=1, source_target_pairs={{0,4},{1,5},{2,6},{3,7},{4,0},{5,1},{6,2},{7,3},{8,12},{9,13},{10,... | collective-permute-start | bytes 172040 | tf_op jit(solution)/shard_map/ppermute | solution.py:25
  13.3 2.0 %collective-permute-start.6 = (f32[14,8,128]{2,1,0:T(8,128)S(1)}, f32[14,8,128]{2,1,0:T(8,128)S(1)}, u32[]{:S(2)}, u32[]{:S(2)}) collective-permute-start(f32[14,8,128]{2,1,0:T(8,128)S(1)} %get-tuple-element.53), channel_id=1, source_target_pairs={{0,2},{1,3},{2,0},{3,1},{4,6},{5,7},{6,4},{7,5},{8,10},{9,11},{10,... | collective-permute-start | bytes 172040 | tf_op jit(solution)/shard_map/ppermute | solution.py:25
  15.6 0.6 %shard_map.38.refs_1_ = bf16[6,128,256]{2,1,0:T(8,128)(2,1)S(1)} custom-call(f32[4,9,8,128]{3,2,1,0:T(8,128)S(1)} %pad_maximum_fusion.2.refs_0_, f32[4,9,8,128]{3,2,1,0:T(8,128)S(1)} %collective-permute-done.3.refs_1_), custom_call_target="tpu_custom_call" | custom-call | flops 113246208 | bytes 600000 | tf_op jit(solution)/shard_map/pallas_call | solution.py:187
  16.3 0.7 %copy-done.2 = s32[4,2]{0,1:T(2,128)S(1)} copy-done((s32[4,2]{0,1:T(2,128)S(1)}, s32[4,2]{0,1:T(2,128)}, u32[]{:S(2)}) %copy-start.2) | copy-done | bytes 56
  16.9 0.5 shard_map.39
  17.7 3.6 %collective-permute-done.8 = f32[14,8,128]{2,1,0:T(8,128)S(1)} collective-permute-done((f32[14,8,128]{2,1,0:T(8,128)S(1)}, f32[14,8,128]{2,1,0:T(8,128)S(1)}, u32[]{:S(2)}, u32[]{:S(2)}) %collective-permute-start.8) | collective-permute-done | bytes 57376 | tf_op jit(solution)/shard_map/ppermute | solution.py:25
  21.4 3.3 %collective-permute-start.4 = (f32[256,128]{1,0:T(8,128)S(1)}, f32[256,128]{1,0:T(8,128)S(1)}, u32[]{:S(2)}, u32[]{:S(2)}) collective-permute-start(f32[256,128]{1,0:T(8,128)S(1)} %get-tuple-element.30), channel_id=1, source_target_pairs={{0,24},{8,0},{16,8},{24,16},{1,25},{9,1},{17,9},{25,17},{2,26},{10... | collective-permute-start | bytes 393224 | tf_op jit(solution)/shard_map/ppermute | solution.py:20
  24.8 1.2 %collective-permute-start.11 = (f32[33,8,128]{2,1,0:T(8,128)S(1)}, f32[33,8,128]{2,1,0:T(8,128)S(1)}, u32[]{:S(2)}, u32[]{:S(2)}) collective-permute-start(f32[33,8,128]{2,1,0:T(8,128)S(1)} %get-tuple-element.51), channel_id=1, source_target_pairs={{0,2},{1,3},{2,0},{3,1},{4,6},{5,7},{6,4},{7,5},{8,10},{9,11},{10,... | collective-permute-start | bytes 405512 | tf_op jit(solution)/shard_map/ppermute | solution.py:25
  26.0 3.2 %collective-permute-start.13 = (f32[33,8,128]{2,1,0:T(8,128)S(1)}, f32[33,8,128]{2,1,0:T(8,128)S(1)}, u32[]{:S(2)}, u32[]{:S(2)}) collective-permute-start(f32[33,8,128]{2,1,0:T(8,128)S(1)} %get-tuple-element.51), channel_id=1, source_target_pairs={{0,6},{1,7},{2,4},{3,5},{4,2},{5,3},{6,0},{7,1},{8,14},{9,15},{10,... | collective-permute-start | bytes 405512 | tf_op jit(solution)/shard_map/ppermute | solution.py:25
  29.2 0.9 %shard_map.40.refs_2_.refs_0_ = bf16[10,128,256]{2,1,0:T(8,128)(2,1)S(1)} custom-call(s32[2,4]{1,0:T(2,128)S(1)} %bitcast.16, bf16[6,128,256]{2,1,0:T(8,128)(2,1)S(1)} %shard_map.38.refs_1_, f32[4,14,8,128]{3,2,1,0:T(8,128)S(1)} %constant_dynamic-update-slice_fusion.refs_2_, f32[4,14,8,128]{3,2,1,0:T(8,128)S(1)} %collective-permute-done.9.refs_3_), custom_call_target="tpu_custom_call" | custom-call | flops 188743680 | bytes 1000000 | tf_op jit(solution)/shard_map/pallas_call | solution.py:187
  30.1 0.9 %shard_map.41 = (f32[256,128]{1,0:T(8,128)S(1)}, f32[256,128]{1,0:T(8,128)S(1)}) custom-call(s32[2,4]{1,0:T(2,128)S(1)} %bitcast.17, f32[256,128]{1,0:T(8,128)S(1)} %get-tuple-element.29.refs_0_, f32[256,128]{1,0:T(8,128)S(1)} %collective-permute-done.4.refs_1_, bf16[10,128,256]{2,1,0:T(8,128)(2,1)S(1)} %shard_map.40.refs_2_.refs_0_), custom_call_target="tpu_custom_call" | custom-call | flops 100663296 | bytes 2000000 | tf_op jit(solution)/shard_map/pallas_call | solution.py:248
  30.9 0.5 collective-permute-start.10
  31.4 1.8 %collective-permute-done.12 = f32[33,8,128]{2,1,0:T(8,128)S(1)} collective-permute-done((f32[33,8,128]{2,1,0:T(8,128)S(1)}, f32[33,8,128]{2,1,0:T(8,128)S(1)}, u32[]{:S(2)}, u32[]{:S(2)}) %collective-permute-start.12) | collective-permute-done | bytes 135200 | tf_op jit(solution)/shard_map/ppermute | solution.py:25
  33.2 3.1 %collective-permute-done.11 = f32[33,8,128]{2,1,0:T(8,128)S(1)} collective-permute-done((f32[33,8,128]{2,1,0:T(8,128)S(1)}, f32[33,8,128]{2,1,0:T(8,128)S(1)}, u32[]{:S(2)}, u32[]{:S(2)}) %collective-permute-start.11) | collective-permute-done | bytes 135200 | tf_op jit(solution)/shard_map/ppermute | solution.py:25
  36.5 0.4 collective-permute-done.10.refs_0_
  36.9 0.6 %collective-permute-start.16 = (f32[4,19,8,128]{3,2,1,0:T(8,128)S(1)}, f32[4,19,8,128]{3,2,1,0:T(8,128)S(1)}, u32[]{:S(2)}, u32[]{:S(2)}) collective-permute-start(f32[4,19,8,128]{3,2,1,0:T(8,128)S(1)} %pad_maximum_fusion.refs_2_.refs_1_), channel_id=1, source_target_pairs={{0,1},{1,0},{2,3},{3,2},{4,5},{5,4},{6,7},{7,6},{8,9},{9,8},{10,11... | collective-permute-start | bytes 933896 | tf_op jit(solution)/shard_map/ppermute | solution.py:25
  37.5 0.9 %collective-permute-done.14.refs_2_ = f32[4,14,8,128]{3,2,1,0:T(8,128)S(1)} collective-permute-done((f32[4,14,8,128]{3,2,1,0:T(8,128)S(1)}, f32[4,14,8,128]{3,2,1,0:T(8,128)S(1)}, u32[]{:S(2)}, u32[]{:S(2)}) %collective-permute-start.14) | collective-permute-done | bytes 229408 | tf_op jit(solution)/shard_map/ppermute | solution.py:25
  38.4 0.8 %shard_map.42.refs_2_.refs_1_ = bf16[10,128,256]{2,1,0:T(8,128)(2,1)S(1)} custom-call(bf16[10,128,256]{2,1,0:T(8,128)(2,1)S(1)} %shard_map.40.refs_2_.refs_0_, f32[4,14,8,128]{3,2,1,0:T(8,128)S(1)} %pad_maximum_fusion.1.refs_1_, f32[4,14,8,128]{3,2,1,0:T(8,128)S(1)} %collective-permute-done.14.refs_2_), custom_call_target="tpu_custom_call" | custom-call | flops 188743680 | bytes 1000000 | tf_op jit(solution)/shard_map/pallas_call | solution.py:187
  39.2 0.9 %shard_map.43 = (f32[256,128]{1,0:T(8,128)S(1)}, f32[256,128]{1,0:T(8,128)S(1)}) custom-call(s32[2,4]{1,0:T(2,128)S(1)} %bitcast.18, f32[256,128]{1,0:T(8,128)S(1)} %collective-permute-done.10.refs_0_, f32[256,128]{1,0:T(8,128)S(1)} %get-tuple-element.38.refs_1_, bf16[10,128,256]{2,1,0:T(8,128)(2,1)S(1)} %shard_map.42.refs_2_.refs_1_), custom_call_target="tpu_custom_call" | custom-call | flops 100663296 | bytes 2000000 | tf_op jit(solution)/shard_map/pallas_call | solution.py:248
  40.1 0.6 %collective-permute-start.15 = (f32[256,128]{1,0:T(8,128)S(1)}, f32[256,128]{1,0:T(8,128)S(1)}, u32[]{:S(2)}, u32[]{:S(2)}) collective-permute-start(f32[256,128]{1,0:T(8,128)S(1)} %get-tuple-element.47), channel_id=1, source_target_pairs={{0,24},{8,0},{16,8},{24,16},{1,25},{9,1},{17,9},{25,17},{2,26},{10... | collective-permute-start | bytes 393224 | tf_op jit(solution)/shard_map/ppermute | solution.py:20
  40.8 0.9 %shard_map.44.refs_2_.refs_0_ = bf16[10,128,256]{2,1,0:T(8,128)(2,1)S(1)} custom-call(s32[2,4]{1,0:T(2,128)S(1)} %bitcast.19, bf16[10,128,256]{2,1,0:T(8,128)(2,1)S(1)} %shard_map.42.refs_2_.refs_1_, f32[4,19,8,128]{3,2,1,0:T(8,128)S(1)} %pad_maximum_fusion.refs_2_.refs_1_, f32[4,19,8,128]{3,2,1,0:T(8,128)S(1)} %collective-permute-done.16.refs_3_.refs_2_), custom_call_target="tpu_custom_call" | custom-call | flops 188743680 | bytes 1000000 | tf_op jit(solution)/shard_map/pallas_call | solution.py:187
  41.7 4.0 %collective-permute-done.15.refs_1_ = f32[256,128]{1,0:T(8,128)S(1)} collective-permute-done((f32[256,128]{1,0:T(8,128)S(1)}, f32[256,128]{1,0:T(8,128)S(1)}, u32[]{:S(2)}, u32[]{:S(2)}) %collective-permute-start.15) | collective-permute-done | bytes 131104 | tf_op jit(solution)/shard_map/ppermute | solution.py:20
  45.7 0.9 %shard_map.45 = (f32[256,128]{1,0:T(8,128)S(1)}, f32[256,128]{1,0:T(8,128)S(1)}) custom-call(s32[2,4]{1,0:T(2,128)S(1)} %bitcast.20, f32[256,128]{1,0:T(8,128)S(1)} %get-tuple-element.46.refs_0_, f32[256,128]{1,0:T(8,128)S(1)} %collective-permute-done.15.refs_1_, bf16[10,128,256]{2,1,0:T(8,128)(2,1)S(1)} %shard_map.44.refs_2_.refs_0_), custom_call_target="tpu_custom_call" | custom-call | flops 100663296 | bytes 2000000 | tf_op jit(solution)/shard_map/pallas_call | solution.py:248
  46.7 0.6 %collective-permute-start.17 = (f32[256,128]{1,0:T(8,128)S(1)}, f32[256,128]{1,0:T(8,128)S(1)}, u32[]{:S(2)}, u32[]{:S(2)}) collective-permute-start(f32[256,128]{1,0:T(8,128)S(1)} %get-tuple-element.49), channel_id=1, source_target_pairs={{0,8},{8,16},{16,24},{24,0},{1,9},{9,17},{17,25},{25,1},{2,10},{10... | collective-permute-start | bytes 393224 | tf_op jit(solution)/shard_map/ppermute | solution.py:20
  47.2 0.4 shard_map.46.refs_2_
  47.7 4.9 %collective-permute-done.17.refs_0_ = f32[256,128]{1,0:T(8,128)S(1)} collective-permute-done((f32[256,128]{1,0:T(8,128)S(1)}, f32[256,128]{1,0:T(8,128)S(1)}, u32[]{:S(2)}, u32[]{:S(2)}) %collective-permute-start.17) | collective-permute-done | bytes 131104 | tf_op jit(solution)/shard_map/ppermute | solution.py:20
  52.6 1.2 %shard_map.47 = f32[512,128]{1,0:T(8,128)} custom-call(s32[2,4]{1,0:T(2,128)S(1)} %bitcast.21, f32[256,128]{1,0:T(8,128)S(1)} %collective-permute-done.17.refs_0_, f32[256,128]{1,0:T(8,128)S(1)} %get-tuple-element.50.refs_1_, bf16[4,128,256]{2,1,0:T(8,128)(2,1)S(1)} %shard_map.46.refs_2_), custom_call_target="tpu_custom_call" | custom-call | flops 100663296 | bytes 2000000 | tf_op jit(solution)/shard_map/pallas_call | solution.py:248
  (39 shorter events, 1.0 us)
Async XLA Ops:
  0.0 0.9 %copy-start.1 = (f32[4,2,4,8,192]{4,3,2,1,0:T(8,128)S(1)}, f32[4,2,4,8,192]{4,3,2,1,0:T(8,128)}, u32[]{:S(2)}) copy-start(f32[4,2,4,8,192]{4,3,2,1,0:T(8,128)} %refl_ref.1) | copy-start | bytes 589828
  1.0 8.4 %collective-permute-start.2 = (f32[9,8,128]{2,1,0:T(8,128)S(1)}, f32[9,8,128]{2,1,0:T(8,128)S(1)}, u32[]{:S(2)}, u32[]{:S(2)}) collective-permute-start(f32[9,8,128]{2,1,0:T(8,128)S(1)} %get-tuple-element.28), channel_id=1, source_target_pairs={{0,6},{1,7},{2,4},{3,5},{4,2},{5,3},{6,0},{7,1},{8,14},{9,15},{10,... | collective-permute-start | bytes 110600 | tf_op jit(solution)/shard_map/ppermute | solution.py:25
  6.2 4.9 %collective-permute-start.1 = (f32[9,8,128]{2,1,0:T(8,128)S(1)}, f32[9,8,128]{2,1,0:T(8,128)S(1)}, u32[]{:S(2)}, u32[]{:S(2)}) collective-permute-start(f32[9,8,128]{2,1,0:T(8,128)S(1)} %get-tuple-element.28), channel_id=1, source_target_pairs={{0,4},{1,5},{2,6},{3,7},{4,0},{5,1},{6,2},{7,3},{8,12},{9,13},{10,... | collective-permute-start | bytes 110600 | tf_op jit(solution)/shard_map/ppermute | solution.py:25
  6.2 4.9 %collective-permute-start = (f32[9,8,128]{2,1,0:T(8,128)S(1)}, f32[9,8,128]{2,1,0:T(8,128)S(1)}, u32[]{:S(2)}, u32[]{:S(2)}) collective-permute-start(f32[9,8,128]{2,1,0:T(8,128)S(1)} %get-tuple-element.28), channel_id=1, source_target_pairs={{0,2},{1,3},{2,0},{3,1},{4,6},{5,7},{6,4},{7,5},{8,10},{9,11},{10,... | collective-permute-start | bytes 110600 | tf_op jit(solution)/shard_map/ppermute | solution.py:25
  6.8 4.3 %collective-permute-start.5 = (f32[10,8,128]{2,1,0:T(8,128)S(1)}, f32[10,8,128]{2,1,0:T(8,128)S(1)}, u32[]{:S(2)}, u32[]{:S(2)}) collective-permute-start(f32[10,8,128]{2,1,0:T(8,128)S(1)} %get-tuple-element.32), channel_id=1, source_target_pairs={{0,24},{8,0},{16,8},{24,16},{1,25},{9,1},{17,9},{25,17},{2,26},{10... | collective-permute-start | bytes 122888 | tf_op jit(solution)/shard_map/ppermute | solution.py:20
  11.0 4.6 %collective-permute-start.3 = (f32[4,9,8,128]{3,2,1,0:T(8,128)S(1)}, f32[4,9,8,128]{3,2,1,0:T(8,128)S(1)}, u32[]{:S(2)}, u32[]{:S(2)}) collective-permute-start(f32[4,9,8,128]{3,2,1,0:T(8,128)S(1)} %pad_maximum_fusion.2.refs_0_), channel_id=1, source_target_pairs={{0,1},{1,0},{2,3},{3,2},{4,5},{5,4},{6,7},{7,6},{8,9},{9,8},{10,11... | collective-permute-start | bytes 442376 | tf_op jit(solution)/shard_map/ppermute | solution.py:25
  11.1 5.1 %copy-start = (f32[512,128]{1,0:T(8,128)S(1)}, f32[512,128]{1,0:T(8,128)}, u32[]{:S(2)}) copy-start(f32[512,128]{1,0:T(8,128)} %refs_0_.1) | copy-start | bytes 786436
  11.2 6.3 %collective-permute-start.7 = (f32[14,8,128]{2,1,0:T(8,128)S(1)}, f32[14,8,128]{2,1,0:T(8,128)S(1)}, u32[]{:S(2)}, u32[]{:S(2)}) collective-permute-start(f32[14,8,128]{2,1,0:T(8,128)S(1)} %get-tuple-element.53), channel_id=1, source_target_pairs={{0,4},{1,5},{2,6},{3,7},{4,0},{5,1},{6,2},{7,3},{8,12},{9,13},{10,... | collective-permute-start | bytes 172040 | tf_op jit(solution)/shard_map/ppermute | solution.py:25
  13.3 4.4 %collective-permute-start.6 = (f32[14,8,128]{2,1,0:T(8,128)S(1)}, f32[14,8,128]{2,1,0:T(8,128)S(1)}, u32[]{:S(2)}, u32[]{:S(2)}) collective-permute-start(f32[14,8,128]{2,1,0:T(8,128)S(1)} %get-tuple-element.53), channel_id=1, source_target_pairs={{0,2},{1,3},{2,0},{3,1},{4,6},{5,7},{6,4},{7,5},{8,10},{9,11},{10,... | collective-permute-start | bytes 172040 | tf_op jit(solution)/shard_map/ppermute | solution.py:25
  15.3 6.0 %collective-permute-start.8 = (f32[14,8,128]{2,1,0:T(8,128)S(1)}, f32[14,8,128]{2,1,0:T(8,128)S(1)}, u32[]{:S(2)}, u32[]{:S(2)}) collective-permute-start(f32[14,8,128]{2,1,0:T(8,128)S(1)} %get-tuple-element.53), channel_id=1, source_target_pairs={{0,6},{1,7},{2,4},{3,5},{4,2},{5,3},{6,0},{7,1},{8,14},{9,15},{10,... | collective-permute-start | bytes 172040 | tf_op jit(solution)/shard_map/ppermute | solution.py:25
  16.2 0.7 %copy-start.2 = (s32[4,2]{0,1:T(2,128)S(1)}, s32[4,2]{0,1:T(2,128)}, u32[]{:S(2)}) copy-start(s32[4,2]{0,1:T(2,128)} %param.4) | copy-start | bytes 100
  21.3 7.8 %collective-permute-start.9 = (f32[4,14,8,128]{3,2,1,0:T(8,128)S(1)}, f32[4,14,8,128]{3,2,1,0:T(8,128)S(1)}, u32[]{:S(2)}, u32[]{:S(2)}) collective-permute-start(f32[4,14,8,128]{3,2,1,0:T(8,128)S(1)} %constant_dynamic-update-slice_fusion.refs_2_), channel_id=1, source_target_pairs={{0,1},{1,0},{2,3},{3,2},{4,5},{5,4},{6,7},{7,6},{8,9},{9,8},{10,11... | collective-permute-start | bytes 688136 | tf_op jit(solution)/shard_map/ppermute | solution.py:25
  21.4 8.6 %collective-permute-start.4 = (f32[256,128]{1,0:T(8,128)S(1)}, f32[256,128]{1,0:T(8,128)S(1)}, u32[]{:S(2)}, u32[]{:S(2)}) collective-permute-start(f32[256,128]{1,0:T(8,128)S(1)} %get-tuple-element.30), channel_id=1, source_target_pairs={{0,24},{8,0},{16,8},{24,16},{1,25},{9,1},{17,9},{25,17},{2,26},{10... | collective-permute-start | bytes 393224 | tf_op jit(solution)/shard_map/ppermute | solution.py:20
  24.7 8.5 %collective-permute-start.12 = (f32[33,8,128]{2,1,0:T(8,128)S(1)}, f32[33,8,128]{2,1,0:T(8,128)S(1)}, u32[]{:S(2)}, u32[]{:S(2)}) collective-permute-start(f32[33,8,128]{2,1,0:T(8,128)S(1)} %get-tuple-element.51), channel_id=1, source_target_pairs={{0,4},{1,5},{2,6},{3,7},{4,0},{5,1},{6,2},{7,3},{8,12},{9,13},{10,... | collective-permute-start | bytes 405512 | tf_op jit(solution)/shard_map/ppermute | solution.py:25
  24.8 11.5 %collective-permute-start.11 = (f32[33,8,128]{2,1,0:T(8,128)S(1)}, f32[33,8,128]{2,1,0:T(8,128)S(1)}, u32[]{:S(2)}, u32[]{:S(2)}) collective-permute-start(f32[33,8,128]{2,1,0:T(8,128)S(1)} %get-tuple-element.51), channel_id=1, source_target_pairs={{0,2},{1,3},{2,0},{3,1},{4,6},{5,7},{6,4},{7,5},{8,10},{9,11},{10,... | collective-permute-start | bytes 405512 | tf_op jit(solution)/shard_map/ppermute | solution.py:25
  26.0 10.4 %collective-permute-start.13 = (f32[33,8,128]{2,1,0:T(8,128)S(1)}, f32[33,8,128]{2,1,0:T(8,128)S(1)}, u32[]{:S(2)}, u32[]{:S(2)}) collective-permute-start(f32[33,8,128]{2,1,0:T(8,128)S(1)} %get-tuple-element.51), channel_id=1, source_target_pairs={{0,6},{1,7},{2,4},{3,5},{4,2},{5,3},{6,0},{7,1},{8,14},{9,15},{10,... | collective-permute-start | bytes 405512 | tf_op jit(solution)/shard_map/ppermute | solution.py:25
  30.9 5.9 %collective-permute-start.10 = (f32[256,128]{1,0:T(8,128)S(1)}, f32[256,128]{1,0:T(8,128)S(1)}, u32[]{:S(2)}, u32[]{:S(2)}) collective-permute-start(f32[256,128]{1,0:T(8,128)S(1)} %get-tuple-element.37), channel_id=1, source_target_pairs={{0,8},{8,16},{16,24},{24,0},{1,9},{9,17},{17,25},{25,1},{2,10},{10... | collective-permute-start | bytes 393224 | tf_op jit(solution)/shard_map/ppermute | solution.py:20
  36.9 1.5 %collective-permute-start.14 = (f32[4,14,8,128]{3,2,1,0:T(8,128)S(1)}, f32[4,14,8,128]{3,2,1,0:T(8,128)S(1)}, u32[]{:S(2)}, u32[]{:S(2)}) collective-permute-start(f32[4,14,8,128]{3,2,1,0:T(8,128)S(1)} %pad_maximum_fusion.1.refs_1_), channel_id=1, source_target_pairs={{0,1},{1,0},{2,3},{3,2},{4,5},{5,4},{6,7},{7,6},{8,9},{9,8},{10,11... | collective-permute-start | bytes 688136 | tf_op jit(solution)/shard_map/ppermute | solution.py:25
  36.9 3.9 %collective-permute-start.16 = (f32[4,19,8,128]{3,2,1,0:T(8,128)S(1)}, f32[4,19,8,128]{3,2,1,0:T(8,128)S(1)}, u32[]{:S(2)}, u32[]{:S(2)}) collective-permute-start(f32[4,19,8,128]{3,2,1,0:T(8,128)S(1)} %pad_maximum_fusion.refs_2_.refs_1_), channel_id=1, source_target_pairs={{0,1},{1,0},{2,3},{3,2},{4,5},{5,4},{6,7},{7,6},{8,9},{9,8},{10,11... | collective-permute-start | bytes 933896 | tf_op jit(solution)/shard_map/ppermute | solution.py:25
  40.1 5.6 %collective-permute-start.15 = (f32[256,128]{1,0:T(8,128)S(1)}, f32[256,128]{1,0:T(8,128)S(1)}, u32[]{:S(2)}, u32[]{:S(2)}) collective-permute-start(f32[256,128]{1,0:T(8,128)S(1)} %get-tuple-element.47), channel_id=1, source_target_pairs={{0,24},{8,0},{16,8},{24,16},{1,25},{9,1},{17,9},{25,17},{2,26},{10... | collective-permute-start | bytes 393224 | tf_op jit(solution)/shard_map/ppermute | solution.py:20
  46.7 5.9 %collective-permute-start.17 = (f32[256,128]{1,0:T(8,128)S(1)}, f32[256,128]{1,0:T(8,128)S(1)}, u32[]{:S(2)}, u32[]{:S(2)}) collective-permute-start(f32[256,128]{1,0:T(8,128)S(1)} %get-tuple-element.49), channel_id=1, source_target_pairs={{0,8},{8,16},{16,24},{24,0},{1,9},{9,17},{17,25},{25,1},{2,10},{10... | collective-permute-start | bytes 393224 | tf_op jit(solution)/shard_map/ppermute | solution.py:20

commit v4 on v1

--- a/solution.py
+++ b/solution.py
@@ -46,7 +46,7 @@
                 for sweep in (2 * ph, 2 * ph + 1):
                     entries += [(sweep, base + k) for k in range(nwin - 1)]
             self.phases.append((entries, self_carry))
-        groups = [[ph] for ph in range(rounds - 1)] + [[rounds - 1, rounds]]
+        groups = [[ph] for ph in range(rounds + 1)]
         self.groups = []
         self.where = {}
         edge_at = 0
@@ -328,9 +328,9 @@
     parts = [evecs]
     mats = None
     results, movements = [], []
-    gather.together(range(2, groups))
+    gather.together(range(2, rounds))
     for ph in range(rounds):
-        if ph < groups:
+        if ph < rounds:
             ready = results[min(ph, 2) - 1] if ph else None
             tiles = gather.receive(ph, movements[1] if ph > 1 else None, ready)
         mats = matrices(plan, ph, offsets, mats, tiles)
@@ -342,6 +342,9 @@
         moved = shifted(result, "row", 1 if away else -1)
         movements.append(moved)
         parts = [moved, kept] if away else [kept, moved]
+    if gather.stepwise:
+        gather.doubled(rounds, after(gather.own[rounds], results[min(2, rounds - 1)]))
+    tiles = gather.receive(rounds, results[-1], results[-1])
     mats = matrices(plan, rounds, offsets, mats, tiles)
     (result,) = phase(rounds, rounds, nwin, offsets, parts, mats, (rows,))
     if rounds % 2:

time: 52.7 us -> 53.7 us (1.019)
  starting transfers between devices: 23 us -> 26.4 us
  waiting for transfers between devices: 19.1 us -> 17 us
    ppermute x12 -> x15, starting transfers between devices: 13 us -> 16.5 us  [swapped(): return lax.ppermute(value, 'col', [(i, i ^ bit) for i in range(devices)])]
    ppermute x5, waiting for transfers between devices: 6.25 us -> 3.29 us  [shifted(): lax.ppermute(value, axis, [(i, (i + by) % devices) for i in range(devices)])]
    ppermute x12 -> x15, waiting for transfers between devices: 12.9 us -> 13.7 us  [swapped(): return lax.ppermute(value, 'col', [(i, i ^ bit) for i in range(devices)])]
  transfers between devices with their start and end apart: 17 -> 20, of which waited for: 9 -> 12; matrix products, arithmetic and copies ran while one was open for 0% -> 0% of each run, Pallas kernels for 11% -> 13%
where the time goes in v4:
time: 53.7 us; the launch traced here: 53.5 us
  starting transfers between devices  26.4 us (49%)
  waiting for transfers between devices  17 us (32%)
  Pallas kernels  8.16 us (15%)
  local copies, waits for them, and re-layouts  1.68 us (3%)
    ppermute x15, starting transfers between devices, swapped(): return lax.ppermute(value, 'col', [(i, i ^ bit) for i in range(devices)])  16.5 us
    ppermute x15, waiting for transfers between devices, swapped(): return lax.ppermute(value, 'col', [(i, i ^ bit) for i in range(devices)])  13.7 us
    ppermute x5, starting transfers between devices, shifted(): lax.ppermute(value, axis, [(i, (i + by) % devices) for i in range(devices)])  9.93 us
    pallas_call x5, Pallas kernels, phase(): pl.pallas_call(functools.partial(phase_kernel, ph, rounds, nwin, len(part...  4.46 us
    pallas_call x5, Pallas kernels, matrices(): pl.pallas_call(functools.partial(matrix_kernel, plan, ph, masked), out_sh...  3.62 us
    ppermute x5, waiting for transfers between devices, shifted(): lax.ppermute(value, axis, [(i, (i + by) % devices) for i in range(devices)])  3.29 us
    unnamed x7, local copies, waits for them, and re-layouts  1.63 us
  transfers between devices with their start and end apart: 20, of which 12 were waited for; matrix products, arithmetic and copies ran while one was open for 0% of the time, Pallas kernels for 13%

profile of v4, /device:TPU:0, one launch (start us, length us, event | category | flops | bytes accessed | tf_op | source)
XLA Modules:
  0.0 53.5 jit_solution(11287622730961725379)
XLA Ops:
  0.0 0.9 %copy-done.1 = f32[4,2,4,8,192]{4,3,2,1,0:T(8,128)S(1)} copy-done((f32[4,2,4,8,192]{4,3,2,1,0:T(8,128)S(1)}, f32[4,2,4,8,192]{4,3,2,1,0:T(8,128)}, u32[]{:S(2)}) %copy-start.1) | copy-done | bytes 196632
  1.0 3.9 %collective-permute-start.5 = (f32[10,8,128]{2,1,0:T(8,128)S(1)}, f32[10,8,128]{2,1,0:T(8,128)S(1)}, u32[]{:S(2)}, u32[]{:S(2)}) collective-permute-start(f32[10,8,128]{2,1,0:T(8,128)S(1)} %get-tuple-element.37), channel_id=1, source_target_pairs={{0,24},{8,0},{16,8},{24,16},{1,25},{9,1},{17,9},{25,17},{2,26},{10... | collective-permute-start | bytes 122888 | tf_op jit(solution)/shard_map/ppermute | solution.py:20
  5.0 3.6 %collective-permute-start.2 = (f32[9,8,128]{2,1,0:T(8,128)S(1)}, f32[9,8,128]{2,1,0:T(8,128)S(1)}, u32[]{:S(2)}, u32[]{:S(2)}) collective-permute-start(f32[9,8,128]{2,1,0:T(8,128)S(1)} %get-tuple-element.33), channel_id=1, source_target_pairs={{0,6},{1,7},{2,4},{3,5},{4,2},{5,3},{6,0},{7,1},{8,14},{9,15},{10,... | collective-permute-start | bytes 110600 | tf_op jit(solution)/shard_map/ppermute | solution.py:25
  8.6 0.8 %collective-permute-start = (f32[9,8,128]{2,1,0:T(8,128)S(1)}, f32[9,8,128]{2,1,0:T(8,128)S(1)}, u32[]{:S(2)}, u32[]{:S(2)}) collective-permute-start(f32[9,8,128]{2,1,0:T(8,128)S(1)} %get-tuple-element.33), channel_id=1, source_target_pairs={{0,2},{1,3},{2,0},{3,1},{4,6},{5,7},{6,4},{7,5},{8,10},{9,11},{10,... | collective-permute-start | bytes 110600 | tf_op jit(solution)/shard_map/ppermute | solution.py:25
  9.4 1.3 %collective-permute-start.6 = (f32[14,8,128]{2,1,0:T(8,128)S(1)}, f32[14,8,128]{2,1,0:T(8,128)S(1)}, u32[]{:S(2)}, u32[]{:S(2)}) collective-permute-start(f32[14,8,128]{2,1,0:T(8,128)S(1)} %pad_maximum_fusion.6), channel_id=1, source_target_pairs={{0,2},{1,3},{2,0},{3,1},{4,6},{5,7},{6,4},{7,5},{8,10},{9,11},{10,... | collective-permute-start | bytes 172040 | tf_op jit(solution)/shard_map/ppermute | solution.py:25
  11.1 2.4 %collective-permute-done.1 = f32[9,8,128]{2,1,0:T(8,128)S(1)} collective-permute-done((f32[9,8,128]{2,1,0:T(8,128)S(1)}, f32[9,8,128]{2,1,0:T(8,128)S(1)}, u32[]{:S(2)}, u32[]{:S(2)}) %collective-permute-start.1) | collective-permute-done | bytes 36896 | tf_op jit(solution)/shard_map/ppermute | solution.py:25
  14.1 2.1 %collective-permute-start.7 = (f32[2,14,8,128]{3,2,1,0:T(8,128)S(1)}, f32[2,14,8,128]{3,2,1,0:T(8,128)S(1)}, u32[]{:S(2)}, u32[]{:S(2)}) collective-permute-start(f32[2,14,8,128]{3,2,1,0:T(8,128)S(1)} %pad_maximum_fusion.3), channel_id=1, source_target_pairs={{0,4},{1,5},{2,6},{3,7},{4,0},{5,1},{6,2},{7,3},{8,12},{9,13},{10,... | collective-permute-start | bytes 344072 | tf_op jit(solution)/shard_map/ppermute | solution.py:25
  16.2 0.6 %shard_map.38.refs_1_ = bf16[6,128,256]{2,1,0:T(8,128)(2,1)S(1)} custom-call(f32[4,9,8,128]{3,2,1,0:T(8,128)S(1)} %pad_maximum_fusion.2.refs_0_, f32[4,9,8,128]{3,2,1,0:T(8,128)S(1)} %collective-permute-done.3.refs_1_), custom_call_target="tpu_custom_call" | custom-call | flops 113246208 | bytes 600000 | tf_op jit(solution)/shard_map/pallas_call | solution.py:187
  16.8 0.7 %copy-done.2 = s32[4,2]{0,1:T(2,128)S(1)} copy-done((s32[4,2]{0,1:T(2,128)S(1)}, s32[4,2]{0,1:T(2,128)}, u32[]{:S(2)}) %copy-start.2) | copy-done | bytes 56
  18.0 4.5 %collective-permute-done.7 = f32[2,14,8,128]{3,2,1,0:T(8,128)S(1)} collective-permute-done((f32[2,14,8,128]{3,2,1,0:T(8,128)S(1)}, f32[2,14,8,128]{3,2,1,0:T(8,128)S(1)}, u32[]{:S(2)}, u32[]{:S(2)}) %collective-permute-start.7) | collective-permute-done | bytes 114720 | tf_op jit(solution)/shard_map/ppermute | solution.py:25
  22.6 0.6 %collective-permute-start.4 = (f32[256,128]{1,0:T(8,128)S(1)}, f32[256,128]{1,0:T(8,128)S(1)}, u32[]{:S(2)}, u32[]{:S(2)}) collective-permute-start(f32[256,128]{1,0:T(8,128)S(1)} %get-tuple-element.35), channel_id=1, source_target_pairs={{0,24},{8,0},{16,8},{24,16},{1,25},{9,1},{17,9},{25,17},{2,26},{10... | collective-permute-start | bytes 393224 | tf_op jit(solution)/shard_map/ppermute | solution.py:20
  23.3 2.5 %collective-permute-start.10 = (f32[28,8,128]{2,1,0:T(8,128)S(1)}, f32[28,8,128]{2,1,0:T(8,128)S(1)}, u32[]{:S(2)}, u32[]{:S(2)}) collective-permute-start(f32[28,8,128]{2,1,0:T(8,128)S(1)} %get-tuple-element.69), channel_id=1, source_target_pairs={{0,2},{1,3},{2,0},{3,1},{4,6},{5,7},{6,4},{7,5},{8,10},{9,11},{10,... | collective-permute-start | bytes 344072 | tf_op jit(solution)/shard_map/ppermute | solution.py:25
  25.8 1.9 %collective-permute-start.12 = (f32[28,8,128]{2,1,0:T(8,128)S(1)}, f32[28,8,128]{2,1,0:T(8,128)S(1)}, u32[]{:S(2)}, u32[]{:S(2)}) collective-permute-start(f32[28,8,128]{2,1,0:T(8,128)S(1)} %get-tuple-element.69), channel_id=1, source_target_pairs={{0,6},{1,7},{2,4},{3,5},{4,2},{5,3},{6,0},{7,1},{8,14},{9,15},{10,... | collective-permute-start | bytes 344072 | tf_op jit(solution)/shard_map/ppermute | solution.py:25
  27.6 0.9 %shard_map.40.refs_2_.refs_0_ = bf16[10,128,256]{2,1,0:T(8,128)(2,1)S(1)} custom-call(s32[2,4]{1,0:T(2,128)S(1)} %bitcast.15, bf16[6,128,256]{2,1,0:T(8,128)(2,1)S(1)} %shard_map.38.refs_1_, f32[4,14,8,128]{3,2,1,0:T(8,128)S(1)} %constant_dynamic-update-slice_fusion.refs_2_, f32[4,14,8,128]{3,2,1,0:T(8,128)S(1)} %collective-permute-done.8.refs_3_), custom_call_target="tpu_custom_call" | custom-call | flops 188743680 | bytes 1000000 | tf_op jit(solution)/shard_map/pallas_call | solution.py:187
  28.5 0.9 %shard_map.41 = (f32[256,128]{1,0:T(8,128)S(1)}, f32[256,128]{1,0:T(8,128)S(1)}) custom-call(s32[2,4]{1,0:T(2,128)S(1)} %bitcast.16, f32[256,128]{1,0:T(8,128)S(1)} %get-tuple-element.34.refs_0_, f32[256,128]{1,0:T(8,128)S(1)} %collective-permute-done.4.refs_1_, bf16[10,128,256]{2,1,0:T(8,128)(2,1)S(1)} %shard_map.40.refs_2_.refs_0_), custom_call_target="tpu_custom_call" | custom-call | flops 100663296 | bytes 2000000 | tf_op jit(solution)/shard_map/pallas_call | solution.py:248
  29.4 1.5 %collective-permute-start.9 = (f32[256,128]{1,0:T(8,128)S(1)}, f32[256,128]{1,0:T(8,128)S(1)}, u32[]{:S(2)}, u32[]{:S(2)}) collective-permute-start(f32[256,128]{1,0:T(8,128)S(1)} %get-tuple-element.42), channel_id=1, source_target_pairs={{0,8},{8,16},{16,24},{24,0},{1,9},{9,17},{17,25},{25,1},{2,10},{10... | collective-permute-start | bytes 393224 | tf_op jit(solution)/shard_map/ppermute | solution.py:20
  31.0 2.8 %collective-permute-done.11 = f32[28,8,128]{2,1,0:T(8,128)S(1)} collective-permute-done((f32[28,8,128]{2,1,0:T(8,128)S(1)}, f32[28,8,128]{2,1,0:T(8,128)S(1)}, u32[]{:S(2)}, u32[]{:S(2)}) %collective-permute-start.11) | collective-permute-done | bytes 114720 | tf_op jit(solution)/shard_map/ppermute | solution.py:25
  34.0 1.4 %collective-permute-done.9.refs_0_ = f32[256,128]{1,0:T(8,128)S(1)} collective-permute-done((f32[256,128]{1,0:T(8,128)S(1)}, f32[256,128]{1,0:T(8,128)S(1)}, u32[]{:S(2)}, u32[]{:S(2)}) %collective-permute-start.9) | collective-permute-done | bytes 131104 | tf_op jit(solution)/shard_map/ppermute | solution.py:20
  35.4 0.6 %collective-permute-start.15 = (f32[4,14,8,128]{3,2,1,0:T(8,128)S(1)}, f32[4,14,8,128]{3,2,1,0:T(8,128)S(1)}, u32[]{:S(2)}, u32[]{:S(2)}) collective-permute-start(f32[4,14,8,128]{3,2,1,0:T(8,128)S(1)} %pad_maximum_fusion.1.refs_2_), channel_id=1, source_target_pairs={{0,1},{1,0},{2,3},{3,2},{4,5},{5,4},{6,7},{7,6},{8,9},{9,8},{10,11... | collective-permute-start | bytes 688136 | tf_op jit(solution)/shard_map/ppermute | solution.py:25
  36.0 0.9 %collective-permute-done.13.refs_2_ = f32[4,14,8,128]{3,2,1,0:T(8,128)S(1)} collective-permute-done((f32[4,14,8,128]{3,2,1,0:T(8,128)S(1)}, f32[4,14,8,128]{3,2,1,0:T(8,128)S(1)}, u32[]{:S(2)}, u32[]{:S(2)}) %collective-permute-start.13) | collective-permute-done | bytes 229408 | tf_op jit(solution)/shard_map/ppermute | solution.py:25
  36.9 0.8 %shard_map.42.refs_2_.refs_1_ = bf16[10,128,256]{2,1,0:T(8,128)(2,1)S(1)} custom-call(bf16[10,128,256]{2,1,0:T(8,128)(2,1)S(1)} %shard_map.40.refs_2_.refs_0_, f32[4,14,8,128]{3,2,1,0:T(8,128)S(1)} %pad_maximum_fusion.refs_1_, f32[4,14,8,128]{3,2,1,0:T(8,128)S(1)} %collective-permute-done.13.refs_2_), custom_call_target="tpu_custom_call" | custom-call | flops 188743680 | bytes 1000000 | tf_op jit(solution)/shard_map/pallas_call | solution.py:187
  37.7 0.9 %shard_map.43 = (f32[256,128]{1,0:T(8,128)S(1)}, f32[256,128]{1,0:T(8,128)S(1)}) custom-call(s32[2,4]{1,0:T(2,128)S(1)} %bitcast.17, f32[256,128]{1,0:T(8,128)S(1)} %collective-permute-done.9.refs_0_, f32[256,128]{1,0:T(8,128)S(1)} %get-tuple-element.43.refs_1_, bf16[10,128,256]{2,1,0:T(8,128)(2,1)S(1)} %shard_map.42.refs_2_.refs_1_), custom_call_target="tpu_custom_call" | custom-call | flops 100663296 | bytes 2000000 | tf_op jit(solution)/shard_map/pallas_call | solution.py:248
  38.6 1.5 %collective-permute-start.17 = (f32[5,8,128]{2,1,0:T(8,128)S(1)}, f32[5,8,128]{2,1,0:T(8,128)S(1)}, u32[]{:S(2)}, u32[]{:S(2)}) collective-permute-start(f32[5,8,128]{2,1,0:T(8,128)S(1)} %get-tuple-element.57), channel_id=1, source_target_pairs={{0,2},{1,3},{2,0},{3,1},{4,6},{5,7},{6,4},{7,5},{8,10},{9,11},{10,... | collective-permute-start | bytes 61448 | tf_op jit(solution)/shard_map/ppermute | solution.py:25
  40.2 1.4 %collective-permute-start.14 = (f32[256,128]{1,0:T(8,128)S(1)}, f32[256,128]{1,0:T(8,128)S(1)}, u32[]{:S(2)}, u32[]{:S(2)}) collective-permute-start(f32[256,128]{1,0:T(8,128)S(1)} %get-tuple-element.52), channel_id=1, source_target_pairs={{0,24},{8,0},{16,8},{24,16},{1,25},{9,1},{17,9},{25,17},{2,26},{10... | collective-permute-start | bytes 393224 | tf_op jit(solution)/shard_map/ppermute | solution.py:20
  41.6 0.9 %collective-permute-done.17 = f32[5,8,128]{2,1,0:T(8,128)S(1)} collective-permute-done((f32[5,8,128]{2,1,0:T(8,128)S(1)}, f32[5,8,128]{2,1,0:T(8,128)S(1)}, u32[]{:S(2)}, u32[]{:S(2)}) %collective-permute-start.17) | collective-permute-done | bytes 20512 | tf_op jit(solution)/shard_map/ppermute | solution.py:25
  42.5 1.9 %collective-permute-start.18 = (f32[2,5,8,128]{3,2,1,0:T(8,128)S(1)}, f32[2,5,8,128]{3,2,1,0:T(8,128)S(1)}, u32[]{:S(2)}, u32[]{:S(2)}) collective-permute-start(f32[2,5,8,128]{3,2,1,0:T(8,128)S(1)} %pad_maximum_fusion.7), channel_id=1, source_target_pairs={{0,4},{1,5},{2,6},{3,7},{4,0},{5,1},{6,2},{7,3},{8,12},{9,13},{10,... | collective-permute-start | bytes 122888 | tf_op jit(solution)/shard_map/ppermute | solution.py:25
  44.4 0.9 %shard_map.44.refs_2_.refs_0_ = bf16[10,128,256]{2,1,0:T(8,128)(2,1)S(1)} custom-call(s32[2,4]{1,0:T(2,128)S(1)} %bitcast.18, bf16[10,128,256]{2,1,0:T(8,128)(2,1)S(1)} %shard_map.42.refs_2_.refs_1_, f32[4,14,8,128]{3,2,1,0:T(8,128)S(1)} %pad_maximum_fusion.1.refs_2_, f32[4,14,8,128]{3,2,1,0:T(8,128)S(1)} %collective-permute-done.15.refs_3_), custom_call_target="tpu_custom_call" | custom-call | flops 188743680 | bytes 1000000 | tf_op jit(solution)/shard_map/pallas_call | solution.py:187
  45.4 0.9 %shard_map.45 = (f32[256,128]{1,0:T(8,128)S(1)}, f32[256,128]{1,0:T(8,128)S(1)}) custom-call(s32[2,4]{1,0:T(2,128)S(1)} %bitcast.19, f32[256,128]{1,0:T(8,128)S(1)} %get-tuple-element.51.refs_0_, f32[256,128]{1,0:T(8,128)S(1)} %collective-permute-done.14.refs_1_, bf16[10,128,256]{2,1,0:T(8,128)(2,1)S(1)} %shard_map.44.refs_2_.refs_0_), custom_call_target="tpu_custom_call" | custom-call | flops 100663296 | bytes 2000000 | tf_op jit(solution)/shard_map/pallas_call | solution.py:248
  46.4 2.4 %collective-permute-start.16 = (f32[256,128]{1,0:T(8,128)S(1)}, f32[256,128]{1,0:T(8,128)S(1)}, u32[]{:S(2)}, u32[]{:S(2)}) collective-permute-start(f32[256,128]{1,0:T(8,128)S(1)} %get-tuple-element.54), channel_id=1, source_target_pairs={{0,8},{8,16},{16,24},{24,0},{1,9},{9,17},{17,25},{25,1},{2,10},{10... | collective-permute-start | bytes 393224 | tf_op jit(solution)/shard_map/ppermute | solution.py:20
  48.9 1.3 %collective-permute-done.19.refs_2_ = f32[4,5,8,128]{3,2,1,0:T(8,128)S(1)} collective-permute-done((f32[4,5,8,128]{3,2,1,0:T(8,128)S(1)}, f32[4,5,8,128]{3,2,1,0:T(8,128)S(1)}, u32[]{:S(2)}, u32[]{:S(2)}) %collective-permute-start.19) | collective-permute-done | bytes 81952 | tf_op jit(solution)/shard_map/ppermute | solution.py:25
  50.6 1.7 %collective-permute-done.16.refs_0_ = f32[256,128]{1,0:T(8,128)S(1)} collective-permute-done((f32[256,128]{1,0:T(8,128)S(1)}, f32[256,128]{1,0:T(8,128)S(1)}, u32[]{:S(2)}, u32[]{:S(2)}) %collective-permute-start.16) | collective-permute-done | bytes 131104 | tf_op jit(solution)/shard_map/ppermute | solution.py:20
  52.3 1.2 %shard_map.47 = f32[512,128]{1,0:T(8,128)} custom-call(s32[2,4]{1,0:T(2,128)S(1)} %bitcast.20, f32[256,128]{1,0:T(8,128)S(1)} %collective-permute-done.16.refs_0_, f32[256,128]{1,0:T(8,128)S(1)} %get-tuple-element.55.refs_1_, bf16[4,128,256]{2,1,0:T(8,128)(2,1)S(1)} %shard_map.46.refs_2_), custom_call_target="tpu_custom_call" | custom-call | flops 100663296 | bytes 2000000 | tf_op jit(solution)/shard_map/pallas_call | solution.py:248
  (38 shorter events, 2.6 us)
Async XLA Ops:
  0.0 0.9 %copy-start.1 = (f32[4,2,4,8,192]{4,3,2,1,0:T(8,128)S(1)}, f32[4,2,4,8,192]{4,3,2,1,0:T(8,128)}, u32[]{:S(2)}) copy-start(f32[4,2,4,8,192]{4,3,2,1,0:T(8,128)} %refl_ref.1) | copy-start | bytes 589828
  1.0 8.3 %collective-permute-start.5 = (f32[10,8,128]{2,1,0:T(8,128)S(1)}, f32[10,8,128]{2,1,0:T(8,128)S(1)}, u32[]{:S(2)}, u32[]{:S(2)}) collective-permute-start(f32[10,8,128]{2,1,0:T(8,128)S(1)} %get-tuple-element.37), channel_id=1, source_target_pairs={{0,24},{8,0},{16,8},{24,16},{1,25},{9,1},{17,9},{25,17},{2,26},{10... | collective-permute-start | bytes 122888 | tf_op jit(solution)/shard_map/ppermute | solution.py:20
  5.0 6.1 %collective-permute-start.2 = (f32[9,8,128]{2,1,0:T(8,128)S(1)}, f32[9,8,128]{2,1,0:T(8,128)S(1)}, u32[]{:S(2)}, u32[]{:S(2)}) collective-permute-start(f32[9,8,128]{2,1,0:T(8,128)S(1)} %get-tuple-element.33), channel_id=1, source_target_pairs={{0,6},{1,7},{2,4},{3,5},{4,2},{5,3},{6,0},{7,1},{8,14},{9,15},{10,... | collective-permute-start | bytes 110600 | tf_op jit(solution)/shard_map/ppermute | solution.py:25
  8.6 5.0 %collective-permute-start.1 = (f32[9,8,128]{2,1,0:T(8,128)S(1)}, f32[9,8,128]{2,1,0:T(8,128)S(1)}, u32[]{:S(2)}, u32[]{:S(2)}) collective-permute-start(f32[9,8,128]{2,1,0:T(8,128)S(1)} %get-tuple-element.33), channel_id=1, source_target_pairs={{0,4},{1,5},{2,6},{3,7},{4,0},{5,1},{6,2},{7,3},{8,12},{9,13},{10,... | collective-permute-start | bytes 110600 | tf_op jit(solution)/shard_map/ppermute | solution.py:25
  8.6 5.0 %collective-permute-start = (f32[9,8,128]{2,1,0:T(8,128)S(1)}, f32[9,8,128]{2,1,0:T(8,128)S(1)}, u32[]{:S(2)}, u32[]{:S(2)}) collective-permute-start(f32[9,8,128]{2,1,0:T(8,128)S(1)} %get-tuple-element.33), channel_id=1, source_target_pairs={{0,2},{1,3},{2,0},{3,1},{4,6},{5,7},{6,4},{7,5},{8,10},{9,11},{10,... | collective-permute-start | bytes 110600 | tf_op jit(solution)/shard_map/ppermute | solution.py:25
  9.4 4.6 %collective-permute-start.6 = (f32[14,8,128]{2,1,0:T(8,128)S(1)}, f32[14,8,128]{2,1,0:T(8,128)S(1)}, u32[]{:S(2)}, u32[]{:S(2)}) collective-permute-start(f32[14,8,128]{2,1,0:T(8,128)S(1)} %pad_maximum_fusion.6), channel_id=1, source_target_pairs={{0,2},{1,3},{2,0},{3,1},{4,6},{5,7},{6,4},{7,5},{8,10},{9,11},{10,... | collective-permute-start | bytes 172040 | tf_op jit(solution)/shard_map/ppermute | solution.py:25
  13.6 2.6 %collective-permute-start.3 = (f32[4,9,8,128]{3,2,1,0:T(8,128)S(1)}, f32[4,9,8,128]{3,2,1,0:T(8,128)S(1)}, u32[]{:S(2)}, u32[]{:S(2)}) collective-permute-start(f32[4,9,8,128]{3,2,1,0:T(8,128)S(1)} %pad_maximum_fusion.2.refs_0_), channel_id=1, source_target_pairs={{0,1},{1,0},{2,3},{3,2},{4,5},{5,4},{6,7},{7,6},{8,9},{9,8},{10,11... | collective-permute-start | bytes 442376 | tf_op jit(solution)/shard_map/ppermute | solution.py:25
  14.0 2.8 %copy-start = (f32[512,128]{1,0:T(8,128)S(1)}, f32[512,128]{1,0:T(8,128)}, u32[]{:S(2)}) copy-start(f32[512,128]{1,0:T(8,128)} %refs_0_.1) | copy-start | bytes 786436
  14.1 8.4 %collective-permute-start.7 = (f32[2,14,8,128]{3,2,1,0:T(8,128)S(1)}, f32[2,14,8,128]{3,2,1,0:T(8,128)S(1)}, u32[]{:S(2)}, u32[]{:S(2)}) collective-permute-start(f32[2,14,8,128]{3,2,1,0:T(8,128)S(1)} %pad_maximum_fusion.3), channel_id=1, source_target_pairs={{0,4},{1,5},{2,6},{3,7},{4,0},{5,1},{6,2},{7,3},{8,12},{9,13},{10,... | collective-permute-start | bytes 344072 | tf_op jit(solution)/shard_map/ppermute | solution.py:25
  16.8 0.7 %copy-start.2 = (s32[4,2]{0,1:T(2,128)S(1)}, s32[4,2]{0,1:T(2,128)}, u32[]{:S(2)}) copy-start(s32[4,2]{0,1:T(2,128)} %param.4) | copy-start | bytes 100
  22.5 5.1 %collective-permute-start.8 = (f32[4,14,8,128]{3,2,1,0:T(8,128)S(1)}, f32[4,14,8,128]{3,2,1,0:T(8,128)S(1)}, u32[]{:S(2)}, u32[]{:S(2)}) collective-permute-start(f32[4,14,8,128]{3,2,1,0:T(8,128)S(1)} %constant_dynamic-update-slice_fusion.refs_2_), channel_id=1, source_target_pairs={{0,1},{1,0},{2,3},{3,2},{4,5},{5,4},{6,7},{7,6},{8,9},{9,8},{10,11... | collective-permute-start | bytes 688136 | tf_op jit(solution)/shard_map/ppermute | solution.py:25
  22.6 5.9 %collective-permute-start.4 = (f32[256,128]{1,0:T(8,128)S(1)}, f32[256,128]{1,0:T(8,128)S(1)}, u32[]{:S(2)}, u32[]{:S(2)}) collective-permute-start(f32[256,128]{1,0:T(8,128)S(1)} %get-tuple-element.35), channel_id=1, source_target_pairs={{0,24},{8,0},{16,8},{24,16},{1,25},{9,1},{17,9},{25,17},{2,26},{10... | collective-permute-start | bytes 393224 | tf_op jit(solution)/shard_map/ppermute | solution.py:20
  23.2 10.6 %collective-permute-start.11 = (f32[28,8,128]{2,1,0:T(8,128)S(1)}, f32[28,8,128]{2,1,0:T(8,128)S(1)}, u32[]{:S(2)}, u32[]{:S(2)}) collective-permute-start(f32[28,8,128]{2,1,0:T(8,128)S(1)} %get-tuple-element.69), channel_id=1, source_target_pairs={{0,4},{1,5},{2,6},{3,7},{4,0},{5,1},{6,2},{7,3},{8,12},{9,13},{10,... | collective-permute-start | bytes 344072 | tf_op jit(solution)/shard_map/ppermute | solution.py:25
  23.3 10.6 %collective-permute-start.10 = (f32[28,8,128]{2,1,0:T(8,128)S(1)}, f32[28,8,128]{2,1,0:T(8,128)S(1)}, u32[]{:S(2)}, u32[]{:S(2)}) collective-permute-start(f32[28,8,128]{2,1,0:T(8,128)S(1)} %get-tuple-element.69), channel_id=1, source_target_pairs={{0,2},{1,3},{2,0},{3,1},{4,6},{5,7},{6,4},{7,5},{8,10},{9,11},{10,... | collective-permute-start | bytes 344072 | tf_op jit(solution)/shard_map/ppermute | solution.py:25
  25.8 8.1 %collective-permute-start.12 = (f32[28,8,128]{2,1,0:T(8,128)S(1)}, f32[28,8,128]{2,1,0:T(8,128)S(1)}, u32[]{:S(2)}, u32[]{:S(2)}) collective-permute-start(f32[28,8,128]{2,1,0:T(8,128)S(1)} %get-tuple-element.69), channel_id=1, source_target_pairs={{0,6},{1,7},{2,4},{3,5},{4,2},{5,3},{6,0},{7,1},{8,14},{9,15},{10,... | collective-permute-start | bytes 344072 | tf_op jit(solution)/shard_map/ppermute | solution.py:25
  29.4 6.0 %collective-permute-start.9 = (f32[256,128]{1,0:T(8,128)S(1)}, f32[256,128]{1,0:T(8,128)S(1)}, u32[]{:S(2)}, u32[]{:S(2)}) collective-permute-start(f32[256,128]{1,0:T(8,128)S(1)} %get-tuple-element.42), channel_id=1, source_target_pairs={{0,8},{8,16},{16,24},{24,0},{1,9},{9,17},{17,25},{25,1},{2,10},{10... | collective-permute-start | bytes 393224 | tf_op jit(solution)/shard_map/ppermute | solution.py:20
  35.4 1.5 %collective-permute-start.13 = (f32[4,14,8,128]{3,2,1,0:T(8,128)S(1)}, f32[4,14,8,128]{3,2,1,0:T(8,128)S(1)}, u32[]{:S(2)}, u32[]{:S(2)}) collective-permute-start(f32[4,14,8,128]{3,2,1,0:T(8,128)S(1)} %pad_maximum_fusion.refs_1_), channel_id=1, source_target_pairs={{0,1},{1,0},{2,3},{3,2},{4,5},{5,4},{6,7},{7,6},{8,9},{9,8},{10,11... | collective-permute-start | bytes 688136 | tf_op jit(solution)/shard_map/ppermute | solution.py:25
  35.4 9.0 %collective-permute-start.15 = (f32[4,14,8,128]{3,2,1,0:T(8,128)S(1)}, f32[4,14,8,128]{3,2,1,0:T(8,128)S(1)}, u32[]{:S(2)}, u32[]{:S(2)}) collective-permute-start(f32[4,14,8,128]{3,2,1,0:T(8,128)S(1)} %pad_maximum_fusion.1.refs_2_), channel_id=1, source_target_pairs={{0,1},{1,0},{2,3},{3,2},{4,5},{5,4},{6,7},{7,6},{8,9},{9,8},{10,11... | collective-permute-start | bytes 688136 | tf_op jit(solution)/shard_map/ppermute | solution.py:25
  38.6 3.8 %collective-permute-start.17 = (f32[5,8,128]{2,1,0:T(8,128)S(1)}, f32[5,8,128]{2,1,0:T(8,128)S(1)}, u32[]{:S(2)}, u32[]{:S(2)}) collective-permute-start(f32[5,8,128]{2,1,0:T(8,128)S(1)} %get-tuple-element.57), channel_id=1, source_target_pairs={{0,2},{1,3},{2,0},{3,1},{4,6},{5,7},{6,4},{7,5},{8,10},{9,11},{10,... | collective-permute-start | bytes 61448 | tf_op jit(solution)/shard_map/ppermute | solution.py:25
  40.2 5.3 %collective-permute-start.14 = (f32[256,128]{1,0:T(8,128)S(1)}, f32[256,128]{1,0:T(8,128)S(1)}, u32[]{:S(2)}, u32[]{:S(2)}) collective-permute-start(f32[256,128]{1,0:T(8,128)S(1)} %get-tuple-element.52), channel_id=1, source_target_pairs={{0,24},{8,0},{16,8},{24,16},{1,25},{9,1},{17,9},{25,17},{2,26},{10... | collective-permute-start | bytes 393224 | tf_op jit(solution)/shard_map/ppermute | solution.py:20
  42.5 6.3 %collective-permute-start.18 = (f32[2,5,8,128]{3,2,1,0:T(8,128)S(1)}, f32[2,5,8,128]{3,2,1,0:T(8,128)S(1)}, u32[]{:S(2)}, u32[]{:S(2)}) collective-permute-start(f32[2,5,8,128]{3,2,1,0:T(8,128)S(1)} %pad_maximum_fusion.7), channel_id=1, source_target_pairs={{0,4},{1,5},{2,6},{3,7},{4,0},{5,1},{6,2},{7,3},{8,12},{9,13},{10,... | collective-permute-start | bytes 122888 | tf_op jit(solution)/shard_map/ppermute | solution.py:25
  46.4 5.9 %collective-permute-start.16 = (f32[256,128]{1,0:T(8,128)S(1)}, f32[256,128]{1,0:T(8,128)S(1)}, u32[]{:S(2)}, u32[]{:S(2)}) collective-permute-start(f32[256,128]{1,0:T(8,128)S(1)} %get-tuple-element.54), channel_id=1, source_target_pairs={{0,8},{8,16},{16,24},{24,0},{1,9},{9,17},{17,25},{25,1},{2,10},{10... | collective-permute-start | bytes 393224 | tf_op jit(solution)/shard_map/ppermute | solution.py:20
  48.8 1.3 %collective-permute-start.19 = (f32[4,5,8,128]{3,2,1,0:T(8,128)S(1)}, f32[4,5,8,128]{3,2,1,0:T(8,128)S(1)}, u32[]{:S(2)}, u32[]{:S(2)}) collective-permute-start(f32[4,5,8,128]{3,2,1,0:T(8,128)S(1)} %pad_maximum_fusion.5.refs_1_), channel_id=1, source_target_pairs={{0,1},{1,0},{2,3},{3,2},{4,5},{5,4},{6,7},{7,6},{8,9},{9,8},{10,11... | collective-permute-start | bytes 245768 | tf_op jit(solution)/shard_map/ppermute | solution.py:25

commit v5 on v1

--- a/solution.py
+++ b/solution.py
@@ -10,7 +10,7 @@
 WINDOW = 128
 HALF = 2 * WINDOW
 CORES = 2
-STAGE = 3
+STAGE = 5
 VMEM_LIMIT = 24 * 1024 * 1024
 VMEM = pl.BlockSpec(memory_space=pltpu.VMEM)
 

time: 52.7 us -> 52.6 us (level)
  transfers between devices with their start and end apart: 17 -> 17, of which waited for: 9 -> 10; matrix products, arithmetic and copies ran while one was open for 0% -> 0% of each run, Pallas kernels for 11% -> 11%
where the time goes in v5:
time: 52.6 us; the launch traced here: 52.2 us
  starting transfers between devices  23 us (44%)
  waiting for transfers between devices  19.5 us (37%)
  Pallas kernels  7.73 us (15%)
  local copies, waits for them, and re-layouts  1.69 us (3%)
    ppermute x12, starting transfers between devices, swapped(): return lax.ppermute(value, 'col', [(i, i ^ bit) for i in range(devices)])  13 us
    ppermute x12, waiting for transfers between devices, swapped(): return lax.ppermute(value, 'col', [(i, i ^ bit) for i in range(devices)])  13 us
    ppermute x5, starting transfers between devices, shifted(): lax.ppermute(value, axis, [(i, (i + by) % devices) for i in range(devices)])  9.91 us
    ppermute x5, waiting for transfers between devices, shifted(): lax.ppermute(value, axis, [(i, (i + by) % devices) for i in range(devices)])  6.49 us
    pallas_call x5, Pallas kernels, phase(): pl.pallas_call(functools.partial(phase_kernel, ph, rounds, nwin, len(part...  4.45 us
    pallas_call x5, Pallas kernels, matrices(): pl.pallas_call(functools.partial(matrix_kernel, plan, ph, masked), out_sh...  3.19 us
    unnamed x7, local copies, waits for them, and re-layouts  1.63 us
  transfers between devices with their start and end apart: 17, of which 10 were waited for; matrix products, arithmetic and copies ran while one was open for 0% of the time, Pallas kernels for 11%

profile of v5, /device:TPU:0, one launch (start us, length us, event | category | flops | bytes accessed | tf_op | source)
XLA Modules:
  0.0 52.2 jit_solution(9882706056640871147)
XLA Ops:
  0.0 0.9 %copy-done.1 = f32[4,2,4,8,192]{4,3,2,1,0:T(8,128)S(1)} copy-done((f32[4,2,4,8,192]{4,3,2,1,0:T(8,128)S(1)}, f32[4,2,4,8,192]{4,3,2,1,0:T(8,128)}, u32[]{:S(2)}) %copy-start.1) | copy-done | bytes 196632
  1.0 3.9 %collective-permute-start.5 = (f32[10,8,128]{2,1,0:T(8,128)S(1)}, f32[10,8,128]{2,1,0:T(8,128)S(1)}, u32[]{:S(2)}, u32[]{:S(2)}) collective-permute-start(f32[10,8,128]{2,1,0:T(8,128)S(1)} %get-tuple-element.32), channel_id=1, source_target_pairs={{0,24},{8,0},{16,8},{24,16},{1,25},{9,1},{17,9},{25,17},{2,26},{10... | collective-permute-start | bytes 122888 | tf_op jit(solution)/shard_map/ppermute | solution.py:20
  5.0 3.6 %collective-permute-start.2 = (f32[9,8,128]{2,1,0:T(8,128)S(1)}, f32[9,8,128]{2,1,0:T(8,128)S(1)}, u32[]{:S(2)}, u32[]{:S(2)}) collective-permute-start(f32[9,8,128]{2,1,0:T(8,128)S(1)} %get-tuple-element.28), channel_id=1, source_target_pairs={{0,6},{1,7},{2,4},{3,5},{4,2},{5,3},{6,0},{7,1},{8,14},{9,15},{10,... | collective-permute-start | bytes 110600 | tf_op jit(solution)/shard_map/ppermute | solution.py:25
  8.6 0.8 %collective-permute-start = (f32[9,8,128]{2,1,0:T(8,128)S(1)}, f32[9,8,128]{2,1,0:T(8,128)S(1)}, u32[]{:S(2)}, u32[]{:S(2)}) collective-permute-start(f32[9,8,128]{2,1,0:T(8,128)S(1)} %get-tuple-element.28), channel_id=1, source_target_pairs={{0,2},{1,3},{2,0},{3,1},{4,6},{5,7},{6,4},{7,5},{8,10},{9,11},{10,... | collective-permute-start | bytes 110600 | tf_op jit(solution)/shard_map/ppermute | solution.py:25
  9.4 1.3 %collective-permute-start.6 = (f32[14,8,128]{2,1,0:T(8,128)S(1)}, f32[14,8,128]{2,1,0:T(8,128)S(1)}, u32[]{:S(2)}, u32[]{:S(2)}) collective-permute-start(f32[14,8,128]{2,1,0:T(8,128)S(1)} %pad_maximum_fusion.5), channel_id=1, source_target_pairs={{0,2},{1,3},{2,0},{3,1},{4,6},{5,7},{6,4},{7,5},{8,10},{9,11},{10,... | collective-permute-start | bytes 172040 | tf_op jit(solution)/shard_map/ppermute | solution.py:25
  10.7 0.4 collective-permute-done.2
  11.1 2.4 %collective-permute-done.1 = f32[9,8,128]{2,1,0:T(8,128)S(1)} collective-permute-done((f32[9,8,128]{2,1,0:T(8,128)S(1)}, f32[9,8,128]{2,1,0:T(8,128)S(1)}, u32[]{:S(2)}, u32[]{:S(2)}) %collective-permute-start.1) | collective-permute-done | bytes 36896 | tf_op jit(solution)/shard_map/ppermute | solution.py:25
  14.1 2.1 %collective-permute-start.7 = (f32[2,14,8,128]{3,2,1,0:T(8,128)S(1)}, f32[2,14,8,128]{3,2,1,0:T(8,128)S(1)}, u32[]{:S(2)}, u32[]{:S(2)}) collective-permute-start(f32[2,14,8,128]{3,2,1,0:T(8,128)S(1)} %pad_maximum_fusion.4), channel_id=1, source_target_pairs={{0,4},{1,5},{2,6},{3,7},{4,0},{5,1},{6,2},{7,3},{8,12},{9,13},{10,... | collective-permute-start | bytes 344072 | tf_op jit(solution)/shard_map/ppermute | solution.py:25
  16.2 0.6 %shard_map.38.refs_1_ = bf16[6,128,256]{2,1,0:T(8,128)(2,1)S(1)} custom-call(f32[4,9,8,128]{3,2,1,0:T(8,128)S(1)} %pad_maximum_fusion.2.refs_0_, f32[4,9,8,128]{3,2,1,0:T(8,128)S(1)} %collective-permute-done.3.refs_1_), custom_call_target="tpu_custom_call" | custom-call | flops 113246208 | bytes 600000 | tf_op jit(solution)/shard_map/pallas_call | solution.py:187
  16.8 0.7 %copy-done.2 = s32[4,2]{0,1:T(2,128)S(1)} copy-done((s32[4,2]{0,1:T(2,128)S(1)}, s32[4,2]{0,1:T(2,128)}, u32[]{:S(2)}) %copy-start.2) | copy-done | bytes 56
  17.5 0.5 shard_map.39
  18.0 4.5 %collective-permute-done.7 = f32[2,14,8,128]{3,2,1,0:T(8,128)S(1)} collective-permute-done((f32[2,14,8,128]{3,2,1,0:T(8,128)S(1)}, f32[2,14,8,128]{3,2,1,0:T(8,128)S(1)}, u32[]{:S(2)}, u32[]{:S(2)}) %collective-permute-start.7) | collective-permute-done | bytes 114720 | tf_op jit(solution)/shard_map/ppermute | solution.py:25
  22.6 0.6 %collective-permute-start.4 = (f32[256,128]{1,0:T(8,128)S(1)}, f32[256,128]{1,0:T(8,128)S(1)}, u32[]{:S(2)}, u32[]{:S(2)}) collective-permute-start(f32[256,128]{1,0:T(8,128)S(1)} %get-tuple-element.30), channel_id=1, source_target_pairs={{0,24},{8,0},{16,8},{24,16},{1,25},{9,1},{17,9},{25,17},{2,26},{10... | collective-permute-start | bytes 393224 | tf_op jit(solution)/shard_map/ppermute | solution.py:20
  23.3 2.5 %collective-permute-start.10 = (f32[33,8,128]{2,1,0:T(8,128)S(1)}, f32[33,8,128]{2,1,0:T(8,128)S(1)}, u32[]{:S(2)}, u32[]{:S(2)}) collective-permute-start(f32[33,8,128]{2,1,0:T(8,128)S(1)} %get-tuple-element.51), channel_id=1, source_target_pairs={{0,2},{1,3},{2,0},{3,1},{4,6},{5,7},{6,4},{7,5},{8,10},{9,11},{10,... | collective-permute-start | bytes 405512 | tf_op jit(solution)/shard_map/ppermute | solution.py:25
  25.8 1.9 %collective-permute-start.12 = (f32[33,8,128]{2,1,0:T(8,128)S(1)}, f32[33,8,128]{2,1,0:T(8,128)S(1)}, u32[]{:S(2)}, u32[]{:S(2)}) collective-permute-start(f32[33,8,128]{2,1,0:T(8,128)S(1)} %get-tuple-element.51), channel_id=1, source_target_pairs={{0,6},{1,7},{2,4},{3,5},{4,2},{5,3},{6,0},{7,1},{8,14},{9,15},{10,... | collective-permute-start | bytes 405512 | tf_op jit(solution)/shard_map/ppermute | solution.py:25
  27.7 0.7 %shard_map.40.refs_2_.refs_0_ = bf16[10,128,256]{2,1,0:T(8,128)(2,1)S(1)} custom-call(s32[2,4]{1,0:T(2,128)S(1)} %bitcast.13, bf16[6,128,256]{2,1,0:T(8,128)(2,1)S(1)} %shard_map.38.refs_1_, f32[4,14,8,128]{3,2,1,0:T(8,128)S(1)} %constant_dynamic-update-slice_fusion.refs_2_, f32[4,14,8,128]{3,2,1,0:T(8,128)S(1)} %collective-permute-done.8.refs_3_), custom_call_target="tpu_custom_call" | custom-call | flops 188743680 | bytes 1000000 | tf_op jit(solution)/shard_map/pallas_call | solution.py:187
  28.5 0.9 %shard_map.41 = (f32[256,128]{1,0:T(8,128)S(1)}, f32[256,128]{1,0:T(8,128)S(1)}) custom-call(s32[2,4]{1,0:T(2,128)S(1)} %bitcast.14, f32[256,128]{1,0:T(8,128)S(1)} %get-tuple-element.29.refs_0_, f32[256,128]{1,0:T(8,128)S(1)} %collective-permute-done.4.refs_1_, bf16[10,128,256]{2,1,0:T(8,128)(2,1)S(1)} %shard_map.40.refs_2_.refs_0_), custom_call_target="tpu_custom_call" | custom-call | flops 100663296 | bytes 2000000 | tf_op jit(solution)/shard_map/pallas_call | solution.py:248
  29.4 1.5 %collective-permute-start.9 = (f32[256,128]{1,0:T(8,128)S(1)}, f32[256,128]{1,0:T(8,128)S(1)}, u32[]{:S(2)}, u32[]{:S(2)}) collective-permute-start(f32[256,128]{1,0:T(8,128)S(1)} %get-tuple-element.37), channel_id=1, source_target_pairs={{0,8},{8,16},{16,24},{24,0},{1,9},{9,17},{17,25},{25,1},{2,10},{10... | collective-permute-start | bytes 393224 | tf_op jit(solution)/shard_map/ppermute | solution.py:20
  30.8 1.8 %collective-permute-done.11 = f32[33,8,128]{2,1,0:T(8,128)S(1)} collective-permute-done((f32[33,8,128]{2,1,0:T(8,128)S(1)}, f32[33,8,128]{2,1,0:T(8,128)S(1)}, u32[]{:S(2)}, u32[]{:S(2)}) %collective-permute-start.11) | collective-permute-done | bytes 135200 | tf_op jit(solution)/shard_map/ppermute | solution.py:25
  32.6 2.6 %collective-permute-done.10 = f32[33,8,128]{2,1,0:T(8,128)S(1)} collective-permute-done((f32[33,8,128]{2,1,0:T(8,128)S(1)}, f32[33,8,128]{2,1,0:T(8,128)S(1)}, u32[]{:S(2)}, u32[]{:S(2)}) %collective-permute-start.10) | collective-permute-done | bytes 135200 | tf_op jit(solution)/shard_map/ppermute | solution.py:25
  35.5 0.6 %collective-permute-start.15 = (f32[4,19,8,128]{3,2,1,0:T(8,128)S(1)}, f32[4,19,8,128]{3,2,1,0:T(8,128)S(1)}, u32[]{:S(2)}, u32[]{:S(2)}) collective-permute-start(f32[4,19,8,128]{3,2,1,0:T(8,128)S(1)} %pad_maximum_fusion.refs_2_.refs_1_), channel_id=1, source_target_pairs={{0,1},{1,0},{2,3},{3,2},{4,5},{5,4},{6,7},{7,6},{8,9},{9,8},{10,11... | collective-permute-start | bytes 933896 | tf_op jit(solution)/shard_map/ppermute | solution.py:25
  36.0 0.9 %collective-permute-done.13.refs_2_ = f32[4,14,8,128]{3,2,1,0:T(8,128)S(1)} collective-permute-done((f32[4,14,8,128]{3,2,1,0:T(8,128)S(1)}, f32[4,14,8,128]{3,2,1,0:T(8,128)S(1)}, u32[]{:S(2)}, u32[]{:S(2)}) %collective-permute-start.13) | collective-permute-done | bytes 229408 | tf_op jit(solution)/shard_map/ppermute | solution.py:25
  36.9 0.7 %shard_map.42.refs_2_.refs_1_ = bf16[10,128,256]{2,1,0:T(8,128)(2,1)S(1)} custom-call(bf16[10,128,256]{2,1,0:T(8,128)(2,1)S(1)} %shard_map.40.refs_2_.refs_0_, f32[4,14,8,128]{3,2,1,0:T(8,128)S(1)} %pad_maximum_fusion.1.refs_1_, f32[4,14,8,128]{3,2,1,0:T(8,128)S(1)} %collective-permute-done.13.refs_2_), custom_call_target="tpu_custom_call" | custom-call | flops 188743680 | bytes 1000000 | tf_op jit(solution)/shard_map/pallas_call | solution.py:187
  37.6 0.9 %shard_map.43 = (f32[256,128]{1,0:T(8,128)S(1)}, f32[256,128]{1,0:T(8,128)S(1)}) custom-call(s32[2,4]{1,0:T(2,128)S(1)} %bitcast.15, f32[256,128]{1,0:T(8,128)S(1)} %collective-permute-done.9.refs_0_, f32[256,128]{1,0:T(8,128)S(1)} %get-tuple-element.38.refs_1_, bf16[10,128,256]{2,1,0:T(8,128)(2,1)S(1)} %shard_map.42.refs_2_.refs_1_), custom_call_target="tpu_custom_call" | custom-call | flops 100663296 | bytes 2000000 | tf_op jit(solution)/shard_map/pallas_call | solution.py:248
  38.5 1.5 %collective-permute-start.14 = (f32[256,128]{1,0:T(8,128)S(1)}, f32[256,128]{1,0:T(8,128)S(1)}, u32[]{:S(2)}, u32[]{:S(2)}) collective-permute-start(f32[256,128]{1,0:T(8,128)S(1)} %get-tuple-element.47), channel_id=1, source_target_pairs={{0,24},{8,0},{16,8},{24,16},{1,25},{9,1},{17,9},{25,17},{2,26},{10... | collective-permute-start | bytes 393224 | tf_op jit(solution)/shard_map/ppermute | solution.py:20
  40.0 0.8 %shard_map.44.refs_2_.refs_0_ = bf16[10,128,256]{2,1,0:T(8,128)(2,1)S(1)} custom-call(s32[2,4]{1,0:T(2,128)S(1)} %bitcast.16, bf16[10,128,256]{2,1,0:T(8,128)(2,1)S(1)} %shard_map.42.refs_2_.refs_1_, f32[4,19,8,128]{3,2,1,0:T(8,128)S(1)} %pad_maximum_fusion.refs_2_.refs_1_, f32[4,19,8,128]{3,2,1,0:T(8,128)S(1)} %collective-permute-done.15.refs_3_.refs_2_), custom_call_target="tpu_custom_call" | custom-call | flops 188743680 | bytes 1000000 | tf_op jit(solution)/shard_map/pallas_call | solution.py:187
  40.8 3.3 %collective-permute-done.14.refs_1_ = f32[256,128]{1,0:T(8,128)S(1)} collective-permute-done((f32[256,128]{1,0:T(8,128)S(1)}, f32[256,128]{1,0:T(8,128)S(1)}, u32[]{:S(2)}, u32[]{:S(2)}) %collective-permute-start.14) | collective-permute-done | bytes 131104 | tf_op jit(solution)/shard_map/ppermute | solution.py:20
  44.1 0.9 %shard_map.45 = (f32[256,128]{1,0:T(8,128)S(1)}, f32[256,128]{1,0:T(8,128)S(1)}) custom-call(s32[2,4]{1,0:T(2,128)S(1)} %bitcast.17, f32[256,128]{1,0:T(8,128)S(1)} %get-tuple-element.46.refs_0_, f32[256,128]{1,0:T(8,128)S(1)} %collective-permute-done.14.refs_1_, bf16[10,128,256]{2,1,0:T(8,128)(2,1)S(1)} %shard_map.44.refs_2_.refs_0_), custom_call_target="tpu_custom_call" | custom-call | flops 100663296 | bytes 2000000 | tf_op jit(solution)/shard_map/pallas_call | solution.py:248
  45.1 2.5 %collective-permute-start.16 = (f32[256,128]{1,0:T(8,128)S(1)}, f32[256,128]{1,0:T(8,128)S(1)}, u32[]{:S(2)}, u32[]{:S(2)}) collective-permute-start(f32[256,128]{1,0:T(8,128)S(1)} %get-tuple-element.49), channel_id=1, source_target_pairs={{0,8},{8,16},{16,24},{24,0},{1,9},{9,17},{17,25},{25,1},{2,10},{10... | collective-permute-start | bytes 393224 | tf_op jit(solution)/shard_map/ppermute | solution.py:20
  47.5 0.4 shard_map.46.refs_2_
  47.9 3.0 %collective-permute-done.16.refs_0_ = f32[256,128]{1,0:T(8,128)S(1)} collective-permute-done((f32[256,128]{1,0:T(8,128)S(1)}, f32[256,128]{1,0:T(8,128)S(1)}, u32[]{:S(2)}, u32[]{:S(2)}) %collective-permute-start.16) | collective-permute-done | bytes 131104 | tf_op jit(solution)/shard_map/ppermute | solution.py:20
  51.0 1.2 %shard_map.47 = f32[512,128]{1,0:T(8,128)} custom-call(s32[2,4]{1,0:T(2,128)S(1)} %bitcast.18, f32[256,128]{1,0:T(8,128)S(1)} %collective-permute-done.16.refs_0_, f32[256,128]{1,0:T(8,128)S(1)} %get-tuple-element.50.refs_1_, bf16[4,128,256]{2,1,0:T(8,128)(2,1)S(1)} %shard_map.46.refs_2_), custom_call_target="tpu_custom_call" | custom-call | flops 100663296 | bytes 2000000 | tf_op jit(solution)/shard_map/pallas_call | solution.py:248
  (36 shorter events, 1.1 us)
Async XLA Ops:
  0.0 0.9 %copy-start.1 = (f32[4,2,4,8,192]{4,3,2,1,0:T(8,128)S(1)}, f32[4,2,4,8,192]{4,3,2,1,0:T(8,128)}, u32[]{:S(2)}) copy-start(f32[4,2,4,8,192]{4,3,2,1,0:T(8,128)} %refl_ref.1) | copy-start | bytes 589828
  1.0 8.3 %collective-permute-start.5 = (f32[10,8,128]{2,1,0:T(8,128)S(1)}, f32[10,8,128]{2,1,0:T(8,128)S(1)}, u32[]{:S(2)}, u32[]{:S(2)}) collective-permute-start(f32[10,8,128]{2,1,0:T(8,128)S(1)} %get-tuple-element.32), channel_id=1, source_target_pairs={{0,24},{8,0},{16,8},{24,16},{1,25},{9,1},{17,9},{25,17},{2,26},{10... | collective-permute-start | bytes 122888 | tf_op jit(solution)/shard_map/ppermute | solution.py:20
  5.0 6.1 %collective-permute-start.2 = (f32[9,8,128]{2,1,0:T(8,128)S(1)}, f32[9,8,128]{2,1,0:T(8,128)S(1)}, u32[]{:S(2)}, u32[]{:S(2)}) collective-permute-start(f32[9,8,128]{2,1,0:T(8,128)S(1)} %get-tuple-element.28), channel_id=1, source_target_pairs={{0,6},{1,7},{2,4},{3,5},{4,2},{5,3},{6,0},{7,1},{8,14},{9,15},{10,... | collective-permute-start | bytes 110600 | tf_op jit(solution)/shard_map/ppermute | solution.py:25
  8.6 5.0 %collective-permute-start.1 = (f32[9,8,128]{2,1,0:T(8,128)S(1)}, f32[9,8,128]{2,1,0:T(8,128)S(1)}, u32[]{:S(2)}, u32[]{:S(2)}) collective-permute-start(f32[9,8,128]{2,1,0:T(8,128)S(1)} %get-tuple-element.28), channel_id=1, source_target_pairs={{0,4},{1,5},{2,6},{3,7},{4,0},{5,1},{6,2},{7,3},{8,12},{9,13},{10,... | collective-permute-start | bytes 110600 | tf_op jit(solution)/shard_map/ppermute | solution.py:25
  8.6 5.0 %collective-permute-start = (f32[9,8,128]{2,1,0:T(8,128)S(1)}, f32[9,8,128]{2,1,0:T(8,128)S(1)}, u32[]{:S(2)}, u32[]{:S(2)}) collective-permute-start(f32[9,8,128]{2,1,0:T(8,128)S(1)} %get-tuple-element.28), channel_id=1, source_target_pairs={{0,2},{1,3},{2,0},{3,1},{4,6},{5,7},{6,4},{7,5},{8,10},{9,11},{10,... | collective-permute-start | bytes 110600 | tf_op jit(solution)/shard_map/ppermute | solution.py:25
  9.4 4.6 %collective-permute-start.6 = (f32[14,8,128]{2,1,0:T(8,128)S(1)}, f32[14,8,128]{2,1,0:T(8,128)S(1)}, u32[]{:S(2)}, u32[]{:S(2)}) collective-permute-start(f32[14,8,128]{2,1,0:T(8,128)S(1)} %pad_maximum_fusion.5), channel_id=1, source_target_pairs={{0,2},{1,3},{2,0},{3,1},{4,6},{5,7},{6,4},{7,5},{8,10},{9,11},{10,... | collective-permute-start | bytes 172040 | tf_op jit(solution)/shard_map/ppermute | solution.py:25
  13.6 2.6 %collective-permute-start.3 = (f32[4,9,8,128]{3,2,1,0:T(8,128)S(1)}, f32[4,9,8,128]{3,2,1,0:T(8,128)S(1)}, u32[]{:S(2)}, u32[]{:S(2)}) collective-permute-start(f32[4,9,8,128]{3,2,1,0:T(8,128)S(1)} %pad_maximum_fusion.2.refs_0_), channel_id=1, source_target_pairs={{0,1},{1,0},{2,3},{3,2},{4,5},{5,4},{6,7},{7,6},{8,9},{9,8},{10,11... | collective-permute-start | bytes 442376 | tf_op jit(solution)/shard_map/ppermute | solution.py:25
  14.0 2.8 %copy-start = (f32[512,128]{1,0:T(8,128)S(1)}, f32[512,128]{1,0:T(8,128)}, u32[]{:S(2)}) copy-start(f32[512,128]{1,0:T(8,128)} %refs_0_.1) | copy-start | bytes 786436
  14.1 8.4 %collective-permute-start.7 = (f32[2,14,8,128]{3,2,1,0:T(8,128)S(1)}, f32[2,14,8,128]{3,2,1,0:T(8,128)S(1)}, u32[]{:S(2)}, u32[]{:S(2)}) collective-permute-start(f32[2,14,8,128]{3,2,1,0:T(8,128)S(1)} %pad_maximum_fusion.4), channel_id=1, source_target_pairs={{0,4},{1,5},{2,6},{3,7},{4,0},{5,1},{6,2},{7,3},{8,12},{9,13},{10,... | collective-permute-start | bytes 344072 | tf_op jit(solution)/shard_map/ppermute | solution.py:25
  16.8 0.7 %copy-start.2 = (s32[4,2]{0,1:T(2,128)S(1)}, s32[4,2]{0,1:T(2,128)}, u32[]{:S(2)}) copy-start(s32[4,2]{0,1:T(2,128)} %param.4) | copy-start | bytes 100
  22.5 5.1 %collective-permute-start.8 = (f32[4,14,8,128]{3,2,1,0:T(8,128)S(1)}, f32[4,14,8,128]{3,2,1,0:T(8,128)S(1)}, u32[]{:S(2)}, u32[]{:S(2)}) collective-permute-start(f32[4,14,8,128]{3,2,1,0:T(8,128)S(1)} %constant_dynamic-update-slice_fusion.refs_2_), channel_id=1, source_target_pairs={{0,1},{1,0},{2,3},{3,2},{4,5},{5,4},{6,7},{7,6},{8,9},{9,8},{10,11... | collective-permute-start | bytes 688136 | tf_op jit(solution)/shard_map/ppermute | solution.py:25
  22.6 5.9 %collective-permute-start.4 = (f32[256,128]{1,0:T(8,128)S(1)}, f32[256,128]{1,0:T(8,128)S(1)}, u32[]{:S(2)}, u32[]{:S(2)}) collective-permute-start(f32[256,128]{1,0:T(8,128)S(1)} %get-tuple-element.30), channel_id=1, source_target_pairs={{0,24},{8,0},{16,8},{24,16},{1,25},{9,1},{17,9},{25,17},{2,26},{10... | collective-permute-start | bytes 393224 | tf_op jit(solution)/shard_map/ppermute | solution.py:20
  23.2 9.4 %collective-permute-start.11 = (f32[33,8,128]{2,1,0:T(8,128)S(1)}, f32[33,8,128]{2,1,0:T(8,128)S(1)}, u32[]{:S(2)}, u32[]{:S(2)}) collective-permute-start(f32[33,8,128]{2,1,0:T(8,128)S(1)} %get-tuple-element.51), channel_id=1, source_target_pairs={{0,4},{1,5},{2,6},{3,7},{4,0},{5,1},{6,2},{7,3},{8,12},{9,13},{10,... | collective-permute-start | bytes 405512 | tf_op jit(solution)/shard_map/ppermute | solution.py:25
  23.3 11.9 %collective-permute-start.10 = (f32[33,8,128]{2,1,0:T(8,128)S(1)}, f32[33,8,128]{2,1,0:T(8,128)S(1)}, u32[]{:S(2)}, u32[]{:S(2)}) collective-permute-start(f32[33,8,128]{2,1,0:T(8,128)S(1)} %get-tuple-element.51), channel_id=1, source_target_pairs={{0,2},{1,3},{2,0},{3,1},{4,6},{5,7},{6,4},{7,5},{8,10},{9,11},{10,... | collective-permute-start | bytes 405512 | tf_op jit(solution)/shard_map/ppermute | solution.py:25
  25.8 9.4 %collective-permute-start.12 = (f32[33,8,128]{2,1,0:T(8,128)S(1)}, f32[33,8,128]{2,1,0:T(8,128)S(1)}, u32[]{:S(2)}, u32[]{:S(2)}) collective-permute-start(f32[33,8,128]{2,1,0:T(8,128)S(1)} %get-tuple-element.51), channel_id=1, source_target_pairs={{0,6},{1,7},{2,4},{3,5},{4,2},{5,3},{6,0},{7,1},{8,14},{9,15},{10,... | collective-permute-start | bytes 405512 | tf_op jit(solution)/shard_map/ppermute | solution.py:25
  29.4 6.0 %collective-permute-start.9 = (f32[256,128]{1,0:T(8,128)S(1)}, f32[256,128]{1,0:T(8,128)S(1)}, u32[]{:S(2)}, u32[]{:S(2)}) collective-permute-start(f32[256,128]{1,0:T(8,128)S(1)} %get-tuple-element.37), channel_id=1, source_target_pairs={{0,8},{8,16},{16,24},{24,0},{1,9},{9,17},{17,25},{25,1},{2,10},{10... | collective-permute-start | bytes 393224 | tf_op jit(solution)/shard_map/ppermute | solution.py:20
  35.4 1.5 %collective-permute-start.13 = (f32[4,14,8,128]{3,2,1,0:T(8,128)S(1)}, f32[4,14,8,128]{3,2,1,0:T(8,128)S(1)}, u32[]{:S(2)}, u32[]{:S(2)}) collective-permute-start(f32[4,14,8,128]{3,2,1,0:T(8,128)S(1)} %pad_maximum_fusion.1.refs_1_), channel_id=1, source_target_pairs={{0,1},{1,0},{2,3},{3,2},{4,5},{5,4},{6,7},{7,6},{8,9},{9,8},{10,11... | collective-permute-start | bytes 688136 | tf_op jit(solution)/shard_map/ppermute | solution.py:25
  35.5 4.6 %collective-permute-start.15 = (f32[4,19,8,128]{3,2,1,0:T(8,128)S(1)}, f32[4,19,8,128]{3,2,1,0:T(8,128)S(1)}, u32[]{:S(2)}, u32[]{:S(2)}) collective-permute-start(f32[4,19,8,128]{3,2,1,0:T(8,128)S(1)} %pad_maximum_fusion.refs_2_.refs_1_), channel_id=1, source_target_pairs={{0,1},{1,0},{2,3},{3,2},{4,5},{5,4},{6,7},{7,6},{8,9},{9,8},{10,11... | collective-permute-start | bytes 933896 | tf_op jit(solution)/shard_map/ppermute | solution.py:25
  38.5 5.6 %collective-permute-start.14 = (f32[256,128]{1,0:T(8,128)S(1)}, f32[256,128]{1,0:T(8,128)S(1)}, u32[]{:S(2)}, u32[]{:S(2)}) collective-permute-start(f32[256,128]{1,0:T(8,128)S(1)} %get-tuple-element.47), channel_id=1, source_target_pairs={{0,24},{8,0},{16,8},{24,16},{1,25},{9,1},{17,9},{25,17},{2,26},{10... | collective-permute-start | bytes 393224 | tf_op jit(solution)/shard_map/ppermute | solution.py:20
  45.1 5.9 %collective-permute-start.16 = (f32[256,128]{1,0:T(8,128)S(1)}, f32[256,128]{1,0:T(8,128)S(1)}, u32[]{:S(2)}, u32[]{:S(2)}) collective-permute-start(f32[256,128]{1,0:T(8,128)S(1)} %get-tuple-element.49), channel_id=1, source_target_pairs={{0,8},{8,16},{16,24},{24,0},{1,9},{9,17},{17,25},{25,1},{2,10},{10... | collective-permute-start | bytes 393224 | tf_op jit(solution)/shard_map/ppermute | solution.py:20
